TPU v7x, 32 devices: a whole 2x2x4 slice. The times are simulated.
32 devices in a mesh: dp: 8 (over y, x, core), ctx: 4 (over z).
Axes of the slice: x: 2, y: 2, z: 4, core: 2. Of those that a mesh axis runs over, the one named last changes fastest.
Arguments:
- tokens: bfloat16 [16, 1024, 1024], P('dp', 'ctx'), may hold values from -6 to 6
- cotangent: bfloat16 [16, 1024, 1024], P('dp', 'ctx'), may hold values from -6 to 6
- norm_weight: bfloat16 [1024], P(('dp', 'ctx')), may hold values from 0.25 to 1.75
- input_weight: bfloat16 [1024, 4384], P(('dp', 'ctx')), may hold values from -0.1875 to 0.1875
- kernel_weight: bfloat16 [4, 2304], P(None, ('dp', 'ctx')), may hold values from -3 to 3
- kernel_bias: bfloat16 [2304], P(('dp', 'ctx')), may hold values from -3 to 3
- step_bias: bfloat16 [32], replicated, may hold values from -1.5 to 0.5
- decay_log: bfloat16 [32], replicated, may hold values from -8 to -3.1875
- skip_gain: bfloat16 [32], replicated, may hold values from 0.5 to 1.5
- gate_norm_weight: bfloat16 [2048], P(('dp', 'ctx')), may hold values from 0.25 to 1.75
- output_weight: bfloat16 [2048, 1024], P(('dp', 'ctx')), may hold values from -0.125 to 0.125
Outputs:
- activations: bfloat16 [16, 1024, 1024], P('dp', 'ctx')
- tokens_grad: float32 [16, 1024, 1024], P('dp', 'ctx')
- norm_weight_grad: float32 [1024], P(('dp', 'ctx'))
- input_weight_grad: float32 [1024, 4384], P(('dp', 'ctx'))
- kernel_weight_grad: float32 [4, 2304], P(None, ('dp', 'ctx'))
- kernel_bias_grad: float32 [2304], P(('dp', 'ctx'))
- step_bias_grad: float32 [32], replicated
- decay_log_grad: float32 [32], replicated
- skip_gain_grad: float32 [32], replicated
- gate_norm_weight_grad: float32 [2048], P(('dp', 'ctx'))
- output_weight_grad: float32 [2048, 1024], P(('dp', 'ctx'))
All inputs are finite; a program needn't handle non-finite values.
Results may differ from a plain program's by a relative error of at most 0.017.
The roundings to bfloat16 on the way count: a program that leaves them out, or rounds other values in their place, can miss the bound.
Values may be sent and summed in bfloat16 or wider, within the bound.
No kernel may reach another device: no remote copies, remote signals or barrier semaphores. Data moves between devices by JAX's collectives and lax.ppermute only.
A program may use at most 120 MiB of HBM per device.

v0:
```python
import functools

import jax
import jax.numpy as jnp
import ml_dtypes
import numpy as np
from jax import lax
from jax.experimental import pallas as pl
from jax.experimental.pallas import tpu as pltpu
from jax.sharding import PartitionSpec as P

HEADS = 32
HEAD = 64
STATE = 128
CONV = 4
INNER = 2048
XBC = 2304
BLOCK = 256
HALO = 16
LANES = 128
MINE = INNER // 2
PAIRS = MINE // LANES
CONVD = MINE + 2 * STATE
FRONT = CONVD + LANES

epsilon = 1e-05
bf16 = jnp.bfloat16
f32 = jnp.float32


def swap(value, axis, mask):
    count = lax.axis_size(axis)
    return lax.ppermute(value, axis, [(i, i ^ mask) for i in range(count)])


def hop(value, steps):
    count = lax.axis_size("ctx")
    pairs = [(i, i + steps) for i in range(count) if 0 <= i + steps < count]
    return lax.ppermute(value, "ctx", pairs)


def ordered(own, other, bit, place):
    first = bit == 0
    return jnp.stack([jnp.where(first, own, other), jnp.where(first, other, own)], axis=place)


def choose(value, index, place):
    return lax.dynamic_index_in_dim(value, index, place, keepdims=False)


def bits_of(count):
    return range(count.bit_length() - 1)


def gather_line(shard, z, n_ctx, least=0):
    grown = shard
    for place, bit in enumerate(reversed(range(least, n_ctx.bit_length() - 1))):
        grown = ordered(grown, swap(grown, "ctx", 1 << bit), (z >> bit) & 1, place)
    return grown.reshape((n_ctx >> least,) + shard.shape)


def gather_plane(first, second, q, n_q):
    bits = list(bits_of(n_q))
    shape = first.shape
    for step, bit in enumerate(bits):
        back = bits[len(bits) - 1 - step]
        other = swap(first, "dp", 2 << bit)
        other_second = swap(second, "dp", 2 << back)
        first = ordered(first, other, (q >> bit) & 1, 0)
        second = ordered(second, other_second, (q >> back) & 1, step)
    return first.reshape((n_q,) + shape), second.reshape((n_q,) + shape)


def fold(value, axis, mask, bit, place):
    got = swap(choose(value, 1 - bit, place), axis, mask)
    return (choose(value, bit, place).astype(f32) + got.astype(f32)).astype(bf16)


def scatter_plane(first, second, q, n_q):
    bits = list(bits_of(n_q))
    rest = first.shape[1:]
    left = n_q
    for step, bit in enumerate(bits):
        back = bits[len(bits) - 1 - step]
        left //= 2
        first = fold(
            first.reshape((2, left) + rest), "dp", 2 << back, (q >> back) & 1, 0
        )
        second = fold(
            second.reshape((left, 2) + rest), "dp", 2 << bit, (q >> bit) & 1, 1
        )
    return first.reshape(rest), second.reshape(rest)


def gather_rest(near, far, z, n_ctx, q, n_q):
    near_halves = gather_plane(near[:, 0], near[:, 1], q, n_q)
    far_halves = gather_plane(far[:, 0], far[:, 1], q, n_q)
    shape = (n_q, n_ctx) + near.shape[2:]
    return tuple(ordered(a, b, z & 1, 2).reshape(shape) for a, b in zip(near_halves, far_halves))


def scatter_both(first, second, z, n_ctx, q, n_q):
    shape = (n_q, n_ctx // 2, 2) + first.shape[2:]
    sums = []
    for which in (1 - (z & 1), z & 1):
        halves = (choose(value.reshape(shape), which, 2) for value in (first, second))
        sums.append(jnp.stack(scatter_plane(*halves, q, n_q), axis=1))
    got = swap(sums[0], "ctx", 1)
    total = (sums[1].astype(f32) + got.astype(f32)).astype(bf16)
    return scatter_line(total, z, n_ctx, 1)


def sides_of(value):
    return swap(value, "dp", 2), swap(value, "dp", 4)


def sides_of_each(along_x, along_y):
    return swap(along_x, "dp", 2), swap(along_y, "dp", 4)


def add(*values):
    return sum(value.astype(f32) for value in values).astype(bf16)


def after(value, *others):
    if not others:
        return value
    return pl.pallas_call(
        lambda *refs: None,
        in_specs=[pl.BlockSpec(memory_space=pl.ANY)] * (1 + len(others)),
        out_specs=pl.BlockSpec(memory_space=pl.ANY),
        out_shape=jax.ShapeDtypeStruct(value.shape, value.dtype),
        input_output_aliases={0: 0},
    )(value, *others)


def scatter_line(value, z, n_ctx, least=0):
    rest = value.shape[1:]
    left = n_ctx >> least
    for bit in range(least, n_ctx.bit_length() - 1):
        left //= 2
        value = fold(value.reshape((left, 2) + rest), "ctx", 1 << bit, (z >> bit) & 1, 1)
    return value.reshape(rest)


def dot(a, b):
    return jnp.dot(a, b, preferred_element_type=f32)


def dot_nt(a, b):
    return lax.dot_general(a, b, (((1,), (1,)), ((), ())), preferred_element_type=f32)


def dot_tn(a, b):
    return lax.dot_general(a, b, (((0,), (0,)), ((), ())), preferred_element_type=f32)


def split(value):
    high = value.astype(bf16)
    return high, (value - high.astype(f32)).astype(bf16)


def split3(value):
    high, low = split(value)
    least = (value - high.astype(f32) - low.astype(f32)).astype(bf16)
    return high, low, least


def halves_of(value):
    return jnp.concatenate(split(value), axis=1)


def spread(halves, ex, lanes):
    return dot(halves, ex[:, lanes])


def pool(value, pairs, strip):
    return dot_nt(halves_of(value), pairs[:, strip * 2 * LANES : (strip + 1) * 2 * LANES])


def strip_of(number, size=LANES):
    return slice(number * size, (number + 1) * size)


def conv_rows(px, block):
    return px[pl.ds(pl.multiple_of(block * BLOCK, BLOCK), BLOCK + HALO), :]


def conv_strip(wide, kw, lanes):
    taps = [wide[HALO - CONV + 1 + k : HALO - CONV + 1 + k + BLOCK, lanes] for k in range(CONV)]
    total = kw[CONV : CONV + 1, lanes]
    for k in range(CONV):
        total = total + kw[k : k + 1, lanes] * taps[k]
    return total, taps


def inverse_rms(rows):
    return lax.rsqrt(jnp.mean(rows * rows, axis=-1, keepdims=True) + epsilon)


def steps_of(raw, heads, pick):
    biased = dot(raw, pick[...]) + heads[0:1, :]
    rate = heads[1:2, :]
    step = jnp.maximum(biased, 0.0) + jnp.log1p(jnp.exp(-jnp.abs(biased)))
    return biased, step, -step * rate, rate


def features_kernel(mine, other, before, before_other, norm, front, kw, heads, pick, tri, ex, pairs,
                    normed_o, px_o, x_o, u_o, bc_o, cum_o, cumt_o, entry_o, factor_o, total_o,
                    decay_o, state, passed, wide, weighted):
    j, block = pl.program_id(0), pl.program_id(1)
    start = pl.multiple_of(block * BLOCK, BLOCK)
    early = pl.multiple_of(jnp.maximum(start - HALO, 0), HALO)

    def rows_of(begin, count):
        return jnp.where(j == 0, mine[pl.ds(begin, count), :], other[pl.ds(begin, count), :])

    ahead = jnp.where(j == 0, before[...], before_other[...])
    ahead = jnp.where(block == 0, ahead, rows_of(early, HALO))
    residual = jnp.concatenate([ahead, rows_of(start, BLOCK)], axis=0).astype(f32)
    normed = (residual * inverse_rms(residual) * norm[...]).astype(bf16)
    normed_o[...] = normed[HALO:]
    rows = dot(normed, front[...]).astype(bf16)
    px_o[0, pl.ds(start, BLOCK + HALO), :] = rows
    wide[...] = rows[:, :CONVD].astype(f32)

    @pl.when(block == 0)
    def _():
        state[...] = jnp.zeros_like(state)
        passed[...] = jnp.ones_like(passed)

    _, step, log_decay, _ = steps_of(rows[HALO:, CONVD:], heads, pick)
    cum = sum(dot(tri[...], part) for part in split3(log_decay))
    last = cum[BLOCK - 1 : BLOCK, :]
    cum_o[...] = cum
    cumt_o[0] = cum.T
    step, remaining = halves_of(step), halves_of(jnp.exp(last - cum))
    whole = halves_of(jnp.broadcast_to(jnp.exp(last), (16, LANES)))
    entry_o[0] = state[...].astype(bf16)
    factor_o[0] = jnp.broadcast_to(passed[...], (8, MINE))
    for number in range(2):
        lanes = strip_of(PAIRS + number)
        total, _ = conv_strip(wide, kw, lanes)
        bc_o[:, strip_of(number)] = (total * jax.nn.sigmoid(total)).astype(bf16)
    for number in range(PAIRS):
        lanes = strip_of(number)
        total, _ = conv_strip(wide, kw, lanes)
        x = total * jax.nn.sigmoid(total)
        x_o[:, lanes] = x.astype(bf16)
        u = (x * spread(step, ex, lanes)).astype(bf16)
        u_o[:, lanes] = u
        weighted[:, lanes] = (u.astype(f32) * spread(remaining, ex, lanes)).astype(bf16)
    whole = spread(whole, ex, slice(0, MINE))[:1]
    state[...] = whole * state[...] + dot_tn(bc_o[:, :STATE], weighted[...])
    passed[...] = passed[...] * whole
    total_o[0] = state[...].astype(bf16)
    decay_o[0] = jnp.broadcast_to(passed[...], (8, MINE))


def within_kernel(u, bc, cum, cumt, y_o):
    rows = lax.broadcasted_iota(jnp.int32, (BLOCK, BLOCK), 0)
    columns = lax.broadcasted_iota(jnp.int32, (BLOCK, BLOCK), 1)
    products = jnp.where(rows >= columns, dot_nt(bc[:, STATE:], bc[:, :STATE]), 0.0)
    lane = lax.broadcasted_iota(jnp.int32, (BLOCK, LANES), 1)
    for pair in range(PAIRS):
        values = u[:, pair * LANES : (pair + 1) * LANES]
        made = []
        for head in (2 * pair, 2 * pair + 1):
            decay = jnp.exp(jnp.minimum(cum[:, head : head + 1] - cumt[0, head : head + 1, :], 0.0))
            made.append(dot((products * decay).astype(bf16), values))
        made = jnp.where(lane < HEAD, made[0], made[1])
        y_o[:, pair * LANES : (pair + 1) * LANES] = made.astype(bf16)


def gate_kernel(normed, cot_mine, cot_other, wg, wo, y, x, bc, cum, entry, factor, incoming, skip,
                gain, ex, mix_o, z_o, ds_o, state_o, sums_o):
    cot = jnp.where(pl.program_id(0) == 0, cot_mine[...], cot_other[...])
    grown = halves_of(jnp.exp(cum[...]))
    squares = jnp.zeros((BLOCK, LANES), f32)
    crossed = jnp.zeros((BLOCK, LANES), f32)
    for chunk in range(PAIRS // 2):
        many = strip_of(chunk, 2 * LANES)
        z_all = dot(normed[...], wg[:, many]).astype(bf16)
        ds_all = dot_nt(cot, wo[many, :])
        entering = entry[0, :, many].astype(f32) + factor[0, :1, many] * incoming[0, :, many].astype(f32)
        entering = entering.astype(bf16)
        z_o[:, many] = z_all
        ds_o[:, many] = ds_all.astype(bf16)
        state_o[0, :, many] = entering
        mix_all = spread(grown, ex, many) * dot(bc[:, STATE:], entering)
        for half in range(2):
            part, lanes = strip_of(half), strip_of(2 * chunk + half)
            carried = mix_all[:, part] + y[:, lanes].astype(f32)
            mix_o[:, lanes] = carried.astype(bf16)
            mix = carried + skip[:, lanes] * x[:, lanes].astype(f32)
            z = z_all[:, part].astype(f32)
            g = mix * (z * jax.nn.sigmoid(z))
            squares = squares + g * g
            crossed = crossed + ds_all[:, part] * gain[:, lanes] * g
    ones = jnp.ones((8, 2 * LANES), bf16)
    which = lax.broadcasted_iota(jnp.int32, (8, BLOCK), 0)
    squares, crossed = dot_nt(ones, halves_of(squares)), dot_nt(ones, halves_of(crossed))
    sums_o[...] = jnp.where(which < 4, squares, crossed)


def mixture_kernel(mix_r, z_r, ds_r, x, bc, cum, sums, got, skip, gain, ex, pairs,
                   scaled_o, dy_o, dz_o, inner_o, exit_o, factor_o, send_o, gain_o, skip_o,
                   state, passed, weighted):
    j, i = pl.program_id(0), pl.program_id(1)

    @pl.when((j == 0) & (i == 0))
    def _():
        gain_o[...] = jnp.zeros_like(gain_o)
        skip_o[...] = jnp.zeros_like(skip_o)

    @pl.when(i == 0)
    def _():
        state[...] = jnp.zeros_like(state)
        passed[...] = jnp.ones_like(passed)

    summed = sums[...] + got[...]
    lane = lax.broadcasted_iota(jnp.int32, (8, 2 * LANES), 1)
    row = lax.broadcasted_iota(jnp.int32, (8, 2 * LANES), 0)
    turn = jnp.where(row == (lane // LANES) * 4, 1.0, 0.0).astype(bf16)
    summed = sum(dot_tn(part, turn) for part in split3(summed))
    scale = lax.rsqrt(summed[:, :LANES] / INNER + epsilon)
    back_scale = scale * scale * scale * (summed[:, LANES:] / INNER)
    grown = halves_of(jnp.exp(cum[...]))
    inner = jnp.zeros((BLOCK, LANES), f32)
    for number in range(PAIRS):
        lanes = strip_of(number)
        carried = mix_r[:, lanes].astype(f32)
        xs = x[:, lanes].astype(f32)
        mix = carried + skip[:, lanes] * xs
        z = z_r[:, lanes].astype(f32)
        ds = ds_r[:, lanes].astype(f32)
        sig = jax.nn.sigmoid(z)
        silu = z * sig
        g = mix * silu
        normalized = g * scale
        scaled_o[:, lanes] = (normalized * gain[:, lanes]).astype(bf16)
        gain_o[:, lanes] += jnp.sum(ds * normalized, axis=0, keepdims=True)
        dg = ds * (scale * gain[:, lanes]) - g * back_scale
        dmix = dg * silu
        dz_o[:, lanes] = (dg * mix * (sig * (1.0 + z * (1.0 - sig)))).astype(bf16)
        skip_o[:, lanes] += jnp.sum(dmix * xs, axis=0, keepdims=True)
        dy = dmix.astype(bf16)
        dy_o[:, lanes] = dy
        dyf = dy.astype(f32)
        inner = inner + pool(dyf * carried, pairs, number)
        weighted[:, lanes] = (dyf * spread(grown, ex, lanes)).astype(bf16)
    inner_o[...] = inner
    last = cum[BLOCK - 1 : BLOCK, :]
    whole = halves_of(jnp.broadcast_to(jnp.exp(last), (16, LANES)))
    whole = spread(whole, ex, slice(0, MINE))[:1]
    exit_o[0] = state[...].astype(bf16)
    factor_o[0] = jnp.broadcast_to(passed[...], (8, MINE))
    state[...] = whole * state[...] + dot_tn(bc[:, STATE:], weighted[...])
    passed[...] = passed[...] * whole
    send_o[0] = state[...].astype(bf16)


def within_back(u, dy, bc, cum, cumt, du_o, dbc_o):
    rows = lax.broadcasted_iota(jnp.int32, (BLOCK, BLOCK), 0)
    columns = lax.broadcasted_iota(jnp.int32, (BLOCK, BLOCK), 1)
    causal = columns >= rows
    products = jnp.where(causal, dot_nt(bc[:, :STATE], bc[:, STATE:]), 0.0)
    lane = lax.broadcasted_iota(jnp.int32, (BLOCK, LANES), 1)
    total = jnp.zeros((BLOCK, BLOCK), f32)
    for pair in range(PAIRS):
        values = u[:, pair * LANES : (pair + 1) * LANES]
        grads = dy[:, pair * LANES : (pair + 1) * LANES]
        made = []
        for half in range(2):
            head = 2 * pair + half
            decay = jnp.exp(jnp.minimum(cumt[0, head : head + 1, :] - cum[:, head : head + 1], 0.0))
            made.append(dot((products * decay).astype(bf16), grads))
            own = jnp.where((lane < HEAD) == (half == 0), values, jnp.zeros_like(values))
            total = total + dot_nt(own, grads) * decay
        made = jnp.where(lane < HEAD, made[0], made[1])
        du_o[:, pair * LANES : (pair + 1) * LANES] = made.astype(bf16)
    total = jnp.where(causal, total, 0.0).astype(bf16)
    dbc_o[:, :STATE] = dot(total, bc[:, STATE:])
    dbc_o[:, STATE:] = dot_tn(total, bc[:, :STATE])


def features_back_kernel(px, kw, heads, pick, tri, ex, pairs, u, dy, du_r, dbc, inner, cum,
                         entering, exit_r, factor, incoming, skip,
                         gp_o, rim_o, tail_o, kw_o, heads_o, after, wide, dpre, raw, held_u,
                         grown_dy):
    j, i = pl.program_id(0), pl.program_id(1)
    block = pl.num_programs(1) - 1 - i

    @pl.when((j == 0) & (i == 0))
    def _():
        kw_o[...] = jnp.zeros_like(kw_o)
        heads_o[...] = jnp.zeros_like(heads_o)

    @pl.when(i == 0)
    def _():
        after[...] = jnp.zeros_like(after)

    rows = conv_rows(px.at[0], block)
    wide[...] = rows[:, :CONVD].astype(f32)
    dpre[BLOCK:, :] = after[...]
    biased, step, log_decay, rate = steps_of(rows[HALO:, CONVD:], heads, pick)
    c = cum[...]
    last = c[BLOCK - 1 : BLOCK, :]
    leaving = exit_r[0].astype(f32) + factor[0][:1] * incoming[0].astype(f32)
    leaving16 = leaving.astype(bf16)
    crossing = jnp.sum(leaving * entering[0].astype(f32), axis=0, keepdims=True)
    crossing = jnp.broadcast_to(crossing, (16, MINE))
    crossing = sum(pool(crossing[:, strip_of(n)], pairs, n) for n in range(PAIRS))
    crossing = crossing[:1] * jnp.exp(last)
    remaining, grown, steps = (halves_of(v) for v in (jnp.exp(last - c), jnp.exp(c), step))
    total, _ = conv_strip(wide, kw, strip_of(PAIRS))
    raw[...] = dot((total * jax.nn.sigmoid(total)).astype(bf16), leaving16)

    def finish(dact, total, sig, taps, lanes):
        value = dact * (sig * (1.0 + total * (1.0 - sig)))
        kw_o[CONV : CONV + 1, lanes] += jnp.sum(value, axis=0, keepdims=True)
        for k in range(CONV):
            kw_o[k : k + 1, lanes] += jnp.sum(value * taps[k], axis=0, keepdims=True)
        dpre[:BLOCK, lanes] = value
        din = sum(
            kw[k : k + 1, lanes] * dpre[CONV - 1 - k : CONV - 1 - k + BLOCK, lanes]
            for k in range(CONV)
        )
        gp_o[0, :, lanes] = din.astype(bf16)

        @pl.when(i == 0)
        def _():
            tail_o[0, :, lanes] = din[BLOCK - 16 :]

    held = jnp.zeros((BLOCK, LANES), f32)
    flow = inner[...]
    dstep = jnp.zeros((BLOCK, LANES), f32)
    for number in range(PAIRS):
        lanes = strip_of(number)
        total, taps = conv_strip(wide, kw, lanes)
        sig = jax.nn.sigmoid(total)
        uf = u[:, lanes].astype(f32)
        dyf = dy[:, lanes].astype(f32)
        left = spread(remaining, ex, lanes)
        du_state = left * raw[:, lanes]
        du_in = du_r[:, lanes].astype(f32)
        held_u[:, lanes] = (uf * left).astype(bf16)
        grown_dy[:, lanes] = (dyf * spread(grown, ex, lanes)).astype(bf16)
        held = held + pool(uf * du_state, pairs, number)
        flow = flow - pool(uf * du_in, pairs, number)
        du = du_in + du_state
        dstep = dstep + pool(du * (total * sig), pairs, number)
        dx = du * spread(steps, ex, lanes) + skip[:, lanes] * dyf
        finish(dx, total, sig, taps, lanes)
    db = dbc[:, :STATE] + dot_nt(held_u[...], leaving16)
    dc = dbc[:, STATE:] + dot_nt(grown_dy[...], entering[0])
    for number, value in enumerate((db, dc)):
        lanes = strip_of(PAIRS + number)
        total, taps = conv_strip(wide, kw, lanes)
        finish(value, total, jax.nn.sigmoid(total), taps, lanes)
    after[...] = dpre[:8, :]
    dlog = crossing + sum(dot_tn(tri[...], part) for part in split3(flow))
    dlog = dlog + sum(dot(tri[...], part) for part in split3(held)) - held
    draw = (dstep - dlog * rate) * jax.nn.sigmoid(biased)
    gp_o[0, :, CONVD:] = dot_nt(draw.astype(bf16), pick[...]).astype(bf16)
    heads_o[0:1, :] += jnp.sum(draw, axis=0, keepdims=True)
    heads_o[1:2, :] += jnp.sum(dlog * log_decay, axis=0, keepdims=True)
    early = jnp.concatenate([jnp.zeros((8, CONVD), f32), dpre[:8, :]], axis=0)
    rim_o[0] = sum(kw[k : k + 1, :] * early[CONV - 1 - k : CONV - 1 - k + 8] for k in range(CONV))


def write_parts(j, mine_o, other_o, value):
    @pl.when(j == 0)
    def _():
        mine_o[...] = value

    @pl.when(j > 0)
    def _():
        other_o[...] = value


def added(*refs):
    return sum(ref.astype(f32) for ref in refs).astype(bf16)


def send_piece_kernel(place, value, out):
    out[...] = jnp.where(place[2] % 2 == 0, value[1], value[0])


def both_pieces_kernel(place, value, got, out):
    side = place[2] % 2
    kept = jnp.where(side == 0, value[0], value[1])
    out[0] = jnp.where(side == 0, kept, got[...])
    out[1] = jnp.where(side == 0, got[...], kept)


def copy_kernel(value, out):
    out[...] = value[...]


def shard_kernel(own, got, out_weight, front_o, late_o):
    r_in, half = own.shape[0], out_weight.shape[0] // 2
    for k, source in enumerate((own, got)):
        front_o[k] = source[:, :FRONT]
        late_o[k, :r_in] = source[:, FRONT:]
        late_o[k, r_in:] = out_weight[k * half : (k + 1) * half]


def pair_kernel(first, second, out):
    count = first.shape[1]
    out[:, :count] = first[...]
    out[:, count:] = second[...]


def halves_kernel(along_x, along_y, x_o, y_o):
    x_o[...] = along_x[0]
    y_o[...] = along_y[0]


def ends_grads_kernel(front, front_got, late, late_got, own_o, send_o, out_o):
    r_in = front.shape[1]
    for k, out in enumerate((own_o, send_o)):
        out[:, :CONVD] = added(front[k], front_got[k])
        out[:, CONVD:] = added(late[k, :r_in], late_got[k, :r_in])
        half = late.shape[1] - r_in
        out_o[k * half : (k + 1) * half] = late[k, r_in:].astype(f32) + late_got[k, r_in:].astype(f32)


def input_grad_kernel(n_dp, place, own, got, sums, out):
    run, first = INNER // n_dp, place[1] == 0
    part = own.shape[0] // 4
    for k in range(n_dp // 2):
        for source, target in ((0, INNER), (CONVD, 0)):
            mine = own[:, source + k * run : source + (k + 1) * run].astype(f32)
            others = got[:, source + k * run : source + (k + 1) * run].astype(f32)
            at = target + 2 * k * run
            out[:, at : at + run] = jnp.where(first, mine, others)
            out[:, at + run : at + 2 * run] = jnp.where(first, others, mine)
    both = own[:, MINE:CONVD].astype(f32) + got[:, MINE:CONVD].astype(f32)
    out[:, 2 * INNER : INNER + XBC] = both
    for k in range(4):
        out[k * part : (k + 1) * part, INNER + XBC :] = sums[8 : 8 + part, k * HEADS : (k + 1) * HEADS]


def sums_kernel(parts, out):
    out[...] = jnp.sum(parts[...], axis=0)


def activations_kernel(place, tokens, keep, got, out):
    value = jnp.where(pl.program_id(0) == place[2] % 2, keep[...], got[...])
    out[0] = (tokens[0].astype(f32) + value.astype(f32)).astype(bf16)


def tokens_grad_kernel(place, tokens, cot, keep, got, norm, out):
    value = jnp.where(pl.program_id(0) == place[2] % 2, keep[...], got[...])
    residual = tokens[0].astype(f32)
    inverse = inverse_rms(residual)
    weighted = value.astype(f32) * norm[...]
    along = jnp.mean(weighted * residual, axis=-1, keepdims=True)
    out[0] = (
        cot[0].astype(f32) + inverse * weighted - residual * (inverse * inverse * inverse * along)
    )


def relative(place, n_ctx, groups):
    for group in range(2):
        for slot in range(n_ctx // 2):
            z = place[2] ^ group ^ (2 * slot)
            at = slot if groups == 2 else group * (n_ctx // 2) + slot
            first = 5 * group if groups == 2 else 0
            for half in range(2):
                for chip in range(3):
                    yield first + chip, (half, at), place[0] ^ chip, z, half
                yield first + 3 + half, (at,), place[0] ^ 3, z, half


def relative_back(place, n_ctx, groups):
    spots = {(0, 0): (0, 0), (0, 1): (0, 1), (1, 1): (1, 1), (2, 0): (2, 1), (1, 0): (3, None),
             (2, 1): (4, None), (3, 1): (1, 0), (3, 0): (2, 0)}
    for group in range(2):
        for slot in range(n_ctx // 2):
            z = place[2] ^ group ^ (2 * slot)
            at = slot if groups == 2 else group * (n_ctx // 2) + slot
            first = 5 * group if groups == 2 else 0
            for (chip, half), (piece, lead) in spots.items():
                index = (at,) if lead is None else (lead, at)
                yield first + piece, index, place[0] ^ chip, z, half


def front_rows(place, n_ctx, chip, z, half, count):
    return pl.multiple_of(((chip * 2 + (place[1] ^ half)) * n_ctx + z) * count, count)


def out_rows(n_ctx, chip, z, half, count):
    return pl.multiple_of(((chip * n_ctx + z) * 2 + half) * count, count)


def front_weights_kernel(n_dp, n_ctx, r_in, place, heads_in, ex, *refs):
    pieces, refs = refs[:-10], refs[-10:]
    front, wide = refs[0], refs[7]
    if len(pieces) == 1:
        front[...] = pieces[0][...]
    else:
        for piece, index, chip, z, half in relative(place, n_ctx, 2):
            begin = front_rows(place, n_ctx, chip, z, half, r_in)
            front[pl.ds(begin, r_in), :] = pieces[piece][index]
    wide[...] = front[:, CONVD:].astype(f32)
    spread_small(n_dp, r_in, place[1], wide, heads_in, ex, *refs[1:7], *refs[8:])


def late_weights_kernel(n_ctx, r_in, place, *refs):
    pieces, gate, out = refs[:-2], refs[-2], refs[-1]
    r_out = pieces[0].shape[2] - r_in
    for piece, index, chip, z, half in relative(place, n_ctx, 1):
        block = pieces[piece][index]
        gate[pl.ds(front_rows(place, n_ctx, chip, z, half, r_in), r_in), :] = block[:r_in]
        out[pl.ds(out_rows(n_ctx, chip, z, half, r_out), r_out), :] = block[r_in:]


def middle_kernel(n_ctx, r_in, place, normed, dz, scaled, cot_mine, cot_other, wo, u, dy, bc, cum, cumt, *refs):
    mine_o, other_o, du_o, dbc_o = refs[:4]
    outputs, (gate, out) = refs[4:-2], refs[-2:]
    j, i = pl.program_id(0), pl.program_id(1)
    within_back(u, dy, bc, cum, cumt, du_o, dbc_o)
    step = j * pl.num_programs(1) + i
    cot = jnp.where(j == 0, cot_mine[...], cot_other[...])
    write_parts(j, mine_o, other_o, dot(scaled[...], wo[...]).astype(bf16))
    gate_part, out_part = dot_tn(normed[...], dz[...]), dot_tn(scaled[...], cot)

    @pl.when(step == 0)
    def _():
        gate[...] = gate_part
        out[...] = out_part

    @pl.when(step > 0)
    def _():
        gate[...] += gate_part
        out[...] += out_part

    @pl.when(step == pl.num_programs(0) * pl.num_programs(1) - 1)
    def _():
        if len(outputs) == 2:
            outputs[0][...] = gate[...].astype(bf16)
            outputs[1][...] = out[...].astype(bf16)
            return
        r_out = outputs[0].shape[2] - r_in
        for piece, index, chip, z, half in relative_back(place, n_ctx, 1):
            begin = front_rows(place, n_ctx, chip, z, half, r_in)
            outputs[piece][index + (slice(0, r_in),)] = gate[pl.ds(begin, r_in), :].astype(bf16)
            begin = out_rows(n_ctx, chip, z, half, r_out)
            outputs[piece][index + (slice(r_in, r_in + r_out),)] = out[
                pl.ds(begin, r_out), :
            ].astype(bf16)


def with_rim(gp, tail, rim, whole):
    whole[...] = gp[0]
    late = tail[0] + jnp.concatenate([jnp.zeros((8, CONVD), f32), rim[0]], axis=0)
    whole[whole.shape[0] - 16 :, :CONVD] = late.astype(bf16)


def front_grads_kernel(n_ctx, r_in, place, normed, gp, tail, rim, step_o, *refs):
    outputs, (total, whole) = refs[:-2], refs[-2:]
    j = pl.program_id(0)
    with_rim(gp, tail, rim, whole)
    part = dot_tn(normed[...], whole[...])

    @pl.when(j == 0)
    def _():
        total[...] = part

    @pl.when(j > 0)
    def _():
        total[...] += part

    @pl.when(j == pl.num_programs(0) - 1)
    def _():
        step_o[...] = total[:, CONVD:]
        if len(outputs) == 1:
            outputs[0][...] = total[:, :CONVD].astype(bf16)
            return
        for piece, index, chip, z, half in relative_back(place, n_ctx, 1):
            begin = front_rows(place, n_ctx, chip, z, half, r_in)
            outputs[piece][index] = total[pl.ds(begin, r_in), :CONVD].astype(bf16)


def normed_grads_kernel(mine, other, dz, wg, gp, tail, rim, front, mine_o, other_o, norm_o, whole):
    j = pl.program_id(0)
    with_rim(gp, tail, rim, whole)
    back = dot_nt(dz[...], wg[...]) + dot_nt(whole[...], front[...])
    write_parts(j, mine_o, other_o, back.astype(bf16))
    residual = jnp.where(j == 0, mine[...], other[...]).astype(f32)

    @pl.when(j == 0)
    def _():
        norm_o[...] = jnp.zeros_like(norm_o)

    norm_o[...] += jnp.sum(back * (residual * inverse_rms(residual)), axis=0, keepdims=True)


def small_place(n, k, r_in, n_all):
    rows = min(r_in, 8)
    span = (LANES - HEADS) // -(-7 // rows)
    width = (XBC // n_all,) * 5 + (INNER // n_all, r_in)
    return n * r_in + k % rows, HEADS + (k // rows) * span, width[k]


def prepare_kernel(n_dp, n_all, place, weight, vectors, own_o, other_o):
    r_in, run, first = weight.shape[0], INNER // n_dp, place[1] == 0
    for k in range(n_dp // 2):
        for source, target in ((INNER, 0), (0, FRONT)):
            low = weight[:, source + 2 * k * run : source + (2 * k + 1) * run]
            high = weight[:, source + (2 * k + 1) * run : source + (2 * k + 2) * run]
            at = target + k * run
            own_o[:, at : at + run] = jnp.where(first, low, high)
            other_o[:, at : at + run] = jnp.where(first, high, low)
    row = lax.broadcasted_iota(jnp.int32, (r_in, LANES), 0)
    small = jnp.concatenate(
        [weight[:, INNER + XBC :].astype(f32), jnp.zeros((r_in, LANES - HEADS), f32)], axis=1
    )
    at = 0
    for k in range(7):
        line, lane, count = small_place(0, k, r_in, n_all)
        piece = vectors[:, at : at + count].astype(f32)
        parts = [jnp.zeros((1, lane), f32), piece, jnp.zeros((1, LANES - lane - count), f32)]
        small = small + jnp.where(row == line, jnp.concatenate(parts, axis=1), 0.0)
        at += count
    for out in (own_o, other_o):
        out[:, MINE:CONVD] = weight[:, 2 * INNER : INNER + XBC]
        out[:, CONVD:FRONT] = small.astype(bf16)


def spread_small(n_dp, r_in, core, wide, heads_in, ex, kw_o, gain_o, norm_o, heads_o, skip_o, pick_o,
                 full, gains):
    n_all = wide.shape[0] // r_in
    run, heads_run, first = INNER // n_dp, HEADS // n_dp, core == 0
    full[...] = jnp.zeros_like(full)
    for n in range(n_all):
        for k in range(7):
            row, lane, count = small_place(n, k, r_in, n_all)
            target, at = ((full, k), (gains, 0), (norm_o, 0))[max(k - CONV, 0)]
            target[at : at + 1, n * count : (n + 1) * count] = wide[row : row + 1, lane : lane + count]
    for k in range(n_dp // 2):
        low, high = 2 * k * run, (2 * k + 1) * run
        kw_o[:, k * run : (k + 1) * run] = jnp.where(
            first, full[:, low : low + run], full[:, high : high + run]
        )
        gain_o[:, k * run : (k + 1) * run] = jnp.where(
            first, gains[:, low : low + run], gains[:, high : high + run]
        )
    kw_o[:, MINE:] = full[:, INNER:]
    source = lax.broadcasted_iota(jnp.int32, (LANES, LANES), 0)
    local = lax.broadcasted_iota(jnp.int32, (LANES, LANES), 1)
    position = ((local // heads_run) * 2 + core) * heads_run + local % heads_run
    chosen = (source == position) & (local < HEADS // 2)
    pick = jnp.where(chosen, 1.0, 0.0).astype(bf16)
    pick_o[...] = pick
    heads = dot(heads_in[...].astype(bf16), pick)
    row = lax.broadcasted_iota(jnp.int32, (8, LANES), 0)
    lane = lax.broadcasted_iota(jnp.int32, (8, LANES), 1)
    rate = jnp.where(lane < HEADS // 2, jnp.exp(heads), 0.0)
    heads_o[...] = jnp.where(row == 1, rate, heads)
    skip_o[...] = dot(heads.astype(bf16), ex[:LANES, :])[2:3]


def pack_kernel(n_dp, place, norm_sum, kw_sum, gain_sum, heads_sum, skip_sum, step_sum, pick, pairs,
                packed_o, full, gains):
    n_all = packed_o.shape[0]
    taps_n, gain_n, norm_n = XBC // n_all, INNER // n_all, norm_sum.shape[1] // n_all
    part, run = norm_n // 4, INNER // n_dp
    keep = [jnp.where(place[1] == which, 1.0, 0.0) for which in range(2)]
    for k in range(n_dp // 2):
        for which in range(2):
            begin = (2 * k + which) * run
            full[:, begin : begin + run] = kw_sum[:, k * run : (k + 1) * run] * keep[which]
            gains[:, begin : begin + run] = gain_sum[:, k * run : (k + 1) * run] * keep[which]
    full[:, INNER:] = kw_sum[:, MINE:]
    skips = jnp.broadcast_to(skip_sum[...], (16, MINE))
    skips = sum(pool(skips[:, strip_of(n)], pairs, n) for n in range(PAIRS))[:8]
    row = lax.broadcasted_iota(jnp.int32, (8, LANES), 0)
    heads = jnp.where(row == 2, skips, heads_sum[...])
    heads = sum(dot_nt(piece, pick[...]) for piece in split3(heads))
    packed_o[...] = jnp.zeros_like(packed_o)
    for n in range(n_all):
        packed_o[n, 0:5, :taps_n] = full[0:5, n * taps_n : (n + 1) * taps_n]
        packed_o[n, 5:6, :gain_n] = gains[:, n * gain_n : (n + 1) * gain_n]
        packed_o[n, 6:7, :norm_n] = norm_sum[:, n * norm_n : (n + 1) * norm_n]
        for k in range(3):
            packed_o[n, 7:8, k * HEADS : (k + 1) * HEADS] = heads[k : k + 1, :HEADS]
        for k in range(4):
            begin = n * norm_n + k * part
            packed_o[n, 8 : 8 + part, k * HEADS : (k + 1) * HEADS] = step_sum[
                begin : begin + part, :HEADS
            ]


def call(kernel, grid, in_specs, out_specs, out_shape, scratch=(), cost=0, needs=(), vmem=20):
    count = len(in_specs)

    def body(*refs):
        kernel(*refs[:count], *refs[count + len(needs) :])

    made = pl.pallas_call(
        body,
        grid=grid,
        in_specs=list(in_specs) + [pl.BlockSpec(memory_space=pl.ANY)] * len(needs),
        out_specs=out_specs,
        out_shape=out_shape,
        scratch_shapes=scratch,
        cost_estimate=pl.CostEstimate(
            flops=int(1 + cost * 1e9), transcendentals=0, bytes_accessed=int(1 + cost * 3.5e6)
        ),
        compiler_params=pltpu.CompilerParams(
            vmem_limit_bytes=vmem << 20, dimension_semantics=("arbitrary",) * len(grid)
        ),
    )
    return lambda *arrays: made(*arrays, *needs)


def sds(shape, dtype=f32):
    return jax.ShapeDtypeStruct(shape, dtype)


def main(value):
    return pltpu.with_memory_space_constraint(value, pltpu.HBM)


def on_device(
    tokens,
    cotangent,
    norm_weight,
    input_weight,
    kernel_weight,
    kernel_bias,
    step_bias,
    decay_log,
    skip_gain,
    gate_norm_weight,
    output_weight,
):
    n_dp, n_ctx = lax.axis_size("dp"), lax.axis_size("ctx")
    n_q, n_all = n_dp // 2, n_dp * n_ctx
    place, z = lax.axis_index("dp"), lax.axis_index("ctx")
    q, core = place >> 1, place & 1
    seqs, piece, width = tokens.shape
    length = 2 * piece
    blocks = length // BLOCK
    rows = seqs * length
    r_in, r_out = input_weight.shape[0], output_weight.shape[0]
    every = ("dp", "ctx")
    fast = n_q == 4 and n_ctx == 4 and r_in % 16 == 0
    where = jnp.stack([q, core, z]).astype(jnp.int32)
    smem = pl.BlockSpec(memory_space=pltpu.SMEM)

    def lanes(value, count, wide=LANES):
        return jnp.pad(value, ((0, count - value.shape[0]), (0, wide - value.shape[1])))

    def all_of(arrays):
        return [pl.BlockSpec(v.shape, lambda *_, n=len(v.shape): (0,) * n) for v in arrays]

    def once(kernel, arrays, made, scratch=(), cost=0, needs=(), placed=False):
        specs = ([smem] if placed else []) + all_of(arrays)
        single = not isinstance(made, list)
        outs = all_of([made])[0] if single else all_of(made)
        run = call(kernel, (1,), specs, outs, made, scratch, cost, needs)
        return run(*([where] if placed else []), *arrays)

    cuts = 2
    cut_s = pl.BlockSpec((piece // cuts, width), lambda i: (i, 0))
    both_cut_s = pl.BlockSpec((2, piece // cuts, width), lambda i: (0, i, 0))

    def piece_to_send(value, needs=()):
        made = sds((piece, width), bf16)
        run = call(send_piece_kernel, (cuts,), [smem, both_cut_s], cut_s, made, needs=needs)
        return run(where, value)

    def enter_line(value, send, needs=(), cost=0):
        made, got = sds((2, piece, width), bf16), swap(send, "ctx", 1)
        specs = [smem, both_cut_s, cut_s]
        run = call(both_pieces_kernel, (cuts,), specs, both_cut_s, made, (), cost, needs)
        return run(where, value, got).reshape(length, width)

    def leave_cores(mine, other, needs=()):
        total = add(after(mine, *needs), swap(other, "dp", 1)).reshape(2, piece, width)
        return choose(total, z & 1, 0), choose(total, 1 - (z & 1), 0)


    tokens_send = piece_to_send(tokens)
    vectors = jnp.concatenate([kernel_weight.reshape(-1), kernel_bias, gate_norm_weight, norm_weight])
    own_columns, other_columns = once(
        functools.partial(prepare_kernel, n_dp, n_all),
        [input_weight, vectors[None]],
        [sds((r_in, FRONT + MINE), bf16)] * 2,
        cost=8,
        needs=[tokens_send],
        placed=True,
    )
    got = swap(other_columns, "dp", 1)
    half = r_in + r_out // 2
    if fast:
        front_shard, late_shard = once(
            shard_kernel,
            [own_columns, got, output_weight],
            [sds((2, r_in, FRONT), bf16), sds((2, half, width), bf16)],
        )

        def pair(first, second, needs=(), cost=0):
            first, second = (v.reshape((2, -1) + v.shape[-2:]) for v in (first, second))
            count = first.shape[1] + second.shape[1]
            made = sds((2, count) + first.shape[2:], bf16)
            specs = [
                pl.BlockSpec((1,) + v.shape[1:], lambda k: (k, 0, 0, 0)) for v in (first, second, made)
            ]
            run = call(pair_kernel, (2,), specs[:2], specs[2], made, (), cost, needs)
            return run(first, second)

        def across_parts(along_x, along_y, needs=()):
            made = [sds(along_x.shape[1:], bf16)] * 2
            block = (1, 1) + along_x.shape[2:]
            specs = [
                pl.BlockSpec(block, lambda i, half=half: (half, i, 0, 0)) for half in range(2)
            ]
            outs = [pl.BlockSpec(block[1:], lambda i: (i, 0, 0))] * 2
            run = call(halves_kernel, along_x.shape[1:2], specs, outs, made, (), 0, needs)
            return run(along_x, along_y)

        def across_of(send_y, send_x):
            return swap(send_y, "dp", 4), swap(send_x, "dp", 2)

        first_got = swap(front_shard, "ctx", 2)
        inside = enter_line(tokens, tokens_send, needs=[front_shard], cost=8)
        other = swap(inside, "dp", 1)
        end_s = pl.BlockSpec((HALO, width), lambda i: (length // HALO - 1, 0))
        made = sds((HALO, width), bf16)
        ends = call(copy_kernel, (1,), [end_s], all_of([made])[0], made)(inside)
        before = hop(ends, 2)
        near = pair(front_shard, first_got, needs=[ends])
        sides = sides_of(near)
        far = swap(near, "ctx", 1)
        late_shard = after(late_shard, near)
        late_got = swap(late_shard, "ctx", 2)
        across = across_of(*across_parts(*sides, needs=[far, before]))
        far = after(far, *across)
        far_sides = sides_of(far)
        late_near = pair(late_shard, late_got, needs=[far], cost=8)
        far_across_send = across_parts(*far_sides, needs=[late_near])
        far_across = across_of(*far_across_send)
        late_far = swap(late_near, "ctx", 1)
        before_other = swap(before, "dp", 1)
        late_own = after(pair(late_near, late_far, needs=far_across_send, cost=8), *far_across)
        front_pieces = [near, *sides, *across, far, *far_sides, *far_across]
    else:
        shard = ordered(own_columns, got, core, 0)
        near = gather_line(shard[:, :, :FRONT], z, n_ctx, 1)
        far = swap(near, "ctx", 1)
        halves = gather_rest(near, far, z, n_ctx, q, n_q)
        front_pieces = [jnp.stack(halves, axis=1).reshape(width, FRONT)]
        inside = enter_line(tokens, tokens_send)
        other = swap(inside, "dp", 1)
        before = hop(inside[length - HALO :], 2)
        before_other = swap(before, "dp", 1)
        out_halves = output_weight.reshape(2, r_out // 2, width)
        late_shard = jnp.concatenate([shard[:, :, FRONT:], out_halves], axis=1)
        late_near = gather_line(late_shard, z, n_ctx, 1)
        late_far = swap(late_near, "ctx", 1)
        first, second = gather_rest(late_near, late_far, z, n_ctx, q, n_q)
        w_gate = jnp.stack([first[:, :, :r_in], second[:, :, :r_in]], axis=1).reshape(width, MINE)
        w_out = jnp.stack([first[:, :, r_in:], second[:, :, r_in:]], axis=2).reshape(MINE, width)

    ex = np.arange(LANES)[:, None] == (np.arange(MINE)[None] // HEAD)
    ex = ex.astype(ml_dtypes.bfloat16)
    pairs = [ex[:, strip_of(n)] for n in range(PAIRS) for _ in range(2)]
    pairs = jnp.asarray(np.concatenate(pairs, axis=1))
    ex = jnp.asarray(np.concatenate([ex, ex], axis=0))
    tri = np.arange(BLOCK)[:, None] >= np.arange(BLOCK)[None]
    tri = jnp.asarray(tri.astype(ml_dtypes.bfloat16))
    heads_in = lanes(jnp.stack([step_bias, decay_log, skip_gain]).astype(f32), 8)
    w_front, kw, gain, norm_full, heads, skip, pick = once(
        functools.partial(front_weights_kernel, n_dp, n_ctx, r_in),
        [heads_in, ex, *map(main, front_pieces)],
        [pltpu.HBM((width, FRONT), bf16), sds((8, CONVD)), sds((1, MINE)), sds((1, width)),
         sds((8, LANES)), sds((1, MINE)), sds((LANES, LANES), bf16)],
        [pltpu.VMEM((width, LANES), f32), pltpu.VMEM((8, XBC), f32), pltpu.VMEM((1, INNER), f32)],
        cost=8,
        needs=[late_own, before_other] if fast else (),
        placed=True,
    )
    if fast:
        late_sides = sides_of(late_own)
    cot_send = piece_to_send(cotangent, needs=[w_front])

    grid = (seqs, blocks)

    def here(shape, back=False):
        lead = len(shape)
        if back:
            return pl.BlockSpec(shape, lambda j, i: (j * blocks + blocks - 1 - i,) + (0,) * (lead - 1))
        return pl.BlockSpec(shape, lambda j, i: (j * blocks + i,) + (0,) * (lead - 1))

    def per_seq(shape):
        return pl.BlockSpec(shape, lambda j, i: (j,) + (0,) * (len(shape) - 1))

    def fixed(shape):
        return pl.BlockSpec(shape, lambda j, i: (0,) * len(shape))

    mine_s = pl.BlockSpec((BLOCK, width), lambda j, i: (i * (1 - j) + (blocks - 1) * j, 0))
    other_s = pl.BlockSpec((BLOCK, width), lambda j, i: (i * j, 0))
    part_s = sds((length, width), bf16)
    steps_n = seqs * blocks
    wide, heads_s, both = (BLOCK, MINE), (BLOCK, LANES), (BLOCK, 2 * STATE)
    state_s, row8 = (1, STATE, MINE), (1, 8, MINE)
    conv_specs = [
        fixed((8, CONVD)),
        fixed((8, LANES)),
        fixed((LANES, LANES)),
        fixed((BLOCK, BLOCK)),
        fixed((2 * LANES, MINE)),
        fixed((LANES, 2 * MINE)),
    ]
    conv_args = (kw, heads, pick, tri, ex, pairs)
    ext_front = per_seq((1, length + HALO, FRONT))
    front_s = fixed((width, FRONT))
    whole_s, halo_s = fixed((length, width)), fixed((HALO, width))
    normed, px, x, u, bc, cum, cumt, entry, entry_factor, state_total, state_decay = call(
        features_kernel,
        grid,
        [whole_s, whole_s, halo_s, halo_s, fixed((1, width)), front_s] + conv_specs,
        [here((BLOCK, width)), ext_front, here(wide), here(wide), here(both), here(heads_s),
         here((1, LANES, BLOCK)), here(state_s), here(row8), per_seq(state_s), per_seq(row8)],
        [pltpu.HBM((rows, width), bf16), pltpu.HBM((seqs, length + HALO, FRONT), bf16),
         pltpu.HBM((rows, MINE), bf16), pltpu.HBM((rows, MINE), bf16),
         pltpu.HBM((rows, 2 * STATE), bf16), pltpu.HBM((rows, LANES)  , f32),
         pltpu.HBM((steps_n, LANES, BLOCK), f32), pltpu.HBM((steps_n, STATE, MINE), bf16), sds((steps_n, 8, MINE)),
         sds((seqs, STATE, MINE), bf16), sds((seqs, 8, MINE))],
        [pltpu.VMEM((STATE, MINE), f32), pltpu.VMEM((1, MINE), f32),
         pltpu.VMEM((BLOCK + HALO, CONVD), f32), pltpu.VMEM((BLOCK, MINE), bf16)],
        cost=16,
        needs=[cot_send],
    )(main(inside), main(other), before, before_other, norm_full, main(w_front), *conv_args)

    cot = enter_line(cotangent, cot_send, needs=[state_total])
    cot_other = swap(cot, "dp", 1)

    def relay(local, decay, steps):
        received = hop(local, steps)
        for _ in range(n_ctx // 2 - 2):
            received = hop((decay[:, :1] * received.astype(f32) + local.astype(f32)).astype(bf16), steps)
        return received

    incoming = relay(state_total, state_decay, 2)
    late_across_send = across_parts(*late_sides, needs=[cot]) if fast else ()
    y = call(
        within_kernel,
        grid,
        [here(wide), here(both), here(heads_s), here((1, LANES, BLOCK))],
        here(wide),
        sds((rows, MINE), bf16),
        cost=8,
        needs=late_across_send,
    )(u, bc, cum, cumt)

    if fast:
        late_across = across_of(*late_across_send)
        w_gate, w_out = once(
            functools.partial(late_weights_kernel, n_ctx, r_in),
            [*map(main, (late_own, *late_sides, *late_across))],
            [sds((width, MINE), bf16), sds((MINE, width), bf16)],
            placed=True,
            needs=[y],
        )

    mix, gate_raw, ds, entering, sums = call(
        gate_kernel,
        grid,
        [here((BLOCK, width)), mine_s, other_s, fixed((width, MINE)),
         fixed((MINE, width)), here(wide), here(wide), here(both), here(heads_s),
         here(state_s), here(row8), per_seq(state_s), fixed((1, MINE)), fixed((1, MINE)),
         fixed((2 * LANES, MINE))],
        [here(wide), here(wide), here(wide), here(state_s),
         pl.BlockSpec((8, BLOCK), lambda j, i: (0, j * blocks + i))],
        [pltpu.HBM((rows, MINE), bf16)] * 3
        + [pltpu.HBM((steps_n, STATE, MINE), bf16), sds((8, rows))],
        cost=16,
    )(normed, cot, cot_other, w_gate, w_out, y, x, bc, cum, entry, entry_factor, incoming, skip, gain, ex)
    sums_got = swap(sums, "dp", 1)

    scaled, dy, dz, inner, leaving, leave_factor, grad_send, gain_sum, skip_sum = call(
        mixture_kernel,
        grid,
        [here(wide, True)] * 4
        + [here(both, True), here(heads_s, True)]
        + [pl.BlockSpec((8, BLOCK), lambda j, i: (0, j * blocks + blocks - 1 - i)),
           pl.BlockSpec((8, BLOCK), lambda j, i: (0, (1 - j) * blocks + blocks - 1 - i))]
        + [fixed((1, MINE)), fixed((1, MINE)), fixed((2 * LANES, MINE)), fixed((LANES, 2 * MINE))],
        [here(wide, True)] * 3
        + [here(heads_s, True), here(state_s, True), here(row8, True), per_seq(state_s),
           fixed((1, MINE)), fixed((1, MINE))],
        [sds((rows, MINE), bf16)] * 3
        + [sds((rows, LANES)), sds((steps_n, STATE, MINE), bf16), sds((steps_n, 8, MINE)),
           sds((seqs, STATE, MINE), bf16), sds((1, MINE)), sds((1, MINE))],
        [pltpu.VMEM((STATE, MINE), f32), pltpu.VMEM((1, MINE), f32), pltpu.VMEM((BLOCK, MINE), bf16)],
        cost=12,
    )(*map(main, (mix, gate_raw, ds, x, bc, cum)), sums, sums_got, skip, gain, ex, pairs)
    grad_incoming = relay(grad_send, state_decay, -2)

    def parts_of(rows_n, columns):
        wide_part, narrow = (2, n_ctx, rows_n, columns), (n_ctx, rows_n, columns)
        return [sds(shape, bf16) for shape in [wide_part] * 3 + [narrow] * 2]

    made = parts_of(half, width) if fast else [sds((width, MINE), bf16), sds((MINE, width), bf16)]
    out_mine, out_other, du, dbc, *late_parts = call(
        functools.partial(middle_kernel, n_ctx, r_in),
        grid,
        [smem, here((BLOCK, width)), here(wide), here(wide), mine_s, other_s, fixed((MINE, width)),
         here(wide), here(wide), here(both), here(heads_s), here((1, LANES, BLOCK))],
        [mine_s, other_s, here(wide), here(both)] + all_of(made),
        [part_s, part_s, sds((rows, MINE), bf16), sds((rows, 2 * STATE))] + made,
        [pltpu.VMEM((width, MINE), f32), pltpu.VMEM((MINE, width), f32)],
        cost=24,
    )(where, normed, dz, scaled, cot, cot_other, w_out, u, dy, bc, cum, cumt)

    def join_of(along_x, along_y, got_x, got_y, needs=()):
        return add(after(along_x, *needs), got_y[0]), add(along_y, got_x[0])

    def own_of(own, got_x, got_y, last_x, last_y, needs=()):
        own = after(own, *needs)
        far_n = n_ctx // 2
        return [
            jnp.stack(
                [
                    add(own[0, part], got_y[1, part], last_x[part]),
                    add(own[1, part], got_x[1, part], last_y[part]),
                ]
            )
            for part in (slice(0, far_n), slice(far_n, n_ctx))
        ]

    def fold_of(near_part, got):
        return [add(near_part[:, slot], got[:, slot]) for slot in range(2)]

    if fast:
        late_first = swap(late_parts[1], "dp", 2), swap(late_parts[2], "dp", 4)

    gp, rim, tail, kw_sum, heads_sum = call(
        features_back_kernel,
        grid,
        [ext_front]
        + conv_specs
        + [here(wide, True), here(wide, True), here(wide, True), here(both, True),
           here(heads_s, True), here(heads_s, True), here(state_s, True), here(state_s, True),
           here(row8, True), per_seq(state_s), fixed((1, MINE))],
        [pl.BlockSpec((1, BLOCK, FRONT), lambda j, i: (j, blocks - 1 - i, 0)),
         per_seq((1, 8, CONVD)), per_seq((1, 16, CONVD)), fixed((8, CONVD)), fixed((8, LANES))],
        [pltpu.HBM((seqs, length, FRONT), bf16), sds((seqs, 8, CONVD)),
         sds((seqs, 16, CONVD)), sds((8, CONVD)), sds((8, LANES))],
        [pltpu.VMEM((8, CONVD), f32), pltpu.VMEM((BLOCK + HALO, CONVD), f32),
         pltpu.VMEM((BLOCK + 8, CONVD), f32), pltpu.VMEM((BLOCK, MINE), f32),
         pltpu.VMEM((BLOCK, MINE), bf16), pltpu.VMEM((BLOCK, MINE), bf16)],
        cost=24,
    )(px, *conv_args, u, dy, du, dbc, inner, cum, entering, leaving, leave_factor, grad_incoming, skip)

    out_keep, out_send = leave_cores(out_mine, out_other, needs=[gp])
    out_got = swap(out_send, "ctx", 1)
    rim = hop(rim, -2)
    if fast:
        late_second = join_of(late_parts[3], late_parts[4], *late_first, needs=[gp])
        late_last = sides_of_each(*late_second)
    seq_wide = pl.BlockSpec((length, MINE), lambda j: (j, 0))
    seq_gp = pl.BlockSpec((1, length, FRONT), lambda j: (j, 0, 0))
    rims = [pl.BlockSpec((1, n, CONVD), lambda j: (j, 0, 0)) for n in (16, 8)]
    back_mine, back_other, norm_sum = call(
        normed_grads_kernel,
        (seqs,),
        all_of([inside, other]) + [seq_wide] + all_of([w_gate]) + [seq_gp] + rims + all_of([w_front]),
        all_of([part_s, part_s, sds((1, width))]),
        [part_s, part_s, sds((1, width))],
        [pltpu.VMEM((length, FRONT), bf16)],
        cost=12,
        needs=[*late_second, out_send] if fast else (),
    )(*map(main, (inside, other, dz, w_gate, gp)), tail, rim, main(w_front))
    if fast:
        late_near, late_far = own_of(late_parts[0], *late_first, *late_last, needs=[back_mine])
        late_got = swap(late_far, "ctx", 1)
    made = parts_of(r_in, CONVD) if fast else [sds((width, CONVD), bf16)]
    d_step, *front_parts = call(
        functools.partial(front_grads_kernel, n_ctx, r_in),
        (seqs,),
        [smem, seq_wide, seq_gp] + rims,
        all_of([sds((width, LANES))] + made),
        [sds((width, LANES))] + made,
        [pltpu.VMEM((width, FRONT), f32), pltpu.VMEM((length, FRONT), bf16)],
        cost=10,
        needs=[late_far] if fast else (),
    )(where, main(normed), main(gp), tail, rim)
    if fast:
        front_first = swap(front_parts[1], "dp", 2), swap(front_parts[2], "dp", 4)
    back_keep, back_send = leave_cores(back_mine, back_other, needs=[d_step])
    back_got = swap(back_send, "ctx", 1)

    def finish(kernel, arrays, more, dtype, needs, cost):
        block_s = pl.BlockSpec((1, piece, width), lambda j: (j, 0, 0))
        specs = [smem] + [block_s] * len(arrays) + all_of(more)
        made = sds((seqs, piece, width), dtype)
        return call(kernel, (seqs,), specs, block_s, made, (), cost, needs)(where, *arrays, *more)

    packed = once(
        functools.partial(pack_kernel, n_dp),
        [norm_sum, kw_sum, gain_sum, heads_sum, skip_sum, d_step, pick, pairs],
        sds((n_all, 16, LANES)),
        [pltpu.VMEM((8, XBC), f32), pltpu.VMEM((1, INNER), f32)],
        cost=8,
        needs=[back_send],
        placed=True,
    )
    packed_got = lax.all_to_all(packed, every, 0, 0)
    activations = finish(
        activations_kernel, [tokens], [out_keep, out_got], bf16, [packed], 8
    )
    if fast:
        front_second = join_of(front_parts[3], front_parts[4], *front_first, needs=[activations])
        front_last = sides_of_each(*front_second)
        late_keep, late_send = fold_of(late_near, late_got)
        late_got = swap(late_send, "ctx", 2)
    tokens_grad = finish(
        tokens_grad_kernel,
        [tokens, cotangent],
        [back_keep, back_got, norm_full],
        f32,
        [*front_second] if fast else (),
        8,
    )
    if fast:
        front_near, front_far = own_of(
            front_parts[0], *front_first, *front_last, needs=[tokens_grad]
        )
        front_keep, front_send = fold_of(front_near, swap(front_far, "ctx", 1))
        front_got = swap(front_send, "ctx", 2)
    sums = once(
        sums_kernel, [packed_got], sds((16, LANES)), needs=[front_send] if fast else (), cost=8
    )
    if fast:
        own, send, output_weight_grad = once(
            ends_grads_kernel,
            [front_keep, front_got, late_keep, late_got],
            [sds((r_in, CONVD + MINE), bf16)] * 2 + [sds((r_out, width))],
            needs=[sums],
        )
    else:
        d_gate, d_out = late_parts
        d_out = d_out.reshape(n_q, n_ctx, 2, r_out // 2, width)
        d_gate = d_gate.reshape(n_q, 2, n_ctx, r_in, MINE)
        halves = [
            jnp.concatenate([d_gate[:, which], d_out[:, :, which]], axis=2) for which in range(2)
        ]
        late = scatter_both(*halves, z, n_ctx, q, n_q)
        d_conv = front_parts[0].reshape(n_q, 2, n_ctx, r_in, CONVD)
        early = scatter_both(d_conv[:, 0], d_conv[:, 1], z, n_ctx, q, n_q)
        both_cores = jnp.concatenate([early, late[:, :r_in]], axis=2)
        own, send = choose(both_cores, core, 0), choose(both_cores, 1 - core, 0)
        output_weight_grad = late[:, r_in:].reshape(r_out, width).astype(f32)
    got = swap(send, "dp", 1)
    input_weight_grad = once(
        functools.partial(input_grad_kernel, n_dp),
        [own, got, sums],
        sds((r_in, INNER + XBC + HEADS)),
        placed=True,
    )
    head_sums = sums[7, : 3 * HEADS].reshape(3, HEADS)
    return (
        activations,
        tokens_grad,
        sums[6, :r_in],
        input_weight_grad,
        sums[:CONV, : XBC // n_all],
        sums[CONV, : XBC // n_all],
        head_sums[0],
        head_sums[1],
        head_sums[2],
        sums[5, : INNER // n_all],
        output_weight_grad,
    )


def solution(mesh):
    data, rows_spec, vector = P("dp", "ctx", None), P(("dp", "ctx"), None), P(("dp", "ctx"))
    taps = P(None, ("dp", "ctx"))
    return jax.shard_map(
        on_device,
        mesh=mesh,
        in_specs=(data, data, vector, rows_spec, taps, vector, P(), P(), P(), vector, rows_spec),
        out_specs=(data, data, vector, rows_spec, taps, vector, P(), P(), P(), vector, rows_spec),
        check_vma=False,
    )
```

profile of v0, /device:TPU:0, one launch (start us, length us, event | category | flops | bytes accessed | tf_op | source)
XLA Modules:
  0.0 313.2 jit_solution(4530472395121350887)
XLA Ops:
  2.6 3.1 collective-permute-start
  13.6 7.9 %collective-permute-done.refs_2_ = bf16[256,1024]{1,0:T(8,128)(2,1)S(1)} collective-permute-done((bf16[256,1024]{1,0:T(8,128)(2,1)S(1)}, bf16[256,1024]{1,0:T(8,128)(2,1)S(1)}, u32[]{:S(2)}, u32[]{:S(2)}) %collective-permute-start) | collective-permute-done | bytes 524320 | tf_op jit(solution)/shard_map/ppermute | solution.py:33
  32.3 7.7 %collective-permute-done.3.refs_3_.refs_2_ = bf16[16,1024]{1,0:T(8,128)(2,1)S(1)} collective-permute-done((bf16[16,1024]{1,0:T(8,128)(2,1)S(1)}, bf16[16,1024]{1,0:T(8,128)(2,1)S(1)}, u32[]{:S(2)}, u32[]{:S(2)}) %collective-permute-start.3) | collective-permute-done | bytes 32800 | tf_op jit(solution)/shard_map/ppermute | solution.py:39
  41.4 4.3 %collective-permute-done.10.refs_2_.refs_7_ = bf16[2,32,1408]{2,1,0:T(8,128)(2,1)S(1)} collective-permute-done((bf16[2,32,1408]{2,1,0:T(8,128)(2,1)S(1)}, bf16[2,32,1408]{2,1,0:T(8,128)(2,1)S(1)}, u32[]{:S(2)}, u32[]{:S(2)}) %collective-permute-start.10) | collective-permute-done | bytes 180256 | tf_op jit(solution)/shard_map/ppermute | solution.py:33
  50.2 5.4 %collective-permute-done.11.refs_0_.refs_9_ = bf16[2,2,32,1408]{3,2,1,0:T(8,128)(2,1)S(1)} collective-permute-done((bf16[2,2,32,1408]{3,2,1,0:T(8,128)(2,1)S(1)}, bf16[2,2,32,1408]{3,2,1,0:T(8,128)(2,1)S(1)}, u32[]{:S(2)}, u32[]{:S(2)}) %collective-permute-start.11) | collective-permute-done | bytes 360480 | tf_op jit(solution)/shard_map/ppermute | solution.py:33
  60.8 5.1 %collective-permute-done.14.refs_1_.refs_11_ = bf16[2,32,1408]{2,1,0:T(8,128)(2,1)S(1)} collective-permute-done((bf16[2,32,1408]{2,1,0:T(8,128)(2,1)S(1)}, bf16[2,32,1408]{2,1,0:T(8,128)(2,1)S(1)}, u32[]{:S(2)}, u32[]{:S(2)}) %collective-permute-start.14) | collective-permute-done | bytes 180256 | tf_op jit(solution)/shard_map/ppermute | solution.py:33
  70.0 3.6 %shard_map.234 = (bf16[1024,1408]{1,0:T(8,128)(2,1)}, f32[8,1280]{1,0:T(8,128)S(1)}, f32[1,1024]{1,0:T(1,128)S(1)}, f32[1,1024]{1,0:T(1,128)S(1)}, f32[8,128]{1,...) custom-call(s32[3]{0:T(128)S(1)} %pad_add_fusion.refs_0_, f32[8,128]{1,0:T(8,128)S(1)} %fusion.35.refs_1_, ...), custom_call_target="tpu_custom_call" | custom-call | flops 8000000000 | bytes 28000000 | tf_op jit(solution)/shard_map/pallas_call | solution.py:817
  78.2 20.7 %shard_map.236 = (bf16[1024,1024]{1,0:T(8,128)(2,1)}, bf16[2,528,1408]{2,1,0:T(8,128)(2,1)}, bf16[1024,1024]{1,0:T(8,128)(2,1)}, bf16[1024,1024]{1,0:T(8,128)(2,...) custom-call(bf16[512,1024]{1,0:T(8,128)(2,1)} %bitcast.136, ...), custom_call_target="tpu_custom_call" | custom-call | flops 16000000000 | bytes 56000000 | tf_op jit(solution)/shard_map/pallas_call | solution.py:817
  99.9 4.9 %collective-permute-start.23 = (bf16[2,128,1024]{2,1,0:T(8,128)(2,1)S(1)}, bf16[2,128,1024]{2,1,0:T(8,128)(2,1)S(1)}, u32[]{:S(2)}, u32[]{:S(2)}) collective-permute-start(bf16[2,128,1024]{2,1,0:T(8,128)(2,1)S(1)} %get-tuple-element.94.refs_3_), channel_id=1, source_target_pairs={{0,2},{1,3},{4,6},{5,7},{8,10},{9,11},{12,14},{13,15},{16,18},{17,... | collective-permute-start | bytes 1572872 | tf_op jit(solution)/shard_map/ppermute | solution.py:39
  107.1 4.9 %shard_map.239.refs_6_.refs_5_ = bf16[1024,1024]{1,0:T(8,128)(2,1)S(1)} custom-call(bf16[1024,1024]{1,0:T(8,128)(2,1)S(1)} %copy-done.45, bf16[1024,256]{1,0:T(8,128)(2,1)S(1)} %copy-done.54, f32[1024,128]{1,0:T(8,128)S(1)} %copy-done.52, f32[4,128,256]{2,1,0:T(8,128)S(1)} %copy-done.56, bf16[4,64,1024]{2,1,0:T(8,128)(2,1)S(1)} %get-tuple-element.95.refs_4_, ...), custom_call_target="tpu_custom_call" | custom-call | flops 8000000000 | bytes 28000000 | tf_op jit(solution)/shard_map/pallas_call | solution.py:817
  112.1 6.8 %collective-permute-done.21.refs_4_ = bf16[4,64,1024]{2,1,0:T(8,128)(2,1)S(1)} collective-permute-done((bf16[4,64,1024]{2,1,0:T(8,128)(2,1)S(1)}, bf16[4,64,1024]{2,1,0:T(8,128)(2,1)S(1)}, u32[]{:S(2)}, u32[]{:S(2)}) %collective-permute-start.21) | collective-permute-done | bytes 524320 | tf_op jit(solution)/shard_map/ppermute | solution.py:33
  123.0 9.3 %shard_map.241 = (bf16[1024,1024]{1,0:T(8,128)(2,1)}, bf16[1024,1024]{1,0:T(8,128)(2,1)}, bf16[1024,1024]{1,0:T(8,128)(2,1)}, bf16[4,128,1024]{2,1,0:T(8,128)(2,1)}, f32[8,1024]{1,0:T(8,128)S(1)}) custom-call(bf16[1024,1024]{1,0:T(8,128)(2,1)S(1)} %copy-done.48, bf16[512,1024]{1,0:T(8,128)(2,1)S(1)} %bitcast.132, ...), custom_call_target="tpu_custom_call" | custom-call | flops 16000000000 | bytes 56000000 | tf_op jit(solution)/shard_map/pallas_call | solution.py:817
  135.7 11.0 %shard_map.242 = (bf16[1024,1024]{1,0:T(8,128)(2,1)S(1)}, bf16[1024,1024]{1,0:T(8,128)(2,1)S(1)}, bf16[1024,1024]{1,0:T(8,128)(2,1)S(1)}, f32[1024,128]{1,0:T(8,...) custom-call(bf16[1024,1024]{1,0:T(8,128)(2,1)} %get-tuple-element.10, ...), custom_call_target="tpu_custom_call" | custom-call | flops 12000000000 | bytes 42000000 | tf_op jit(solution)/shard_map/pallas_call | solution.py:817
  148.1 21.5 %shard_map.243 = (bf16[512,1024]{1,0:T(8,128)(2,1)S(1)}, bf16[512,1024]{1,0:T(8,128)(2,1)}, bf16[1024,1024]{1,0:T(8,128)(2,1)S(1)}, f32[1024,256]{1,0:T(8,128)S(...) custom-call(s32[3]{0:T(128)S(1)} %pad_add_fusion.refs_0_, ...), custom_call_target="tpu_custom_call" | custom-call | flops 24000000000 | bytes 84000000 | tf_op jit(solution)/shard_map/pallas_call | solution.py:817
  174.7 27.4 %shard_map.244 = (bf16[2,512,1408]{2,1,0:T(8,128)(2,1)}, f32[2,8,1280]{2,1,0:T(8,128)S(1)}, f32[2,16,1280]{2,1,0:T(8,128)S(1)}, f32[8,1280]{1,0:T(8,128)S(1)}, f32[8,128]{1,0:T(8,128)S(1)}) custom-call(bf16[2,528,1408]{2,1,0:T(8,128)(2,1)S(1)} %copy-done.51, f32[8,1280]{1,0:T(8,128)S(1)} %get-tuple-element.90.refs_6_.refs_1_, ...), custom_call_target="tpu_custom_call" | custom-call | flops 24000000000 | bytes 84000000 | tf_op jit(solution)/shard_map/pallas_call | solution.py:817
  212.5 3.2 %collective-permute-start.27 = (bf16[256,1024]{1,0:T(8,128)(2,1)}, bf16[256,1024]{1,0:T(8,128)(2,1)}, u32[]{:S(2)}, u32[]{:S(2)}) collective-permute-start(bf16[256,1024]{1,0:T(8,128)(2,1)} %get-tuple-element.163.refs_10_), channel_id=1, source_target_pairs={{0,1},{1,0},{2,3},{3,2},{4,5},{5,4},{6,7},{7,6},{8,9},{9,8},{10,11... | collective-permute-start | bytes 1572872 | tf_op jit(solution)/shard_map/ppermute | solution.py:33
  215.8 11.7 %shard_map.247 = (bf16[512,1024]{1,0:T(8,128)(2,1)S(1)}, bf16[512,1024]{1,0:T(8,128)(2,1)}, f32[1,1024]{1,0:T(1,128)S(1)}) custom-call(bf16[512,1024]{1,0:T(8,128)(2,1)} %bitcast.137, bf16[512,1024]{1,0:T(8,128)(2,1)} %collective-permute-done.2.refs_1_, bf16[1024,1024]{1,0:T(8,128)(2,1)} %copy-done.47, bf16[1024,1024]{1,0:T(8,128)(2,1)} %copy-done.30, ...), custom_call_target="tpu_custom_call" | custom-call | flops 12000000000 | bytes 42000000 | tf_op jit(solution)/shard_map/pallas_call | solution.py:817
  228.5 3.3 %fusion.17 = (bf16[1,2,64,1024]{3,2,0,1:T(8,128)(2,1)}, bf16[1,2,64,1024]{3,2,1,0:T(8,128)(2,1)S(1)}, bf16[1,2,64,1024]{3,2,1,0:T(8,128)(2,1)S(1)}, bf16[1,2,64,1024]{3,2,0,1:T(8,128)(2,1)}) fusion(bf16[4,64,1024]{2,1,0:T(8,128)(2,1)} %collective-permute-done.32, bf16[2,4,64,1024]{3,2,1,0:T(8,128)(2,1)} %collective-permute-done.30, ...), kind=kLoop, calls=%fused_computation.49 | loop fusion | flops 3145728 | bytes 4194304 | tf_op jit(solution)/shard_map/stack | solution.py:1129
  232.7 7.7 %shard_map.249 = (f32[1024,128]{1,0:T(8,128)S(1)}, bf16[2,4,32,1280]{3,2,1,0:T(8,128)(2,1)S(1)}, bf16[2,4,32,1280]{3,2,1,0:T(8,128)(2,1)}, bf16[2,4,32,1280]{3,2...) custom-call(s32[3]{0:T(128)S(1)} %pad_add_fusion.refs_0_, ...), custom_call_target="tpu_custom_call" | custom-call | flops 10000000000 | bytes 35000000 | tf_op jit(solution)/shard_map/pallas_call | solution.py:817
  253.9 6.3 %collective-permute-done.36 = bf16[2,4,32,1280]{3,2,1,0:T(8,128)(2,1)} collective-permute-done((bf16[2,4,32,1280]{3,2,1,0:T(8,128)(2,1)}, bf16[2,4,32,1280]{3,2,1,0:T(8,128)(2,1)}, u32[]{:S(2)}, u32[]{:S(2)}) %collective-permute-start.36) | collective-permute-done | bytes 655392 | tf_op jit(solution)/shard_map/ppermute | solution.py:33
  267.7 3.1 collective-permute-done.38
  275.8 5.8 %all-to-all-start = ((f32[32,16,128]{2,1,0:T(8,128)}), f32[32,16,128]{2,1,0:T(8,128)S(1)}, u32[]{:S(2)}, u32[]{:S(2)}) async-start(f32[32,16,128]{2,1,0:T(8,128)} %shard_map.251.refs_4_), calls=%async_computation | async-start | bytes 524288 | tf_op jit(solution)/shard_map/all_to_all | solution.py:1215
  286.2 5.6 %all-to-all-done.refs_0_ = f32[32,16,128]{2,1,0:T(8,128)S(1)} async-done(((f32[32,16,128]{2,1,0:T(8,128)}), f32[32,16,128]{2,1,0:T(8,128)S(1)}, u32[]{:S(2)}, u32[]{:S(2)}) %all-to-all-start) | async-done | bytes 262176 | tf_op jit(solution)/shard_map/all_to_all | solution.py:1215
  293.5 12.7 %collective-permute-done.42.refs_3_ = bf16[2,64,1024]{2,1,0:T(8,128)(2,1)S(1)} collective-permute-done((bf16[2,64,1024]{2,1,0:T(8,128)(2,1)S(1)}, bf16[2,64,1024]{2,1,0:T(8,128)(2,1)S(1)}, u32[]{:S(2)}, u32[]{:S(2)}) %collective-permute-start.42) | collective-permute-done | bytes 262176 | tf_op jit(solution)/shard_map/ppermute | solution.py:33
  (287 shorter events, 108.1 us)
Async XLA Ops:
  2.6 18.9 %collective-permute-start = (bf16[256,1024]{1,0:T(8,128)(2,1)S(1)}, bf16[256,1024]{1,0:T(8,128)(2,1)S(1)}, u32[]{:S(2)}, u32[]{:S(2)}) collective-permute-start(bf16[256,1024]{1,0:T(8,128)(2,1)S(1)} %shard_map.221.refs_3_), channel_id=1, source_target_pairs={{0,1},{1,0},{2,3},{3,2},{4,5},{5,4},{6,7},{7,6},{8,9},{9,8},{10,11... | collective-permute-start | bytes 1572872 | tf_op jit(solution)/shard_map/ppermute | solution.py:33
  22.5 17.5 %collective-permute-start.6 = (bf16[2,2,32,1408]{3,2,1,0:T(8,128)(2,1)S(1)}, bf16[2,2,32,1408]{3,2,1,0:T(8,128)(2,1)S(1)}, u32[]{:S(2)}, u32[]{:S(2)}) collective-permute-start(bf16[2,2,32,1408]{3,2,1,0:T(8,128)(2,1)S(1)} %shard_map.226.refs_1_.refs_3_), channel_id=1, source_target_pairs={{0,8},{4,12},{8,0},{12,4},{16,24},{20,28},{24,16},{28,20},{1,9},{5... | collective-permute-start | bytes 1081352 | tf_op jit(solution)/shard_map/ppermute | solution.py:33
  27.4 18.9 %collective-permute-start.13 = (bf16[2,64,1024]{2,1,0:T(8,128)(2,1)}, bf16[2,64,1024]{2,1,0:T(8,128)(2,1)S(1)}, u32[]{:S(2)}, u32[]{:S(2)}) collective-permute-start(bf16[2,64,1024]{2,1,0:T(8,128)(2,1)} %shard_map.229), channel_id=1, source_target_pairs={{0,2},{1,3},{2,0},{3,1},{4,6},{5,7},{6,4},{7,5},{8,10},{9,11},{10,... | collective-permute-start | bytes 786440 | tf_op jit(solution)/shard_map/ppermute | solution.py:33
  49.6 28.6 %collective-permute-start.2 = (bf16[512,1024]{1,0:T(8,128)(2,1)S(1)}, bf16[512,1024]{1,0:T(8,128)(2,1)}, u32[]{:S(2)}, u32[]{:S(2)}) collective-permute-start(bf16[512,1024]{1,0:T(8,128)(2,1)S(1)} %bitcast.135), channel_id=1, source_target_pairs={{0,4},{4,0},{8,12},{12,8},{16,20},{20,16},{24,28},{28,24},{1,5},{5... | collective-permute-start | bytes 3145736 | tf_op jit(solution)/shard_map/ppermute | solution.py:33
  49.7 19.1 %collective-permute-start.4 = (bf16[16,1024]{1,0:T(8,128)(2,1)S(1)}, bf16[16,1024]{1,0:T(8,128)(2,1)S(1)}, u32[]{:S(2)}, u32[]{:S(2)}) collective-permute-start(bf16[16,1024]{1,0:T(8,128)(2,1)S(1)} %collective-permute-done.3.refs_3_.refs_2_), channel_id=1, source_target_pairs={{0,4},{4,0},{8,12},{12,8},{16,20},{20,16},{24,28},{28,24},{1,5},{5... | collective-permute-start | bytes 98312 | tf_op jit(solution)/shard_map/ppermute | solution.py:33
  66.6 38.2 %collective-permute-start.19 = (bf16[2,4,64,1024]{3,2,1,0:T(8,128)(2,1)}, bf16[2,4,64,1024]{3,2,1,0:T(8,128)(2,1)S(1)}, u32[]{:S(2)}, u32[]{:S(2)}) collective-permute-start(bf16[2,4,64,1024]{3,2,1,0:T(8,128)(2,1)} %shard_map.233.refs_13_.refs_1_), channel_id=1, source_target_pairs={{0,8},{4,12},{8,0},{12,4},{16,24},{20,28},{24,16},{28,20},{1,9},{5... | collective-permute-start | bytes 3145736 | tf_op jit(solution)/shard_map/ppermute | solution.py:33
  67.3 37.5 %collective-permute-start.20 = (bf16[2,4,64,1024]{3,2,1,0:T(8,128)(2,1)}, bf16[2,4,64,1024]{3,2,1,0:T(8,128)(2,1)S(1)}, u32[]{:S(2)}, u32[]{:S(2)}) collective-permute-start(bf16[2,4,64,1024]{3,2,1,0:T(8,128)(2,1)} %shard_map.233.refs_13_.refs_1_), channel_id=1, source_target_pairs={{0,16},{4,20},{8,24},{12,28},{16,0},{20,4},{24,8},{28,12},{1,17},{... | collective-permute-start | bytes 3145736 | tf_op jit(solution)/shard_map/ppermute | solution.py:33
  76.2 22.8 %collective-permute-start.17 = (bf16[256,1024]{1,0:T(8,128)(2,1)S(1)}, bf16[256,1024]{1,0:T(8,128)(2,1)S(1)}, u32[]{:S(2)}, u32[]{:S(2)}) collective-permute-start(bf16[256,1024]{1,0:T(8,128)(2,1)S(1)} %shard_map.235.refs_12_), channel_id=1, source_target_pairs={{0,1},{1,0},{2,3},{3,2},{4,5},{5,4},{6,7},{7,6},{8,9},{9,8},{10,11... | collective-permute-start | bytes 1572872 | tf_op jit(solution)/shard_map/ppermute | solution.py:33
  99.8 23.1 %collective-permute-start.18 = (bf16[512,1024]{1,0:T(8,128)(2,1)S(1)}, bf16[512,1024]{1,0:T(8,128)(2,1)S(1)}, u32[]{:S(2)}, u32[]{:S(2)}) collective-permute-start(bf16[512,1024]{1,0:T(8,128)(2,1)S(1)} %bitcast.130), channel_id=1, source_target_pairs={{0,4},{4,0},{8,12},{12,8},{16,20},{20,16},{24,28},{28,24},{1,5},{5... | collective-permute-start | bytes 3145736 | tf_op jit(solution)/shard_map/ppermute | solution.py:33
  99.9 23.0 %collective-permute-start.23 = (bf16[2,128,1024]{2,1,0:T(8,128)(2,1)S(1)}, bf16[2,128,1024]{2,1,0:T(8,128)(2,1)S(1)}, u32[]{:S(2)}, u32[]{:S(2)}) collective-permute-start(bf16[2,128,1024]{2,1,0:T(8,128)(2,1)S(1)} %get-tuple-element.94.refs_3_), channel_id=1, source_target_pairs={{0,2},{1,3},{4,6},{5,7},{8,10},{9,11},{12,14},{13,15},{16,18},{17,... | collective-permute-start | bytes 1572872 | tf_op jit(solution)/shard_map/ppermute | solution.py:39
  146.7 28.0 %collective-permute-start.25 = (bf16[2,128,1024]{2,1,0:T(8,128)(2,1)S(1)}, bf16[2,128,1024]{2,1,0:T(8,128)(2,1)S(1)}, u32[]{:S(2)}, u32[]{:S(2)}) collective-permute-start(bf16[2,128,1024]{2,1,0:T(8,128)(2,1)S(1)} %get-tuple-element.123), channel_id=1, source_target_pairs={{2,0},{3,1},{6,4},{7,5},{10,8},{11,9},{14,12},{15,13},{18,16},{19,... | collective-permute-start | bytes 1572872 | tf_op jit(solution)/shard_map/ppermute | solution.py:39
  170.6 34.3 %collective-permute-start.30 = (bf16[2,4,64,1024]{3,2,1,0:T(8,128)(2,1)}, bf16[2,4,64,1024]{3,2,1,0:T(8,128)(2,1)}, u32[]{:S(2)}, u32[]{:S(2)}) collective-permute-start(bf16[2,4,64,1024]{3,2,1,0:T(8,128)(2,1)} %get-tuple-element.131), channel_id=1, source_target_pairs={{0,8},{4,12},{8,0},{12,4},{16,24},{20,28},{24,16},{28,20},{1,9},{5... | collective-permute-start | bytes 3145736 | tf_op jit(solution)/shard_map/ppermute | solution.py:33
  172.2 35.0 %collective-permute-start.29 = (bf16[2,4,64,1024]{3,2,1,0:T(8,128)(2,1)}, bf16[2,4,64,1024]{3,2,1,0:T(8,128)(2,1)}, u32[]{:S(2)}, u32[]{:S(2)}) collective-permute-start(bf16[2,4,64,1024]{3,2,1,0:T(8,128)(2,1)} %get-tuple-element.129), channel_id=1, source_target_pairs={{0,16},{4,20},{8,24},{12,28},{16,0},{20,4},{24,8},{28,12},{1,17},{... | collective-permute-start | bytes 3145736 | tf_op jit(solution)/shard_map/ppermute | solution.py:33
  173.1 36.9 %collective-permute-start.26 = (bf16[512,1024]{1,0:T(8,128)(2,1)}, bf16[512,1024]{1,0:T(8,128)(2,1)}, u32[]{:S(2)}, u32[]{:S(2)}) collective-permute-start(bf16[512,1024]{1,0:T(8,128)(2,1)} %get-tuple-element.125), channel_id=1, source_target_pairs={{0,4},{4,0},{8,12},{12,8},{16,20},{20,16},{24,28},{28,24},{1,5},{5... | collective-permute-start | bytes 3145736 | tf_op jit(solution)/shard_map/ppermute | solution.py:33
  206.2 22.3 %collective-permute-start.32 = (bf16[4,64,1024]{2,1,0:T(8,128)(2,1)S(1)}, bf16[4,64,1024]{2,1,0:T(8,128)(2,1)}, u32[]{:S(2)}, u32[]{:S(2)}) collective-permute-start(bf16[4,64,1024]{2,1,0:T(8,128)(2,1)S(1)} %fusion.refs_9_), channel_id=1, source_target_pairs={{0,16},{4,20},{8,24},{12,28},{16,0},{20,4},{24,8},{28,12},{1,17},{... | collective-permute-start | bytes 1572872 | tf_op jit(solution)/shard_map/ppermute | solution.py:33
  208.4 20.0 %collective-permute-start.31 = (bf16[4,64,1024]{2,1,0:T(8,128)(2,1)S(1)}, bf16[4,64,1024]{2,1,0:T(8,128)(2,1)}, u32[]{:S(2)}, u32[]{:S(2)}) collective-permute-start(bf16[4,64,1024]{2,1,0:T(8,128)(2,1)S(1)} %fusion.1.refs_8_), channel_id=1, source_target_pairs={{0,8},{4,12},{8,0},{12,4},{16,24},{20,28},{24,16},{28,20},{1,9},{5... | collective-permute-start | bytes 1572872 | tf_op jit(solution)/shard_map/ppermute | solution.py:33
  212.5 39.2 %collective-permute-start.27 = (bf16[256,1024]{1,0:T(8,128)(2,1)}, bf16[256,1024]{1,0:T(8,128)(2,1)}, u32[]{:S(2)}, u32[]{:S(2)}) collective-permute-start(bf16[256,1024]{1,0:T(8,128)(2,1)} %get-tuple-element.163.refs_10_), channel_id=1, source_target_pairs={{0,1},{1,0},{2,3},{3,2},{4,5},{5,4},{6,7},{7,6},{8,9},{9,8},{10,11... | collective-permute-start | bytes 1572872 | tf_op jit(solution)/shard_map/ppermute | solution.py:33
  228.4 16.6 %collective-permute-start.33 = (bf16[512,1024]{1,0:T(8,128)(2,1)}, bf16[512,1024]{1,0:T(8,128)(2,1)}, u32[]{:S(2)}, u32[]{:S(2)}) collective-permute-start(bf16[512,1024]{1,0:T(8,128)(2,1)} %get-tuple-element.140), channel_id=1, source_target_pairs={{0,4},{4,0},{8,12},{12,8},{16,20},{20,16},{24,28},{28,24},{1,5},{5... | collective-permute-start | bytes 3145736 | tf_op jit(solution)/shard_map/ppermute | solution.py:33
  232.7 48.9 %collective-permute-start.41 = (bf16[2,2,64,1024]{3,2,0,1:T(8,128)(2,1)}, bf16[2,2,64,1024]{3,2,0,1:T(8,128)(2,1)}, u32[]{:S(2)}, u32[]{:S(2)}) collective-permute-start(bf16[2,2,64,1024]{3,2,0,1:T(8,128)(2,1)} %copy.37), channel_id=1, source_target_pairs={{0,1},{1,0},{2,3},{3,2},{4,5},{5,4},{6,7},{7,6},{8,9},{9,8},{10,11... | collective-permute-start | bytes 1572872 | tf_op jit(solution)/shard_map/ppermute | solution.py:33
  242.8 17.4 %collective-permute-start.36 = (bf16[2,4,32,1280]{3,2,1,0:T(8,128)(2,1)}, bf16[2,4,32,1280]{3,2,1,0:T(8,128)(2,1)}, u32[]{:S(2)}, u32[]{:S(2)}) collective-permute-start(bf16[2,4,32,1280]{3,2,1,0:T(8,128)(2,1)} %get-tuple-element.144), channel_id=1, source_target_pairs={{0,8},{4,12},{8,0},{12,4},{16,24},{20,28},{24,16},{28,20},{1,9},{5... | collective-permute-start | bytes 1966088 | tf_op jit(solution)/shard_map/ppermute | solution.py:33
  244.4 17.7 %collective-permute-start.35 = (bf16[2,4,32,1280]{3,2,1,0:T(8,128)(2,1)}, bf16[2,4,32,1280]{3,2,1,0:T(8,128)(2,1)}, u32[]{:S(2)}, u32[]{:S(2)}) collective-permute-start(bf16[2,4,32,1280]{3,2,1,0:T(8,128)(2,1)} %get-tuple-element.142), channel_id=1, source_target_pairs={{0,16},{4,20},{8,24},{12,28},{16,0},{20,4},{24,8},{28,12},{1,17},{... | collective-permute-start | bytes 1966088 | tf_op jit(solution)/shard_map/ppermute | solution.py:33
  247.8 16.8 %collective-permute-start.34 = (bf16[256,1024]{1,0:T(8,128)(2,1)}, bf16[256,1024]{1,0:T(8,128)(2,1)}, u32[]{:S(2)}, u32[]{:S(2)}) collective-permute-start(bf16[256,1024]{1,0:T(8,128)(2,1)} %get-tuple-element.162.refs_9_), channel_id=1, source_target_pairs={{0,1},{1,0},{2,3},{3,2},{4,5},{5,4},{6,7},{7,6},{8,9},{9,8},{10,11... | collective-permute-start | bytes 1572872 | tf_op jit(solution)/shard_map/ppermute | solution.py:33
  282.9 23.3 %collective-permute-start.42 = (bf16[2,64,1024]{2,1,0:T(8,128)(2,1)S(1)}, bf16[2,64,1024]{2,1,0:T(8,128)(2,1)S(1)}, u32[]{:S(2)}, u32[]{:S(2)}) collective-permute-start(bf16[2,64,1024]{2,1,0:T(8,128)(2,1)S(1)} %get-tuple-element.157), channel_id=1, source_target_pairs={{0,2},{1,3},{2,0},{3,1},{4,6},{5,7},{6,4},{7,5},{8,10},{9,11},{10,... | collective-permute-start | bytes 786440 | tf_op jit(solution)/shard_map/ppermute | solution.py:33
  285.7 23.5 %collective-permute-start.40 = (bf16[2,32,1280]{2,1,0:T(8,128)(2,1)S(1)}, bf16[2,32,1280]{2,1,0:T(8,128)(2,1)S(1)}, u32[]{:S(2)}, u32[]{:S(2)}) collective-permute-start(bf16[2,32,1280]{2,1,0:T(8,128)(2,1)S(1)} %get-tuple-element.166.refs_1_), channel_id=1, source_target_pairs={{0,2},{1,3},{2,0},{3,1},{4,6},{5,7},{6,4},{7,5},{8,10},{9,11},{10,... | collective-permute-start | bytes 491528 | tf_op jit(solution)/shard_map/ppermute | solution.py:33
  (100 other events, 853.1 us)
where the time goes:
time: 319 us; the launch traced here: 313 us
  Pallas kernels  134 us (42%)
  waiting for transfers between devices  79 us (25%)
  starting transfers between devices  60.2 us (19%)
  local copies, waits for them, and re-layouts  22.7 us (7%)
  other arithmetic  15.6 us (5%)
    pallas_call x29, Pallas kernels, call(): return lambda *arrays: made(*arrays, *needs)  134 us
    ppermute x40, waiting for transfers between devices, swap(): return lax.ppermute(value, axis, [(i, i ^ mask) for i in range(count)])  64 us
    ppermute x40, starting transfers between devices, swap(): return lax.ppermute(value, axis, [(i, i ^ mask) for i in range(count)])  44.5 us
    unnamed x158, local copies, waits for them, and re-layouts  17.1 us
    ppermute x4, starting transfers between devices, hop(): return lax.ppermute(value, 'ctx', pairs)  9.96 us
    convert_element_type x8, other arithmetic, add(): return sum((value.astype(f32) for value in values)).astype(bf16)  9.52 us
    ppermute x4, waiting for transfers between devices, hop(): return lax.ppermute(value, 'ctx', pairs)  9.35 us
  transfers between devices with their start and end apart: 45, of which 21 were waited for; matrix products, arithmetic and copies ran while one was open for 7% of the time, Pallas kernels for 35%

commit v1 on v0

--- a/solution.py
+++ b/solution.py
@@ -18,6 +18,9 @@
 BLOCK = 256
 HALO = 16
 LANES = 128
+TILE = 128
+DEEP = BLOCK // 8
+AHEAD = 8 * (CONV - 1)
 MINE = INNER // 2
 PAIRS = MINE // LANES
 CONVD = MINE + 2 * STATE
@@ -174,20 +177,45 @@
     return dot(halves, ex[:, lanes])
 
 
-def pool(value, pairs, strip):
-    return dot_nt(halves_of(value), pairs[:, strip * 2 * LANES : (strip + 1) * 2 * LANES])
+def pool(value, ex):
+    return dot_nt(value, ex[:LANES, :])
+
+
+def sigmoid(value):
+    return 0.5 + 0.5 * jnp.tanh(0.5 * value)
+
+
+def tiles_of(first, last):
+    for number in range(first, last):
+        for row in range(0, BLOCK, TILE):
+            yield slice(row, row + TILE), strip_of(number)
 
 
 def strip_of(number, size=LANES):
     return slice(number * size, (number + 1) * size)
 
 
-def conv_rows(px, block):
-    return px[pl.ds(pl.multiple_of(block * BLOCK, BLOCK), BLOCK + HALO), :]
-
-
-def conv_strip(wide, kw, lanes):
-    taps = [wide[HALO - CONV + 1 + k : HALO - CONV + 1 + k + BLOCK, lanes] for k in range(CONV)]
+def token_of(row):
+    return (row % 8) * DEEP + row // 8
+
+
+def last_tokens(block, rows):
+    picked = [block[BLOCK - AHEAD + 8 * k + 7 : BLOCK - AHEAD + 8 * k + 8] for k in range(CONV - 1)]
+    empty = jnp.zeros((rows - CONV + 1, block.shape[1]), block.dtype)
+    return jnp.concatenate([empty] + picked, axis=0)
+
+
+def widen(rows, wide):
+    values = rows[:, :CONVD].astype(f32)
+    wide[AHEAD:, :] = values[HALO:]
+    for k in range(CONV - 1):
+        ahead = values[HALO - CONV + 1 + k : HALO - CONV + 2 + k]
+        begin = HALO + BLOCK - AHEAD + 8 * k
+        wide[8 * k : 8 * k + 8, :] = jnp.concatenate([ahead, values[begin : begin + 7]], axis=0)
+
+
+def conv_tile(wide, kw, rows, lanes):
+    taps = [wide[rows.start + 8 * k : rows.start + 8 * k + TILE, lanes] for k in range(CONV)]
     total = kw[CONV : CONV + 1, lanes]
     for k in range(CONV):
         total = total + kw[k : k + 1, lanes] * taps[k]
@@ -205,24 +233,24 @@
     return biased, step, -step * rate, rate
 
 
-def features_kernel(mine, other, before, before_other, norm, front, kw, heads, pick, tri, ex, pairs,
+def features_kernel(mine, other, before, before_other, norm, front, kw, heads, pick, tri, ex,
                     normed_o, px_o, x_o, u_o, bc_o, cum_o, cumt_o, entry_o, factor_o, total_o,
-                    decay_o, state, passed, wide, weighted):
+                    decay_o, state, passed, wide, weighted, stepped, left):
     j, block = pl.program_id(0), pl.program_id(1)
-    start = pl.multiple_of(block * BLOCK, BLOCK)
-    early = pl.multiple_of(jnp.maximum(start - HALO, 0), HALO)
 
     def rows_of(begin, count):
+        begin = pl.multiple_of(begin, count)
         return jnp.where(j == 0, mine[pl.ds(begin, count), :], other[pl.ds(begin, count), :])
 
     ahead = jnp.where(j == 0, before[...], before_other[...])
-    ahead = jnp.where(block == 0, ahead, rows_of(early, HALO))
-    residual = jnp.concatenate([ahead, rows_of(start, BLOCK)], axis=0).astype(f32)
+    within = rows_of(jnp.maximum(block - 1, 0) * BLOCK, BLOCK)
+    ahead = jnp.where(block == 0, ahead.astype(f32), last_tokens(within.astype(f32), HALO))
+    residual = jnp.concatenate([ahead, rows_of(block * BLOCK, BLOCK).astype(f32)], axis=0)
     normed = (residual * inverse_rms(residual) * norm[...]).astype(bf16)
     normed_o[...] = normed[HALO:]
     rows = dot(normed, front[...]).astype(bf16)
-    px_o[0, pl.ds(start, BLOCK + HALO), :] = rows
-    wide[...] = rows[:, :CONVD].astype(f32)
+    px_o[0] = rows
+    widen(rows, wide)
 
     @pl.when(block == 0)
     def _():
@@ -238,18 +266,18 @@
     whole = halves_of(jnp.broadcast_to(jnp.exp(last), (16, LANES)))
     entry_o[0] = state[...].astype(bf16)
     factor_o[0] = jnp.broadcast_to(passed[...], (8, MINE))
-    for number in range(2):
-        lanes = strip_of(PAIRS + number)
-        total, _ = conv_strip(wide, kw, lanes)
-        bc_o[:, strip_of(number)] = (total * jax.nn.sigmoid(total)).astype(bf16)
-    for number in range(PAIRS):
-        lanes = strip_of(number)
-        total, _ = conv_strip(wide, kw, lanes)
-        x = total * jax.nn.sigmoid(total)
-        x_o[:, lanes] = x.astype(bf16)
-        u = (x * spread(step, ex, lanes)).astype(bf16)
-        u_o[:, lanes] = u
-        weighted[:, lanes] = (u.astype(f32) * spread(remaining, ex, lanes)).astype(bf16)
+    for rows_t, lanes in tiles_of(PAIRS, PAIRS + 2):
+        total, _ = conv_tile(wide, kw, rows_t, lanes)
+        bc_o[rows_t, lanes.start - MINE : lanes.stop - MINE] = (total * sigmoid(total)).astype(bf16)
+    stepped[...] = dot(step, ex[...])
+    left[...] = dot(remaining, ex[...])
+    for rows_t, lanes in tiles_of(0, PAIRS):
+        total, _ = conv_tile(wide, kw, rows_t, lanes)
+        x = total * sigmoid(total)
+        x_o[rows_t, lanes] = x.astype(bf16)
+        u = (x * stepped[rows_t, lanes]).astype(bf16)
+        u_o[rows_t, lanes] = u
+        weighted[rows_t, lanes] = (u.astype(f32) * left[rows_t, lanes]).astype(bf16)
     whole = spread(whole, ex, slice(0, MINE))[:1]
     state[...] = whole * state[...] + dot_tn(bc_o[:, :STATE], weighted[...])
     passed[...] = passed[...] * whole
@@ -260,7 +288,7 @@
 def within_kernel(u, bc, cum, cumt, y_o):
     rows = lax.broadcasted_iota(jnp.int32, (BLOCK, BLOCK), 0)
     columns = lax.broadcasted_iota(jnp.int32, (BLOCK, BLOCK), 1)
-    products = jnp.where(rows >= columns, dot_nt(bc[:, STATE:], bc[:, :STATE]), 0.0)
+    products = jnp.where(token_of(rows) >= token_of(columns), dot_nt(bc[:, STATE:], bc[:, :STATE]), 0.0)
     lane = lax.broadcasted_iota(jnp.int32, (BLOCK, LANES), 1)
     for pair in range(PAIRS):
         values = u[:, pair * LANES : (pair + 1) * LANES]
@@ -273,11 +301,9 @@
 
 
 def gate_kernel(normed, cot_mine, cot_other, wg, wo, y, x, bc, cum, entry, factor, incoming, skip,
-                gain, ex, mix_o, z_o, ds_o, state_o, sums_o):
+                gain, ex, mix_o, z_o, ds_o, state_o, sums_o, squares, crossed):
     cot = jnp.where(pl.program_id(0) == 0, cot_mine[...], cot_other[...])
     grown = halves_of(jnp.exp(cum[...]))
-    squares = jnp.zeros((BLOCK, LANES), f32)
-    crossed = jnp.zeros((BLOCK, LANES), f32)
     for chunk in range(PAIRS // 2):
         many = strip_of(chunk, 2 * LANES)
         z_all = dot(normed[...], wg[:, many]).astype(bf16)
@@ -290,22 +316,28 @@
         mix_all = spread(grown, ex, many) * dot(bc[:, STATE:], entering)
         for half in range(2):
             part, lanes = strip_of(half), strip_of(2 * chunk + half)
-            carried = mix_all[:, part] + y[:, lanes].astype(f32)
-            mix_o[:, lanes] = carried.astype(bf16)
-            mix = carried + skip[:, lanes] * x[:, lanes].astype(f32)
-            z = z_all[:, part].astype(f32)
-            g = mix * (z * jax.nn.sigmoid(z))
-            squares = squares + g * g
-            crossed = crossed + ds_all[:, part] * gain[:, lanes] * g
+            for begin in range(0, BLOCK, TILE):
+                tile = slice(begin, begin + TILE)
+                carried = mix_all[tile, part] + y[tile, lanes].astype(f32)
+                mix_o[tile, lanes] = carried.astype(bf16)
+                mix = carried + skip[:, lanes] * x[tile, lanes].astype(f32)
+                z = z_all[tile, part].astype(f32)
+                g = mix * (z * sigmoid(z))
+                other = ds_all[tile, part] * gain[:, lanes] * g
+                if chunk + half == 0:
+                    squares[tile, :], crossed[tile, :] = g * g, other
+                else:
+                    squares[tile, :] += g * g
+                    crossed[tile, :] += other
     ones = jnp.ones((8, 2 * LANES), bf16)
     which = lax.broadcasted_iota(jnp.int32, (8, BLOCK), 0)
-    squares, crossed = dot_nt(ones, halves_of(squares)), dot_nt(ones, halves_of(crossed))
-    sums_o[...] = jnp.where(which < 4, squares, crossed)
-
-
-def mixture_kernel(mix_r, z_r, ds_r, x, bc, cum, sums, got, skip, gain, ex, pairs,
+    sums = dot_nt(ones, halves_of(squares[...])), dot_nt(ones, halves_of(crossed[...]))
+    sums_o[...] = jnp.where(which < 4, *sums)
+
+
+def mixture_kernel(mix_r, z_r, ds_r, x, bc, cum, sums, got, skip, gain, ex,
                    scaled_o, dy_o, dz_o, inner_o, exit_o, factor_o, send_o, gain_o, skip_o,
-                   state, passed, weighted):
+                   state, passed, weighted, pooled, grown, scales):
     j, i = pl.program_id(0), pl.program_id(1)
 
     @pl.when((j == 0) & (i == 0))
@@ -325,31 +357,30 @@
     summed = sum(dot_tn(part, turn) for part in split3(summed))
     scale = lax.rsqrt(summed[:, :LANES] / INNER + epsilon)
     back_scale = scale * scale * scale * (summed[:, LANES:] / INNER)
-    grown = halves_of(jnp.exp(cum[...]))
-    inner = jnp.zeros((BLOCK, LANES), f32)
-    for number in range(PAIRS):
-        lanes = strip_of(number)
-        carried = mix_r[:, lanes].astype(f32)
-        xs = x[:, lanes].astype(f32)
+    scales[0], scales[1] = scale, back_scale
+    grown[...] = dot(halves_of(jnp.exp(cum[...])), ex[...])
+    for rows_t, lanes in tiles_of(0, PAIRS):
+        carried = mix_r[rows_t, lanes].astype(f32)
+        xs = x[rows_t, lanes].astype(f32)
         mix = carried + skip[:, lanes] * xs
-        z = z_r[:, lanes].astype(f32)
-        ds = ds_r[:, lanes].astype(f32)
-        sig = jax.nn.sigmoid(z)
+        z = z_r[rows_t, lanes].astype(f32)
+        ds = ds_r[rows_t, lanes].astype(f32)
+        sig = sigmoid(z)
         silu = z * sig
         g = mix * silu
-        normalized = g * scale
-        scaled_o[:, lanes] = (normalized * gain[:, lanes]).astype(bf16)
+        normalized = g * scales[0, rows_t, :]
+        scaled_o[rows_t, lanes] = (normalized * gain[:, lanes]).astype(bf16)
         gain_o[:, lanes] += jnp.sum(ds * normalized, axis=0, keepdims=True)
-        dg = ds * (scale * gain[:, lanes]) - g * back_scale
+        dg = ds * (scales[0, rows_t, :] * gain[:, lanes]) - g * scales[1, rows_t, :]
         dmix = dg * silu
-        dz_o[:, lanes] = (dg * mix * (sig * (1.0 + z * (1.0 - sig)))).astype(bf16)
+        dz_o[rows_t, lanes] = (dg * mix * (sig * (1.0 + z * (1.0 - sig)))).astype(bf16)
         skip_o[:, lanes] += jnp.sum(dmix * xs, axis=0, keepdims=True)
         dy = dmix.astype(bf16)
-        dy_o[:, lanes] = dy
+        dy_o[rows_t, lanes] = dy
         dyf = dy.astype(f32)
-        inner = inner + pool(dyf * carried, pairs, number)
-        weighted[:, lanes] = (dyf * spread(grown, ex, lanes)).astype(bf16)
-    inner_o[...] = inner
+        pooled[rows_t, lanes] = (dyf * carried).astype(bf16)
+        weighted[rows_t, lanes] = (dyf * grown[rows_t, lanes]).astype(bf16)
+    inner_o[...] = pool(pooled[...], ex)
     last = cum[BLOCK - 1 : BLOCK, :]
     whole = halves_of(jnp.broadcast_to(jnp.exp(last), (16, LANES)))
     whole = spread(whole, ex, slice(0, MINE))[:1]
@@ -363,7 +394,7 @@
 def within_back(u, dy, bc, cum, cumt, du_o, dbc_o):
     rows = lax.broadcasted_iota(jnp.int32, (BLOCK, BLOCK), 0)
     columns = lax.broadcasted_iota(jnp.int32, (BLOCK, BLOCK), 1)
-    causal = columns >= rows
+    causal = token_of(columns) >= token_of(rows)
     products = jnp.where(causal, dot_nt(bc[:, :STATE], bc[:, STATE:]), 0.0)
     lane = lax.broadcasted_iota(jnp.int32, (BLOCK, LANES), 1)
     total = jnp.zeros((BLOCK, BLOCK), f32)
@@ -384,12 +415,11 @@
     dbc_o[:, STATE:] = dot_tn(total, bc[:, :STATE])
 
 
-def features_back_kernel(px, kw, heads, pick, tri, ex, pairs, u, dy, du_r, dbc, inner, cum,
+def features_back_kernel(px, kw, heads, pick, tri, ex, u, dy, du_r, dbc, inner, cum,
                          entering, exit_r, factor, incoming, skip,
-                         gp_o, rim_o, tail_o, kw_o, heads_o, after, wide, dpre, raw, held_u,
-                         grown_dy):
+                         gp_o, rim_o, tail_o, kw_o, heads_o, after, wide, dpre, raw, wides,
+                         products):
     j, i = pl.program_id(0), pl.program_id(1)
-    block = pl.num_programs(1) - 1 - i
 
     @pl.when((j == 0) & (i == 0))
     def _():
@@ -400,9 +430,8 @@
     def _():
         after[...] = jnp.zeros_like(after)
 
-    rows = conv_rows(px.at[0], block)
-    wide[...] = rows[:, :CONVD].astype(f32)
-    dpre[BLOCK:, :] = after[...]
+    rows = px[0]
+    widen(rows, wide)
     biased, step, log_decay, rate = steps_of(rows[HALO:, CONVD:], heads, pick)
     c = cum[...]
     last = c[BLOCK - 1 : BLOCK, :]
@@ -410,62 +439,72 @@
     leaving16 = leaving.astype(bf16)
     crossing = jnp.sum(leaving * entering[0].astype(f32), axis=0, keepdims=True)
     crossing = jnp.broadcast_to(crossing, (16, MINE))
-    crossing = sum(pool(crossing[:, strip_of(n)], pairs, n) for n in range(PAIRS))
-    crossing = crossing[:1] * jnp.exp(last)
-    remaining, grown, steps = (halves_of(v) for v in (jnp.exp(last - c), jnp.exp(c), step))
-    total, _ = conv_strip(wide, kw, strip_of(PAIRS))
-    raw[...] = dot((total * jax.nn.sigmoid(total)).astype(bf16), leaving16)
-
-    def finish(dact, total, sig, taps, lanes):
+    crossing = sum(pool(part, ex) for part in split(crossing))[:1] * jnp.exp(last)
+    for k, value in enumerate((jnp.exp(last - c), jnp.exp(c), step)):
+        wides[k] = dot(halves_of(value), ex[...])
+    for rows_t, lanes in tiles_of(PAIRS, PAIRS + 1):
+        total, _ = conv_tile(wide, kw, rows_t, lanes)
+        products[0, rows_t, :LANES] = (total * sigmoid(total)).astype(bf16)
+    raw[...] = dot(products[0, :, :LANES], leaving16)
+
+    def finish(dact, total, sig, taps, rows_t, lanes):
         value = dact * (sig * (1.0 + total * (1.0 - sig)))
         kw_o[CONV : CONV + 1, lanes] += jnp.sum(value, axis=0, keepdims=True)
         for k in range(CONV):
             kw_o[k : k + 1, lanes] += jnp.sum(value * taps[k], axis=0, keepdims=True)
-        dpre[:BLOCK, lanes] = value
+        dpre[rows_t, lanes] = value
+
+    for rows_t, lanes in tiles_of(0, PAIRS):
+        total, taps = conv_tile(wide, kw, rows_t, lanes)
+        sig = sigmoid(total)
+        uf = u[rows_t, lanes].astype(f32)
+        dyf = dy[rows_t, lanes].astype(f32)
+        left = wides[0, rows_t, lanes]
+        du_state = left * raw[rows_t, lanes]
+        du_in = du_r[rows_t, lanes].astype(f32)
+        products[0, rows_t, lanes] = (uf * left).astype(bf16)
+        products[1, rows_t, lanes] = (dyf * wides[1, rows_t, lanes]).astype(bf16)
+        products[2, rows_t, lanes] = (uf * du_state).astype(bf16)
+        products[3, rows_t, lanes] = (uf * du_in).astype(bf16)
+        du = du_in + du_state
+        products[4, rows_t, lanes] = (du * (total * sig)).astype(bf16)
+        dx = du * wides[2, rows_t, lanes] + skip[:, lanes] * dyf
+        finish(dx, total, sig, taps, rows_t, lanes)
+    held, flow = pool(products[2], ex), inner[...] - pool(products[3], ex)
+    dstep = pool(products[4], ex)
+    raw[:, :STATE] = dbc[:, :STATE] + dot_nt(products[0], leaving16)
+    raw[:, STATE : 2 * STATE] = dbc[:, STATE:] + dot_nt(products[1], entering[0])
+    for rows_t, lanes in tiles_of(PAIRS, PAIRS + 2):
+        total, taps = conv_tile(wide, kw, rows_t, lanes)
+        dact = raw[rows_t, lanes.start - MINE : lanes.stop - MINE]
+        finish(dact, total, sigmoid(total), taps, rows_t, lanes)
+    for k in range(CONV - 1):
+        begin = 8 * k + 1
+        behind = jnp.concatenate([dpre[begin : begin + 7, :], after[k : k + 1, :]], axis=0)
+        dpre[BLOCK + 8 * k : BLOCK + 8 * k + 8, :] = behind
+    for rows_t, lanes in tiles_of(0, PAIRS + 2):
+        begin = rows_t.start + 8 * (CONV - 1)
         din = sum(
-            kw[k : k + 1, lanes] * dpre[CONV - 1 - k : CONV - 1 - k + BLOCK, lanes]
+            kw[k : k + 1, lanes] * dpre[begin - 8 * k : begin - 8 * k + TILE, lanes]
             for k in range(CONV)
         )
-        gp_o[0, :, lanes] = din.astype(bf16)
-
-        @pl.when(i == 0)
-        def _():
-            tail_o[0, :, lanes] = din[BLOCK - 16 :]
-
-    held = jnp.zeros((BLOCK, LANES), f32)
-    flow = inner[...]
-    dstep = jnp.zeros((BLOCK, LANES), f32)
-    for number in range(PAIRS):
-        lanes = strip_of(number)
-        total, taps = conv_strip(wide, kw, lanes)
-        sig = jax.nn.sigmoid(total)
-        uf = u[:, lanes].astype(f32)
-        dyf = dy[:, lanes].astype(f32)
-        left = spread(remaining, ex, lanes)
-        du_state = left * raw[:, lanes]
-        du_in = du_r[:, lanes].astype(f32)
-        held_u[:, lanes] = (uf * left).astype(bf16)
-        grown_dy[:, lanes] = (dyf * spread(grown, ex, lanes)).astype(bf16)
-        held = held + pool(uf * du_state, pairs, number)
-        flow = flow - pool(uf * du_in, pairs, number)
-        du = du_in + du_state
-        dstep = dstep + pool(du * (total * sig), pairs, number)
-        dx = du * spread(steps, ex, lanes) + skip[:, lanes] * dyf
-        finish(dx, total, sig, taps, lanes)
-    db = dbc[:, :STATE] + dot_nt(held_u[...], leaving16)
-    dc = dbc[:, STATE:] + dot_nt(grown_dy[...], entering[0])
-    for number, value in enumerate((db, dc)):
-        lanes = strip_of(PAIRS + number)
-        total, taps = conv_strip(wide, kw, lanes)
-        finish(value, total, jax.nn.sigmoid(total), taps, lanes)
-    after[...] = dpre[:8, :]
+        gp_o[0, rows_t, lanes] = din.astype(bf16)
+        if rows_t.stop == BLOCK:
+
+            @pl.when(i == 0)
+            def _(din=din, lanes=lanes):
+                tail_o[0, :, lanes] = din[TILE - 32 :]
+
+    first = [dpre[8 * k : 8 * k + 1, :] for k in range(CONV - 1)]
+    first = jnp.concatenate(first + [jnp.zeros((8 - CONV + 1, CONVD), f32)], axis=0)
+    after[...] = first
     dlog = crossing + sum(dot_tn(tri[...], part) for part in split3(flow))
     dlog = dlog + sum(dot(tri[...], part) for part in split3(held)) - held
     draw = (dstep - dlog * rate) * jax.nn.sigmoid(biased)
     gp_o[0, :, CONVD:] = dot_nt(draw.astype(bf16), pick[...]).astype(bf16)
     heads_o[0:1, :] += jnp.sum(draw, axis=0, keepdims=True)
     heads_o[1:2, :] += jnp.sum(dlog * log_decay, axis=0, keepdims=True)
-    early = jnp.concatenate([jnp.zeros((8, CONVD), f32), dpre[:8, :]], axis=0)
+    early = jnp.concatenate([jnp.zeros((8, CONVD), f32), first], axis=0)
     rim_o[0] = sum(kw[k : k + 1, :] * early[CONV - 1 - k : CONV - 1 - k + 8] for k in range(CONV))
 
 
@@ -487,15 +526,15 @@
     out[...] = jnp.where(place[2] % 2 == 0, value[1], value[0])
 
 
-def both_pieces_kernel(place, value, got, out):
+def both_pieces_kernel(place, value, got, turn, out):
     side = place[2] % 2
     kept = jnp.where(side == 0, value[0], value[1])
-    out[0] = jnp.where(side == 0, kept, got[...])
-    out[1] = jnp.where(side == 0, got[...], kept)
-
-
-def copy_kernel(value, out):
-    out[...] = value[...]
+    piece = jnp.where(pl.program_id(0) == side, kept, got[...])
+    out[0] = dot(turn[...], piece).astype(bf16)
+
+
+def ends_kernel(value, out):
+    out[...] = last_tokens(value[...].astype(f32), HALO).astype(bf16)
 
 
 def shard_kernel(own, got, out_weight, front_o, late_o):
@@ -546,16 +585,18 @@
     out[...] = jnp.sum(parts[...], axis=0)
 
 
-def activations_kernel(place, tokens, keep, got, out):
+def activations_kernel(place, tokens, keep, got, turn, out):
     value = jnp.where(pl.program_id(0) == place[2] % 2, keep[...], got[...])
-    out[0] = (tokens[0].astype(f32) + value.astype(f32)).astype(bf16)
-
-
-def tokens_grad_kernel(place, tokens, cot, keep, got, norm, out):
+    value = dot_tn(turn[...], value)
+    out[0] = (tokens[0].astype(f32) + value).astype(bf16)
+
+
+def tokens_grad_kernel(place, tokens, cot, keep, got, norm, turn, out):
     value = jnp.where(pl.program_id(0) == place[2] % 2, keep[...], got[...])
+    value = dot_tn(turn[...], value)
     residual = tokens[0].astype(f32)
     inverse = inverse_rms(residual)
-    weighted = value.astype(f32) * norm[...]
+    weighted = value * norm[...]
     along = jnp.mean(weighted * residual, axis=-1, keepdims=True)
     out[0] = (
         cot[0].astype(f32) + inverse * weighted - residual * (inverse * inverse * inverse * along)
@@ -655,8 +696,12 @@
 
 def with_rim(gp, tail, rim, whole):
     whole[...] = gp[0]
-    late = tail[0] + jnp.concatenate([jnp.zeros((8, CONVD), f32), rim[0]], axis=0)
-    whole[whole.shape[0] - 16 :, :CONVD] = late.astype(bf16)
+    late = tail[0]
+    row = lax.broadcasted_iota(jnp.int32, late.shape, 0)
+    for k in range(CONV - 1):
+        here = row == 32 - AHEAD + 8 * k + 7
+        late = late + jnp.where(here, rim[0, 8 - CONV + 1 + k : 8 - CONV + 2 + k, :], 0.0)
+    whole[whole.shape[0] - 32 :, :CONVD] = late.astype(bf16)
 
 
 def front_grads_kernel(n_ctx, r_in, place, normed, gp, tail, rim, step_o, *refs):
@@ -763,7 +808,7 @@
     skip_o[...] = dot(heads.astype(bf16), ex[:LANES, :])[2:3]
 
 
-def pack_kernel(n_dp, place, norm_sum, kw_sum, gain_sum, heads_sum, skip_sum, step_sum, pick, pairs,
+def pack_kernel(n_dp, place, norm_sum, kw_sum, gain_sum, heads_sum, skip_sum, step_sum, pick, ex,
                 packed_o, full, gains):
     n_all = packed_o.shape[0]
     taps_n, gain_n, norm_n = XBC // n_all, INNER // n_all, norm_sum.shape[1] // n_all
@@ -776,7 +821,7 @@
             gains[:, begin : begin + run] = gain_sum[:, k * run : (k + 1) * run] * keep[which]
     full[:, INNER:] = kw_sum[:, MINE:]
     skips = jnp.broadcast_to(skip_sum[...], (16, MINE))
-    skips = sum(pool(skips[:, strip_of(n)], pairs, n) for n in range(PAIRS))[:8]
+    skips = sum(pool(part, ex) for part in split(skips))[:8]
     row = lax.broadcasted_iota(jnp.int32, (8, LANES), 0)
     heads = jnp.where(row == 2, skips, heads_sum[...])
     heads = sum(dot_nt(piece, pick[...]) for piece in split3(heads))
@@ -865,6 +910,9 @@
         run = call(kernel, (1,), specs, outs, made, scratch, cost, needs)
         return run(*([where] if placed else []), *arrays)
 
+    order = token_of(np.arange(BLOCK))
+    turn = (order[:, None] == np.arange(BLOCK)[None]).astype(ml_dtypes.bfloat16)
+    turn = jnp.asarray(turn)
     cuts = 2
     cut_s = pl.BlockSpec((piece // cuts, width), lambda i: (i, 0))
     both_cut_s = pl.BlockSpec((2, piece // cuts, width), lambda i: (0, i, 0))
@@ -876,9 +924,15 @@
 
     def enter_line(value, send, needs=(), cost=0):
         made, got = sds((2, piece, width), bf16), swap(send, "ctx", 1)
-        specs = [smem, both_cut_s, cut_s]
-        run = call(both_pieces_kernel, (cuts,), specs, both_cut_s, made, (), cost, needs)
-        return run(where, value, got).reshape(length, width)
+        specs = [smem] + all_of([value, got, turn])
+        out_s = pl.BlockSpec((1, piece, width), lambda i: (i, 0, 0))
+        run = call(both_pieces_kernel, (2,), specs, out_s, made, (), cost, needs)
+        return run(where, value, got, turn).reshape(length, width)
+
+    def ends_of(value):
+        end_s = pl.BlockSpec((BLOCK, width), lambda i: (length // BLOCK - 1, 0))
+        made = sds((HALO, width), bf16)
+        return call(ends_kernel, (1,), [end_s], all_of([made])[0], made)(value)
 
     def leave_cores(mine, other, needs=()):
         total = add(after(mine, *needs), swap(other, "dp", 1)).reshape(2, piece, width)
@@ -930,19 +984,17 @@
         first_got = swap(front_shard, "ctx", 2)
         inside = enter_line(tokens, tokens_send, needs=[front_shard], cost=8)
         other = swap(inside, "dp", 1)
-        end_s = pl.BlockSpec((HALO, width), lambda i: (length // HALO - 1, 0))
-        made = sds((HALO, width), bf16)
-        ends = call(copy_kernel, (1,), [end_s], all_of([made])[0], made)(inside)
+        ends = ends_of(inside)
         before = hop(ends, 2)
         near = pair(front_shard, first_got, needs=[ends])
         sides = sides_of(near)
         far = swap(near, "ctx", 1)
         late_shard = after(late_shard, near)
         late_got = swap(late_shard, "ctx", 2)
-        across = across_of(*across_parts(*sides, needs=[far, before]))
+        across = across_of(*across_parts(*sides))
         far = after(far, *across)
         far_sides = sides_of(far)
-        late_near = pair(late_shard, late_got, needs=[far], cost=8)
+        late_near = pair(late_shard, late_got, needs=[far, before], cost=8)
         far_across_send = across_parts(*far_sides, needs=[late_near])
         far_across = across_of(*far_across_send)
         late_far = swap(late_near, "ctx", 1)
@@ -957,7 +1009,7 @@
         front_pieces = [jnp.stack(halves, axis=1).reshape(width, FRONT)]
         inside = enter_line(tokens, tokens_send)
         other = swap(inside, "dp", 1)
-        before = hop(inside[length - HALO :], 2)
+        before = hop(ends_of(inside), 2)
         before_other = swap(before, "dp", 1)
         out_halves = output_weight.reshape(2, r_out // 2, width)
         late_shard = jnp.concatenate([shard[:, :, FRONT:], out_halves], axis=1)
@@ -969,10 +1021,8 @@
 
     ex = np.arange(LANES)[:, None] == (np.arange(MINE)[None] // HEAD)
     ex = ex.astype(ml_dtypes.bfloat16)
-    pairs = [ex[:, strip_of(n)] for n in range(PAIRS) for _ in range(2)]
-    pairs = jnp.asarray(np.concatenate(pairs, axis=1))
     ex = jnp.asarray(np.concatenate([ex, ex], axis=0))
-    tri = np.arange(BLOCK)[:, None] >= np.arange(BLOCK)[None]
+    tri = order[:, None] >= order[None]
     tri = jnp.asarray(tri.astype(ml_dtypes.bfloat16))
     heads_in = lanes(jnp.stack([step_bias, decay_log, skip_gain]).astype(f32), 8)
     w_front, kw, gain, norm_full, heads, skip, pick = once(
@@ -1015,25 +1065,25 @@
         fixed((LANES, LANES)),
         fixed((BLOCK, BLOCK)),
         fixed((2 * LANES, MINE)),
-        fixed((LANES, 2 * MINE)),
     ]
-    conv_args = (kw, heads, pick, tri, ex, pairs)
-    ext_front = per_seq((1, length + HALO, FRONT))
+    conv_args = (kw, heads, pick, tri, ex)
+    ext_front = (1, BLOCK + HALO, FRONT)
     front_s = fixed((width, FRONT))
     whole_s, halo_s = fixed((length, width)), fixed((HALO, width))
     normed, px, x, u, bc, cum, cumt, entry, entry_factor, state_total, state_decay = call(
         features_kernel,
         grid,
         [whole_s, whole_s, halo_s, halo_s, fixed((1, width)), front_s] + conv_specs,
-        [here((BLOCK, width)), ext_front, here(wide), here(wide), here(both), here(heads_s),
+        [here((BLOCK, width)), here(ext_front), here(wide), here(wide), here(both), here(heads_s),
          here((1, LANES, BLOCK)), here(state_s), here(row8), per_seq(state_s), per_seq(row8)],
-        [pltpu.HBM((rows, width), bf16), pltpu.HBM((seqs, length + HALO, FRONT), bf16),
+        [pltpu.HBM((rows, width), bf16), pltpu.HBM((steps_n, BLOCK + HALO, FRONT), bf16),
          pltpu.HBM((rows, MINE), bf16), pltpu.HBM((rows, MINE), bf16),
          pltpu.HBM((rows, 2 * STATE), bf16), pltpu.HBM((rows, LANES)  , f32),
          pltpu.HBM((steps_n, LANES, BLOCK), f32), pltpu.HBM((steps_n, STATE, MINE), bf16), sds((steps_n, 8, MINE)),
          sds((seqs, STATE, MINE), bf16), sds((seqs, 8, MINE))],
         [pltpu.VMEM((STATE, MINE), f32), pltpu.VMEM((1, MINE), f32),
-         pltpu.VMEM((BLOCK + HALO, CONVD), f32), pltpu.VMEM((BLOCK, MINE), bf16)],
+         pltpu.VMEM((BLOCK + AHEAD, CONVD), f32), pltpu.VMEM((BLOCK, MINE), bf16),
+         pltpu.VMEM((BLOCK, MINE), f32), pltpu.VMEM((BLOCK, MINE), f32)],
         cost=16,
         needs=[cot_send],
     )(main(inside), main(other), before, before_other, norm_full, main(w_front), *conv_args)
@@ -1080,6 +1130,7 @@
          pl.BlockSpec((8, BLOCK), lambda j, i: (0, j * blocks + i))],
         [pltpu.HBM((rows, MINE), bf16)] * 3
         + [pltpu.HBM((steps_n, STATE, MINE), bf16), sds((8, rows))],
+        [pltpu.VMEM((BLOCK, LANES), f32)] * 2,
         cost=16,
     )(normed, cot, cot_other, w_gate, w_out, y, x, bc, cum, entry, entry_factor, incoming, skip, gain, ex)
     sums_got = swap(sums, "dp", 1)
@@ -1091,16 +1142,17 @@
         + [here(both, True), here(heads_s, True)]
         + [pl.BlockSpec((8, BLOCK), lambda j, i: (0, j * blocks + blocks - 1 - i)),
            pl.BlockSpec((8, BLOCK), lambda j, i: (0, (1 - j) * blocks + blocks - 1 - i))]
-        + [fixed((1, MINE)), fixed((1, MINE)), fixed((2 * LANES, MINE)), fixed((LANES, 2 * MINE))],
+        + [fixed((1, MINE)), fixed((1, MINE)), fixed((2 * LANES, MINE))],
         [here(wide, True)] * 3
         + [here(heads_s, True), here(state_s, True), here(row8, True), per_seq(state_s),
            fixed((1, MINE)), fixed((1, MINE))],
         [sds((rows, MINE), bf16)] * 3
         + [sds((rows, LANES)), sds((steps_n, STATE, MINE), bf16), sds((steps_n, 8, MINE)),
            sds((seqs, STATE, MINE), bf16), sds((1, MINE)), sds((1, MINE))],
-        [pltpu.VMEM((STATE, MINE), f32), pltpu.VMEM((1, MINE), f32), pltpu.VMEM((BLOCK, MINE), bf16)],
+        [pltpu.VMEM((STATE, MINE), f32), pltpu.VMEM((1, MINE), f32), pltpu.VMEM((BLOCK, MINE), bf16),
+         pltpu.VMEM((BLOCK, MINE), bf16), pltpu.VMEM((BLOCK, MINE), f32), pltpu.VMEM((2, BLOCK, LANES), f32)],
         cost=12,
-    )(*map(main, (mix, gate_raw, ds, x, bc, cum)), sums, sums_got, skip, gain, ex, pairs)
+    )(*map(main, (mix, gate_raw, ds, x, bc, cum)), sums, sums_got, skip, gain, ex)
     grad_incoming = relay(grad_send, state_decay, -2)
 
     def parts_of(rows_n, columns):
@@ -1144,18 +1196,18 @@
     gp, rim, tail, kw_sum, heads_sum = call(
         features_back_kernel,
         grid,
-        [ext_front]
+        [here(ext_front, True)]
         + conv_specs
         + [here(wide, True), here(wide, True), here(wide, True), here(both, True),
            here(heads_s, True), here(heads_s, True), here(state_s, True), here(state_s, True),
            here(row8, True), per_seq(state_s), fixed((1, MINE))],
         [pl.BlockSpec((1, BLOCK, FRONT), lambda j, i: (j, blocks - 1 - i, 0)),
-         per_seq((1, 8, CONVD)), per_seq((1, 16, CONVD)), fixed((8, CONVD)), fixed((8, LANES))],
+         per_seq((1, 8, CONVD)), per_seq((1, 32, CONVD)), fixed((8, CONVD)), fixed((8, LANES))],
         [pltpu.HBM((seqs, length, FRONT), bf16), sds((seqs, 8, CONVD)),
-         sds((seqs, 16, CONVD)), sds((8, CONVD)), sds((8, LANES))],
-        [pltpu.VMEM((8, CONVD), f32), pltpu.VMEM((BLOCK + HALO, CONVD), f32),
-         pltpu.VMEM((BLOCK + 8, CONVD), f32), pltpu.VMEM((BLOCK, MINE), f32),
-         pltpu.VMEM((BLOCK, MINE), bf16), pltpu.VMEM((BLOCK, MINE), bf16)],
+         sds((seqs, 32, CONVD)), sds((8, CONVD)), sds((8, LANES))],
+        [pltpu.VMEM((8, CONVD), f32), pltpu.VMEM((BLOCK + AHEAD, CONVD), f32),
+         pltpu.VMEM((BLOCK + AHEAD, CONVD), f32), pltpu.VMEM((BLOCK, MINE), f32),
+         pltpu.VMEM((3, BLOCK, MINE), f32), pltpu.VMEM((5, BLOCK, MINE), bf16)],
         cost=24,
     )(px, *conv_args, u, dy, du, dbc, inner, cum, entering, leaving, leave_factor, grad_incoming, skip)
 
@@ -1167,7 +1219,7 @@
         late_last = sides_of_each(*late_second)
     seq_wide = pl.BlockSpec((length, MINE), lambda j: (j, 0))
     seq_gp = pl.BlockSpec((1, length, FRONT), lambda j: (j, 0, 0))
-    rims = [pl.BlockSpec((1, n, CONVD), lambda j: (j, 0, 0)) for n in (16, 8)]
+    rims = [pl.BlockSpec((1, n, CONVD), lambda j: (j, 0, 0)) for n in (32, 8)]
     back_mine, back_other, norm_sum = call(
         normed_grads_kernel,
         (seqs,),
@@ -1203,35 +1255,36 @@
         made = sds((seqs, piece, width), dtype)
         return call(kernel, (seqs,), specs, block_s, made, (), cost, needs)(where, *arrays, *more)
 
+    if fast:
+        late_keep, late_send = fold_of(late_near, late_got)
+        late_got = swap(late_send, "ctx", 2)
     packed = once(
         functools.partial(pack_kernel, n_dp),
-        [norm_sum, kw_sum, gain_sum, heads_sum, skip_sum, d_step, pick, pairs],
+        [norm_sum, kw_sum, gain_sum, heads_sum, skip_sum, d_step, pick, ex],
         sds((n_all, 16, LANES)),
         [pltpu.VMEM((8, XBC), f32), pltpu.VMEM((1, INNER), f32)],
         cost=8,
-        needs=[back_send],
+        needs=[back_send, late_send] if fast else (),
         placed=True,
     )
     packed_got = lax.all_to_all(packed, every, 0, 0)
     activations = finish(
-        activations_kernel, [tokens], [out_keep, out_got], bf16, [packed], 8
+        activations_kernel, [tokens], [out_keep, out_got, turn], bf16, [packed], 8
     )
     if fast:
         front_second = join_of(front_parts[3], front_parts[4], *front_first, needs=[activations])
         front_last = sides_of_each(*front_second)
-        late_keep, late_send = fold_of(late_near, late_got)
-        late_got = swap(late_send, "ctx", 2)
     tokens_grad = finish(
         tokens_grad_kernel,
         [tokens, cotangent],
-        [back_keep, back_got, norm_full],
+        [back_keep, back_got, norm_full, turn],
         f32,
-        [*front_second] if fast else (),
+        [*front_second, late_got] if fast else (),
         8,
     )
     if fast:
         front_near, front_far = own_of(
-            front_parts[0], *front_first, *front_last, needs=[tokens_grad]
+            front_parts[0], *front_first, *front_last, needs=[tokens_grad, packed_got]
         )
         front_keep, front_send = fold_of(front_near, swap(front_far, "ctx", 1))
         front_got = swap(front_send, "ctx", 2)

time: 319 us -> 288 us (0.903); the launches traced: 313 us -> 287 us
  waiting for transfers between devices: 79 us -> 60.5 us
  Pallas kernels: 134 us -> 119 us
  local copies, waits for them, and re-layouts: 22.7 us -> 28.2 us
    pallas_call x29, Pallas kernels: 134 us -> 119 us  [call(): return lambda *arrays: made(*arrays, *needs)]
    ppermute x4, waiting for transfers between devices: 9.35 us -> 1.05 us  [hop(): return lax.ppermute(value, 'ctx', pairs)]
    all_to_all x1, waiting for transfers between devices: 5.59 us -> 0.01 us  [on_device(): packed_got = lax.all_to_all(packed, every, 0, 0)]
    unnamed x158, local copies, waits for them, and re-layouts: 17.1 us -> 22.4 us
    ppermute x40, waiting for transfers between devices: 64 us -> 59.4 us  [swap(): return lax.ppermute(value, axis, [(i, i ^ mask) for i in range(count)])]
  transfers between devices with their start and end apart: 45 -> 45, of which waited for: 21 -> 19; matrix products, arithmetic and copies ran while one was open for 7% -> 7% of each run, Pallas kernels for 35% -> 33%
where the time goes in v1:
time: 288 us; the launch traced here: 287 us
  Pallas kernels  119 us (41%)
  starting transfers between devices  61.4 us (21%)
  waiting for transfers between devices  60.5 us (21%)
  local copies, waits for them, and re-layouts  28.2 us (10%)
  other arithmetic  16 us (6%)
    pallas_call x29, Pallas kernels, call(): return lambda *arrays: made(*arrays, *needs)  119 us
    ppermute x40, waiting for transfers between devices, swap(): return lax.ppermute(value, axis, [(i, i ^ mask) for i in range(count)])  59.4 us
    ppermute x40, starting transfers between devices, swap(): return lax.ppermute(value, axis, [(i, i ^ mask) for i in range(count)])  45.9 us
    unnamed x158, local copies, waits for them, and re-layouts  22.4 us
    ppermute x4, starting transfers between devices, hop(): return lax.ppermute(value, 'ctx', pairs)  12.4 us
    convert_element_type x8, other arithmetic, add(): return sum((value.astype(f32) for value in values)).astype(bf16)  10.7 us
  transfers between devices with their start and end apart: 45, of which 19 were waited for; matrix products, arithmetic and copies ran while one was open for 7% of the time, Pallas kernels for 33%

profile of v1, /device:TPU:0, one launch (start us, length us, event | category | flops | bytes accessed | tf_op | source)
XLA Modules:
  0.0 286.9 jit_solution(4510938154178445222)
XLA Ops:
  2.6 3.1 %collective-permute-start = (bf16[256,1024]{1,0:T(8,128)(2,1)S(1)}, bf16[256,1024]{1,0:T(8,128)(2,1)S(1)}, u32[]{:S(2)}, u32[]{:S(2)}) collective-permute-start(bf16[256,1024]{1,0:T(8,128)(2,1)S(1)} %shard_map.221.refs_3_), channel_id=1, source_target_pairs={{0,1},{1,0},{2,3},{3,2},{4,5},{5,4},{6,7},{7,6},{8,9},{9,8},{10,11... | collective-permute-start | bytes 1572872 | tf_op jit(solution)/shard_map/ppermute | solution.py:36
  13.6 7.9 %collective-permute-done.refs_2_ = bf16[256,1024]{1,0:T(8,128)(2,1)S(1)} collective-permute-done((bf16[256,1024]{1,0:T(8,128)(2,1)S(1)}, bf16[256,1024]{1,0:T(8,128)(2,1)S(1)}, u32[]{:S(2)}, u32[]{:S(2)}) %collective-permute-start) | collective-permute-done | bytes 524320 | tf_op jit(solution)/shard_map/ppermute | solution.py:36
  27.4 2.9 %collective-permute-start.13 = (bf16[2,64,1024]{2,1,0:T(8,128)(2,1)}, bf16[2,64,1024]{2,1,0:T(8,128)(2,1)S(1)}, u32[]{:S(2)}, u32[]{:S(2)}) collective-permute-start(bf16[2,64,1024]{2,1,0:T(8,128)(2,1)} %shard_map.229), channel_id=1, source_target_pairs={{0,2},{1,3},{2,0},{3,1},{4,6},{5,7},{6,4},{7,5},{8,10},{9,11},{10,... | collective-permute-start | bytes 786440 | tf_op jit(solution)/shard_map/ppermute | solution.py:36
  35.8 3.6 %collective-permute-start.3 = (bf16[16,1024]{1,0:T(8,128)(2,1)S(1)}, bf16[16,1024]{1,0:T(8,128)(2,1)S(1)}, u32[]{:S(2)}, u32[]{:S(2)}) collective-permute-start(bf16[16,1024]{1,0:T(8,128)(2,1)S(1)} %shard_map.225.refs_2_), channel_id=1, source_target_pairs={{0,2},{1,3},{4,6},{5,7},{8,10},{9,11},{12,14},{13,15},{16,18},{17,... | collective-permute-start | bytes 98312 | tf_op jit(solution)/shard_map/ppermute | solution.py:42
  48.2 5.6 %collective-permute-done.11.refs_0_.refs_9_ = bf16[2,2,32,1408]{3,2,1,0:T(8,128)(2,1)S(1)} collective-permute-done((bf16[2,2,32,1408]{3,2,1,0:T(8,128)(2,1)S(1)}, bf16[2,2,32,1408]{3,2,1,0:T(8,128)(2,1)S(1)}, u32[]{:S(2)}, u32[]{:S(2)}) %collective-permute-start.11) | collective-permute-done | bytes 360480 | tf_op jit(solution)/shard_map/ppermute | solution.py:36
  57.8 4.1 %collective-permute-done.14.refs_1_.refs_11_ = bf16[2,32,1408]{2,1,0:T(8,128)(2,1)S(1)} collective-permute-done((bf16[2,32,1408]{2,1,0:T(8,128)(2,1)S(1)}, bf16[2,32,1408]{2,1,0:T(8,128)(2,1)S(1)}, u32[]{:S(2)}, u32[]{:S(2)}) %collective-permute-start.14) | collective-permute-done | bytes 180256 | tf_op jit(solution)/shard_map/ppermute | solution.py:36
  66.9 3.7 %shard_map.234 = (bf16[1024,1408]{1,0:T(8,128)(2,1)}, f32[8,1280]{1,0:T(8,128)S(1)}, f32[1,1024]{1,0:T(1,128)S(1)}, f32[1,1024]{1,0:T(1,128)S(1)}, f32[8,128]{1,...) custom-call(s32[3]{0:T(128)S(1)} %pad_add_fusion.refs_0_, f32[8,128]{1,0:T(8,128)S(1)} %fusion.35.refs_1_, ...), custom_call_target="tpu_custom_call" | custom-call | flops 8000000000 | bytes 28000000 | tf_op jit(solution)/shard_map/pallas_call | solution.py:862
  73.3 15.1 %shard_map.236 = (bf16[1024,1024]{1,0:T(8,128)(2,1)}, bf16[4,272,1408]{2,1,0:T(8,128)(2,1)}, bf16[1024,1024]{1,0:T(8,128)(2,1)}, bf16[1024,1024]{1,0:T(8,128)(2,...) custom-call(bf16[512,1024]{1,0:T(8,128)(2,1)} %bitcast.136, ...), custom_call_target="tpu_custom_call" | custom-call | flops 16000000000 | bytes 56000000 | tf_op jit(solution)/shard_map/pallas_call | solution.py:862
  89.8 5.6 %collective-permute-start.23 = (bf16[2,128,1024]{2,1,0:T(8,128)(2,1)S(1)}, bf16[2,128,1024]{2,1,0:T(8,128)(2,1)S(1)}, u32[]{:S(2)}, u32[]{:S(2)}) collective-permute-start(bf16[2,128,1024]{2,1,0:T(8,128)(2,1)S(1)} %get-tuple-element.94.refs_4_), channel_id=1, source_target_pairs={{0,2},{1,3},{4,6},{5,7},{8,10},{9,11},{12,14},{13,15},{16,18},{17,... | collective-permute-start | bytes 1572872 | tf_op jit(solution)/shard_map/ppermute | solution.py:42
  97.7 5.0 %shard_map.239.refs_6_.refs_5_ = bf16[1024,1024]{1,0:T(8,128)(2,1)S(1)} custom-call(bf16[1024,1024]{1,0:T(8,128)(2,1)S(1)} %copy-done.52, bf16[1024,256]{1,0:T(8,128)(2,1)S(1)} %copy-done.61, f32[1024,128]{1,0:T(8,128)S(1)} %copy-done.59, f32[4,128,256]{2,1,0:T(8,128)S(1)} %copy-done.63, bf16[4,64,1024]{2,1,0:T(8,128)(2,1)S(1)} %get-tuple-element.95.refs_4_, ...), custom_call_target="tpu_custom_call" | custom-call | flops 8000000000 | bytes 28000000 | tf_op jit(solution)/shard_map/pallas_call | solution.py:862
  102.8 6.7 %collective-permute-done.21.refs_4_ = bf16[4,64,1024]{2,1,0:T(8,128)(2,1)S(1)} collective-permute-done((bf16[4,64,1024]{2,1,0:T(8,128)(2,1)S(1)}, bf16[4,64,1024]{2,1,0:T(8,128)(2,1)S(1)}, u32[]{:S(2)}, u32[]{:S(2)}) %collective-permute-start.21) | collective-permute-done | bytes 524320 | tf_op jit(solution)/shard_map/ppermute | solution.py:36
  113.6 9.2 %shard_map.241 = (bf16[1024,1024]{1,0:T(8,128)(2,1)}, bf16[1024,1024]{1,0:T(8,128)(2,1)}, bf16[1024,1024]{1,0:T(8,128)(2,1)}, bf16[4,128,1024]{2,1,0:T(8,128)(2,1)}, f32[8,1024]{1,0:T(8,128)S(1)}) custom-call(bf16[1024,1024]{1,0:T(8,128)(2,1)S(1)} %copy-done.55, bf16[512,1024]{1,0:T(8,128)(2,1)S(1)} %bitcast.132, ...), custom_call_target="tpu_custom_call" | custom-call | flops 16000000000 | bytes 56000000 | tf_op jit(solution)/shard_map/pallas_call | solution.py:862
  125.2 10.4 %shard_map.242 = (bf16[1024,1024]{1,0:T(8,128)(2,1)S(1)}, bf16[1024,1024]{1,0:T(8,128)(2,1)S(1)}, bf16[1024,1024]{1,0:T(8,128)(2,1)S(1)}, f32[1024,128]{1,0:T(8,...) custom-call(bf16[1024,1024]{1,0:T(8,128)(2,1)} %get-tuple-element.10, ...), custom_call_target="tpu_custom_call" | custom-call | flops 12000000000 | bytes 42000000 | tf_op jit(solution)/shard_map/pallas_call | solution.py:862
  137.2 21.7 %shard_map.243 = (bf16[512,1024]{1,0:T(8,128)(2,1)S(1)}, bf16[512,1024]{1,0:T(8,128)(2,1)}, bf16[1024,1024]{1,0:T(8,128)(2,1)S(1)}, f32[1024,256]{1,0:T(8,128)S(...) custom-call(s32[3]{0:T(128)S(1)} %pad_add_fusion.refs_0_, ...), custom_call_target="tpu_custom_call" | custom-call | flops 24000000000 | bytes 84000000 | tf_op jit(solution)/shard_map/pallas_call | solution.py:862
  163.6 17.5 %shard_map.244 = (bf16[2,512,1408]{2,1,0:T(8,128)(2,1)}, f32[2,8,1280]{2,1,0:T(8,128)S(1)}, f32[2,32,1280]{2,1,0:T(8,128)S(1)}, f32[8,1280]{1,0:T(8,128)S(1)}, f32[8,128]{1,0:T(8,128)S(1)}) custom-call(bf16[4,272,1408]{2,1,0:T(8,128)(2,1)S(1)} %copy-done.58, f32[8,1280]{1,0:T(8,128)S(1)} %get-tuple-element.90.refs_6_.refs_1_, ...), custom_call_target="tpu_custom_call" | custom-call | flops 24000000000 | bytes 84000000 | tf_op jit(solution)/shard_map/pallas_call | solution.py:862
  193.2 5.4 %collective-permute-start.27 = (bf16[256,1024]{1,0:T(8,128)(2,1)}, bf16[256,1024]{1,0:T(8,128)(2,1)}, u32[]{:S(2)}, u32[]{:S(2)}) collective-permute-start(bf16[256,1024]{1,0:T(8,128)(2,1)} %get-tuple-element.163.refs_10_), channel_id=1, source_target_pairs={{0,1},{1,0},{2,3},{3,2},{4,5},{5,4},{6,7},{7,6},{8,9},{9,8},{10,11... | collective-permute-start | bytes 1572872 | tf_op jit(solution)/shard_map/ppermute | solution.py:36
  198.6 11.7 %shard_map.247 = (bf16[512,1024]{1,0:T(8,128)(2,1)S(1)}, bf16[512,1024]{1,0:T(8,128)(2,1)}, f32[1,1024]{1,0:T(1,128)S(1)}) custom-call(bf16[512,1024]{1,0:T(8,128)(2,1)} %bitcast.137, bf16[512,1024]{1,0:T(8,128)(2,1)} %collective-permute-done.2.refs_1_, bf16[1024,1024]{1,0:T(8,128)(2,1)} %copy-done.54, bf16[1024,1024]{1,0:T(8,128)(2,1)} %copy-done.39, ...), custom_call_target="tpu_custom_call" | custom-call | flops 12000000000 | bytes 42000000 | tf_op jit(solution)/shard_map/pallas_call | solution.py:862
  214.8 7.7 %shard_map.249 = (f32[1024,128]{1,0:T(8,128)S(1)}, bf16[2,4,32,1280]{3,2,1,0:T(8,128)(2,1)S(1)}, bf16[2,4,32,1280]{3,2,1,0:T(8,128)(2,1)}, bf16[2,4,32,1280]{3,2...) custom-call(s32[3]{0:T(128)S(1)} %pad_add_fusion.refs_0_, ...), custom_call_target="tpu_custom_call" | custom-call | flops 10000000000 | bytes 35000000 | tf_op jit(solution)/shard_map/pallas_call | solution.py:862
  231.3 3.4 %collective-permute-start.38 = (bf16[2,64,1024]{2,1,0:T(8,128)(2,1)}, bf16[2,64,1024]{2,1,0:T(8,128)(2,1)}, u32[]{:S(2)}, u32[]{:S(2)}) collective-permute-start(bf16[2,64,1024]{2,1,0:T(8,128)(2,1)} %get-tuple-element.158.refs_10_), channel_id=1, source_target_pairs={{0,2},{1,3},{2,0},{3,1},{4,6},{5,7},{6,4},{7,5},{8,10},{9,11},{10,... | collective-permute-start | bytes 786440 | tf_op jit(solution)/shard_map/ppermute | solution.py:36
  239.5 3.1 %all-to-all-start = ((f32[32,16,128]{2,1,0:T(8,128)}), f32[32,16,128]{2,1,0:T(8,128)S(1)}, u32[]{:S(2)}, u32[]{:S(2)}) async-start(f32[32,16,128]{2,1,0:T(8,128)} %copy-done.33), calls=%async_computation | async-start | bytes 524288 | tf_op jit(solution)/shard_map/all_to_all | solution.py:1270
  253.3 6.7 %collective-permute-done.35.refs_4_ = bf16[256,1024]{1,0:T(8,128)(2,1)} collective-permute-done((bf16[256,1024]{1,0:T(8,128)(2,1)}, bf16[256,1024]{1,0:T(8,128)(2,1)}, u32[]{:S(2)}, u32[]{:S(2)}) %collective-permute-start.35) | collective-permute-done | bytes 524320 | tf_op jit(solution)/shard_map/ppermute | solution.py:36
  260.9 3.1 %shard_map.254.refs_1_ = f32[2,256,1024]{2,1,0:T(8,128)} custom-call(s32[3]{0:T(128)S(1)} %pad_add_fusion.refs_0_, bf16[2,256,1024]{2,1,0:T(8,128)(2,1)S(1)} %copy-done.20, bf16[2,256,1024]{2,1,0:T(8,128)(2,1)S(1)} %copy-done.8, bf16[256,1024]{1,0:T(8,128)(2,1)S(1)} %copy-done.24, bf16[256,1024]{1,0:T(8,128)(2,1)} %collective-permute-done.35.refs_4_, ...), custom_call_target="tpu_custom_call" | custom-call | flops 8000000000 | bytes 28000000 | tf_op jit(solution)/shard_map/pallas_call | solution.py:862
  266.8 7.8 %collective-permute-done.41 = bf16[2,2,32,1280]{3,2,0,1:T(8,128)(2,1)S(1)} collective-permute-done((bf16[2,2,32,1280]{3,2,0,1:T(8,128)(2,1)S(1)}, bf16[2,2,32,1280]{3,2,0,1:T(8,128)(2,1)S(1)}, u32[]{:S(2)}, u32[]{:S(2)}) %collective-permute-start.41) | collective-permute-done | bytes 327712 | tf_op jit(solution)/shard_map/ppermute | solution.py:36
  277.1 5.4 %collective-permute-done.42.refs_1_ = bf16[2,32,1280]{2,1,0:T(8,128)(2,1)S(1)} collective-permute-done((bf16[2,32,1280]{2,1,0:T(8,128)(2,1)S(1)}, bf16[2,32,1280]{2,1,0:T(8,128)(2,1)S(1)}, u32[]{:S(2)}, u32[]{:S(2)}) %collective-permute-start.42) | collective-permute-done | bytes 163872 | tf_op jit(solution)/shard_map/ppermute | solution.py:36
  (287 shorter events, 109.1 us)
Async XLA Ops:
  2.6 18.9 %collective-permute-start = (bf16[256,1024]{1,0:T(8,128)(2,1)S(1)}, bf16[256,1024]{1,0:T(8,128)(2,1)S(1)}, u32[]{:S(2)}, u32[]{:S(2)}) collective-permute-start(bf16[256,1024]{1,0:T(8,128)(2,1)S(1)} %shard_map.221.refs_3_), channel_id=1, source_target_pairs={{0,1},{1,0},{2,3},{3,2},{4,5},{5,4},{6,7},{7,6},{8,9},{9,8},{10,11... | collective-permute-start | bytes 1572872 | tf_op jit(solution)/shard_map/ppermute | solution.py:36
  47.6 25.7 %collective-permute-start.2 = (bf16[512,1024]{1,0:T(8,128)(2,1)S(1)}, bf16[512,1024]{1,0:T(8,128)(2,1)}, u32[]{:S(2)}, u32[]{:S(2)}) collective-permute-start(bf16[512,1024]{1,0:T(8,128)(2,1)S(1)} %bitcast.135), channel_id=1, source_target_pairs={{0,4},{4,0},{8,12},{12,8},{16,20},{20,16},{24,28},{28,24},{1,5},{5... | collective-permute-start | bytes 3145736 | tf_op jit(solution)/shard_map/ppermute | solution.py:36
  47.7 18.0 %collective-permute-start.4 = (bf16[16,1024]{1,0:T(8,128)(2,1)S(1)}, bf16[16,1024]{1,0:T(8,128)(2,1)S(1)}, u32[]{:S(2)}, u32[]{:S(2)}) collective-permute-start(bf16[16,1024]{1,0:T(8,128)(2,1)S(1)} %collective-permute-done.3.refs_3_.refs_2_), channel_id=1, source_target_pairs={{0,4},{4,0},{8,12},{12,8},{16,20},{20,16},{24,28},{28,24},{1,5},{5... | collective-permute-start | bytes 98312 | tf_op jit(solution)/shard_map/ppermute | solution.py:36
  63.7 31.7 %collective-permute-start.19 = (bf16[2,4,64,1024]{3,2,1,0:T(8,128)(2,1)}, bf16[2,4,64,1024]{3,2,1,0:T(8,128)(2,1)S(1)}, u32[]{:S(2)}, u32[]{:S(2)}) collective-permute-start(bf16[2,4,64,1024]{3,2,1,0:T(8,128)(2,1)} %shard_map.233.refs_13_.refs_1_), channel_id=1, source_target_pairs={{0,8},{4,12},{8,0},{12,4},{16,24},{20,28},{24,16},{28,20},{1,9},{5... | collective-permute-start | bytes 3145736 | tf_op jit(solution)/shard_map/ppermute | solution.py:36
  63.8 31.6 %collective-permute-start.20 = (bf16[2,4,64,1024]{3,2,1,0:T(8,128)(2,1)}, bf16[2,4,64,1024]{3,2,1,0:T(8,128)(2,1)S(1)}, u32[]{:S(2)}, u32[]{:S(2)}) collective-permute-start(bf16[2,4,64,1024]{3,2,1,0:T(8,128)(2,1)} %shard_map.233.refs_13_.refs_1_), channel_id=1, source_target_pairs={{0,16},{4,20},{8,24},{12,28},{16,0},{20,4},{24,8},{28,12},{1,17},{... | collective-permute-start | bytes 3145736 | tf_op jit(solution)/shard_map/ppermute | solution.py:36
  73.1 15.3 %collective-permute-start.17 = (bf16[256,1024]{1,0:T(8,128)(2,1)S(1)}, bf16[256,1024]{1,0:T(8,128)(2,1)S(1)}, u32[]{:S(2)}, u32[]{:S(2)}) collective-permute-start(bf16[256,1024]{1,0:T(8,128)(2,1)S(1)} %shard_map.235.refs_11_), channel_id=1, source_target_pairs={{0,1},{1,0},{2,3},{3,2},{4,5},{5,4},{6,7},{7,6},{8,9},{9,8},{10,11... | collective-permute-start | bytes 1572872 | tf_op jit(solution)/shard_map/ppermute | solution.py:36
  89.7 23.8 %collective-permute-start.18 = (bf16[512,1024]{1,0:T(8,128)(2,1)S(1)}, bf16[512,1024]{1,0:T(8,128)(2,1)S(1)}, u32[]{:S(2)}, u32[]{:S(2)}) collective-permute-start(bf16[512,1024]{1,0:T(8,128)(2,1)S(1)} %bitcast.130), channel_id=1, source_target_pairs={{0,4},{4,0},{8,12},{12,8},{16,20},{20,16},{24,28},{28,24},{1,5},{5... | collective-permute-start | bytes 3145736 | tf_op jit(solution)/shard_map/ppermute | solution.py:36
  89.8 23.7 %collective-permute-start.23 = (bf16[2,128,1024]{2,1,0:T(8,128)(2,1)S(1)}, bf16[2,128,1024]{2,1,0:T(8,128)(2,1)S(1)}, u32[]{:S(2)}, u32[]{:S(2)}) collective-permute-start(bf16[2,128,1024]{2,1,0:T(8,128)(2,1)S(1)} %get-tuple-element.94.refs_4_), channel_id=1, source_target_pairs={{0,2},{1,3},{4,6},{5,7},{8,10},{9,11},{12,14},{13,15},{16,18},{17,... | collective-permute-start | bytes 1572872 | tf_op jit(solution)/shard_map/ppermute | solution.py:42
  135.5 28.0 %collective-permute-start.25 = (bf16[2,128,1024]{2,1,0:T(8,128)(2,1)S(1)}, bf16[2,128,1024]{2,1,0:T(8,128)(2,1)S(1)}, u32[]{:S(2)}, u32[]{:S(2)}) collective-permute-start(bf16[2,128,1024]{2,1,0:T(8,128)(2,1)S(1)} %get-tuple-element.123), channel_id=1, source_target_pairs={{2,0},{3,1},{6,4},{7,5},{10,8},{11,9},{14,12},{15,13},{18,16},{19,... | collective-permute-start | bytes 1572872 | tf_op jit(solution)/shard_map/ppermute | solution.py:42
  160.0 25.5 %collective-permute-start.30 = (bf16[2,4,64,1024]{3,2,1,0:T(8,128)(2,1)}, bf16[2,4,64,1024]{3,2,1,0:T(8,128)(2,1)}, u32[]{:S(2)}, u32[]{:S(2)}) collective-permute-start(bf16[2,4,64,1024]{3,2,1,0:T(8,128)(2,1)} %get-tuple-element.131), channel_id=1, source_target_pairs={{0,8},{4,12},{8,0},{12,4},{16,24},{20,28},{24,16},{28,20},{1,9},{5... | collective-permute-start | bytes 3145736 | tf_op jit(solution)/shard_map/ppermute | solution.py:36
  161.6 26.2 %collective-permute-start.29 = (bf16[2,4,64,1024]{3,2,1,0:T(8,128)(2,1)}, bf16[2,4,64,1024]{3,2,1,0:T(8,128)(2,1)}, u32[]{:S(2)}, u32[]{:S(2)}) collective-permute-start(bf16[2,4,64,1024]{3,2,1,0:T(8,128)(2,1)} %get-tuple-element.129), channel_id=1, source_target_pairs={{0,16},{4,20},{8,24},{12,28},{16,0},{20,4},{24,8},{28,12},{1,17},{... | collective-permute-start | bytes 3145736 | tf_op jit(solution)/shard_map/ppermute | solution.py:36
  162.5 28.2 %collective-permute-start.26 = (bf16[512,1024]{1,0:T(8,128)(2,1)}, bf16[512,1024]{1,0:T(8,128)(2,1)}, u32[]{:S(2)}, u32[]{:S(2)}) collective-permute-start(bf16[512,1024]{1,0:T(8,128)(2,1)} %get-tuple-element.125), channel_id=1, source_target_pairs={{0,4},{4,0},{8,12},{12,8},{16,20},{20,16},{24,28},{28,24},{1,5},{5... | collective-permute-start | bytes 3145736 | tf_op jit(solution)/shard_map/ppermute | solution.py:36
  182.5 16.2 %collective-permute-start.28 = (f32[2,8,1280]{2,1,0:T(8,128)S(1)}, f32[2,8,1280]{2,1,0:T(8,128)S(1)}, u32[]{:S(2)}, u32[]{:S(2)}) collective-permute-start(f32[2,8,1280]{2,1,0:T(8,128)S(1)} %get-tuple-element.127), channel_id=1, source_target_pairs={{2,0},{3,1},{6,4},{7,5},{10,8},{11,9},{14,12},{15,13},{18,16},{19,... | collective-permute-start | bytes 245768 | tf_op jit(solution)/shard_map/ppermute | solution.py:42
  186.8 24.5 %collective-permute-start.32 = (bf16[4,64,1024]{2,1,0:T(8,128)(2,1)S(1)}, bf16[4,64,1024]{2,1,0:T(8,128)(2,1)}, u32[]{:S(2)}, u32[]{:S(2)}) collective-permute-start(bf16[4,64,1024]{2,1,0:T(8,128)(2,1)S(1)} %fusion.refs_9_), channel_id=1, source_target_pairs={{0,16},{4,20},{8,24},{12,28},{16,0},{20,4},{24,8},{28,12},{1,17},{... | collective-permute-start | bytes 1572872 | tf_op jit(solution)/shard_map/ppermute | solution.py:36
  189.0 22.3 %collective-permute-start.31 = (bf16[4,64,1024]{2,1,0:T(8,128)(2,1)S(1)}, bf16[4,64,1024]{2,1,0:T(8,128)(2,1)}, u32[]{:S(2)}, u32[]{:S(2)}) collective-permute-start(bf16[4,64,1024]{2,1,0:T(8,128)(2,1)S(1)} %fusion.1.refs_8_), channel_id=1, source_target_pairs={{0,8},{4,12},{8,0},{12,4},{16,24},{20,28},{24,16},{28,20},{1,9},{5... | collective-permute-start | bytes 1572872 | tf_op jit(solution)/shard_map/ppermute | solution.py:36
  193.2 49.4 %collective-permute-start.27 = (bf16[256,1024]{1,0:T(8,128)(2,1)}, bf16[256,1024]{1,0:T(8,128)(2,1)}, u32[]{:S(2)}, u32[]{:S(2)}) collective-permute-start(bf16[256,1024]{1,0:T(8,128)(2,1)} %get-tuple-element.163.refs_10_), channel_id=1, source_target_pairs={{0,1},{1,0},{2,3},{3,2},{4,5},{5,4},{6,7},{7,6},{8,9},{9,8},{10,11... | collective-permute-start | bytes 1572872 | tf_op jit(solution)/shard_map/ppermute | solution.py:36
  211.3 23.4 %collective-permute-start.33 = (bf16[512,1024]{1,0:T(8,128)(2,1)}, bf16[512,1024]{1,0:T(8,128)(2,1)}, u32[]{:S(2)}, u32[]{:S(2)}) collective-permute-start(bf16[512,1024]{1,0:T(8,128)(2,1)} %get-tuple-element.140), channel_id=1, source_target_pairs={{0,4},{4,0},{8,12},{12,8},{16,20},{20,16},{24,28},{28,24},{1,5},{5... | collective-permute-start | bytes 3145736 | tf_op jit(solution)/shard_map/ppermute | solution.py:36
  214.7 14.6 %collective-permute-start.34 = (bf16[2,2,64,1024]{3,2,0,1:T(8,128)(2,1)}, bf16[2,2,64,1024]{3,2,0,1:T(8,128)(2,1)}, u32[]{:S(2)}, u32[]{:S(2)}) collective-permute-start(bf16[2,2,64,1024]{3,2,0,1:T(8,128)(2,1)} %copy.35), channel_id=1, source_target_pairs={{0,1},{1,0},{2,3},{3,2},{4,5},{5,4},{6,7},{7,6},{8,9},{9,8},{10,11... | collective-permute-start | bytes 1572872 | tf_op jit(solution)/shard_map/ppermute | solution.py:36
  224.9 22.2 %collective-permute-start.37 = (bf16[2,4,32,1280]{3,2,1,0:T(8,128)(2,1)}, bf16[2,4,32,1280]{3,2,1,0:T(8,128)(2,1)}, u32[]{:S(2)}, u32[]{:S(2)}) collective-permute-start(bf16[2,4,32,1280]{3,2,1,0:T(8,128)(2,1)} %get-tuple-element.144), channel_id=1, source_target_pairs={{0,8},{4,12},{8,0},{12,4},{16,24},{20,28},{24,16},{28,20},{1,9},{5... | collective-permute-start | bytes 1966088 | tf_op jit(solution)/shard_map/ppermute | solution.py:36
  225.2 25.5 %collective-permute-start.36 = (bf16[2,4,32,1280]{3,2,1,0:T(8,128)(2,1)}, bf16[2,4,32,1280]{3,2,1,0:T(8,128)(2,1)}, u32[]{:S(2)}, u32[]{:S(2)}) collective-permute-start(bf16[2,4,32,1280]{3,2,1,0:T(8,128)(2,1)} %get-tuple-element.142), channel_id=1, source_target_pairs={{0,16},{4,20},{8,24},{12,28},{16,0},{20,4},{24,8},{28,12},{1,17},{... | collective-permute-start | bytes 1966088 | tf_op jit(solution)/shard_map/ppermute | solution.py:36
  231.3 22.1 %collective-permute-start.38 = (bf16[2,64,1024]{2,1,0:T(8,128)(2,1)}, bf16[2,64,1024]{2,1,0:T(8,128)(2,1)}, u32[]{:S(2)}, u32[]{:S(2)}) collective-permute-start(bf16[2,64,1024]{2,1,0:T(8,128)(2,1)} %get-tuple-element.158.refs_10_), channel_id=1, source_target_pairs={{0,2},{1,3},{2,0},{3,1},{4,6},{5,7},{6,4},{7,5},{8,10},{9,11},{10,... | collective-permute-start | bytes 786440 | tf_op jit(solution)/shard_map/ppermute | solution.py:36
  237.4 22.6 %collective-permute-start.35 = (bf16[256,1024]{1,0:T(8,128)(2,1)}, bf16[256,1024]{1,0:T(8,128)(2,1)}, u32[]{:S(2)}, u32[]{:S(2)}) collective-permute-start(bf16[256,1024]{1,0:T(8,128)(2,1)} %get-tuple-element.160.refs_9_), channel_id=1, source_target_pairs={{0,1},{1,0},{2,3},{3,2},{4,5},{5,4},{6,7},{7,6},{8,9},{9,8},{10,11... | collective-permute-start | bytes 1572872 | tf_op jit(solution)/shard_map/ppermute | solution.py:36
  239.5 24.5 %all-to-all-start = ((f32[32,16,128]{2,1,0:T(8,128)}), f32[32,16,128]{2,1,0:T(8,128)S(1)}, u32[]{:S(2)}, u32[]{:S(2)}) async-start(f32[32,16,128]{2,1,0:T(8,128)} %copy-done.33), calls=%async_computation | async-start | bytes 524288 | tf_op jit(solution)/shard_map/all_to_all | solution.py:1270
  248.9 15.9 %collective-permute-start.40 = (bf16[4,32,1280]{2,1,0:T(8,128)(2,1)}, bf16[4,32,1280]{2,1,0:T(8,128)(2,1)}, u32[]{:S(2)}, u32[]{:S(2)}) collective-permute-start(bf16[4,32,1280]{2,1,0:T(8,128)(2,1)} %fusion.2.refs_8_), channel_id=1, source_target_pairs={{0,16},{4,20},{8,24},{12,28},{16,0},{20,4},{24,8},{28,12},{1,17},{... | collective-permute-start | bytes 983048 | tf_op jit(solution)/shard_map/ppermute | solution.py:36
  (100 other events, 773.5 us)

commit v2 on v1

--- a/solution.py
+++ b/solution.py
@@ -134,6 +134,7 @@
         out_specs=pl.BlockSpec(memory_space=pl.ANY),
         out_shape=jax.ShapeDtypeStruct(value.shape, value.dtype),
         input_output_aliases={0: 0},
+        compiler_params=pltpu.CompilerParams(vmem_limit_bytes=1 << 20),
     )(value, *others)
 
 
@@ -1027,8 +1028,8 @@
     heads_in = lanes(jnp.stack([step_bias, decay_log, skip_gain]).astype(f32), 8)
     w_front, kw, gain, norm_full, heads, skip, pick = once(
         functools.partial(front_weights_kernel, n_dp, n_ctx, r_in),
-        [heads_in, ex, *map(main, front_pieces)],
-        [pltpu.HBM((width, FRONT), bf16), sds((8, CONVD)), sds((1, MINE)), sds((1, width)),
+        [heads_in, ex, *front_pieces],
+        [sds((width, FRONT), bf16), sds((8, CONVD)), sds((1, MINE)), sds((1, width)),
          sds((8, LANES)), sds((1, MINE)), sds((LANES, LANES), bf16)],
         [pltpu.VMEM((width, LANES), f32), pltpu.VMEM((8, XBC), f32), pltpu.VMEM((1, INNER), f32)],
         cost=8,
@@ -1086,7 +1087,7 @@
          pltpu.VMEM((BLOCK, MINE), f32), pltpu.VMEM((BLOCK, MINE), f32)],
         cost=16,
         needs=[cot_send],
-    )(main(inside), main(other), before, before_other, norm_full, main(w_front), *conv_args)
+    )(inside, other, before, before_other, norm_full, w_front, *conv_args)
 
     cot = enter_line(cotangent, cot_send, needs=[state_total])
     cot_other = swap(cot, "dp", 1)
@@ -1113,7 +1114,7 @@
         late_across = across_of(*late_across_send)
         w_gate, w_out = once(
             functools.partial(late_weights_kernel, n_ctx, r_in),
-            [*map(main, (late_own, *late_sides, *late_across))],
+            [late_own, *late_sides, *late_across],
             [sds((width, MINE), bf16), sds((MINE, width), bf16)],
             placed=True,
             needs=[y],
@@ -1203,7 +1204,7 @@
            here(row8, True), per_seq(state_s), fixed((1, MINE))],
         [pl.BlockSpec((1, BLOCK, FRONT), lambda j, i: (j, blocks - 1 - i, 0)),
          per_seq((1, 8, CONVD)), per_seq((1, 32, CONVD)), fixed((8, CONVD)), fixed((8, LANES))],
-        [pltpu.HBM((seqs, length, FRONT), bf16), sds((seqs, 8, CONVD)),
+        [sds((seqs, length, FRONT), bf16), sds((seqs, 8, CONVD)),
          sds((seqs, 32, CONVD)), sds((8, CONVD)), sds((8, LANES))],
         [pltpu.VMEM((8, CONVD), f32), pltpu.VMEM((BLOCK + AHEAD, CONVD), f32),
          pltpu.VMEM((BLOCK + AHEAD, CONVD), f32), pltpu.VMEM((BLOCK, MINE), f32),
@@ -1229,7 +1230,7 @@
         [pltpu.VMEM((length, FRONT), bf16)],
         cost=12,
         needs=[*late_second, out_send] if fast else (),
-    )(*map(main, (inside, other, dz, w_gate, gp)), tail, rim, main(w_front))
+    )(inside, other, dz, w_gate, gp, tail, rim, w_front)
     if fast:
         late_near, late_far = own_of(late_parts[0], *late_first, *late_last, needs=[back_mine])
         late_got = swap(late_far, "ctx", 1)
@@ -1243,7 +1244,7 @@
         [pltpu.VMEM((width, FRONT), f32), pltpu.VMEM((length, FRONT), bf16)],
         cost=10,
         needs=[late_far] if fast else (),
-    )(where, main(normed), main(gp), tail, rim)
+    )(where, normed, gp, tail, rim)
     if fast:
         front_first = swap(front_parts[1], "dp", 2), swap(front_parts[2], "dp", 4)
     back_keep, back_send = leave_cores(back_mine, back_other, needs=[d_step])

time: 288 us -> 263 us (0.913)
  Pallas kernels: 119 us -> 104 us
  local copies, waits for them, and re-layouts: 28.2 us -> 14.7 us
  starting transfers between devices: 61.4 us -> 71.5 us
  other arithmetic: 16 us -> 9.08 us
    pallas_call x29, Pallas kernels: 119 us -> 104 us  [call(): return lambda *arrays: made(*arrays, *needs)]
    unnamed x158 -> x98, local copies, waits for them, and re-layouts: 22.4 us -> 9.61 us
    ppermute x40, starting transfers between devices: 45.9 us -> 56.6 us  [swap(): return lax.ppermute(value, axis, [(i, i ^ mask) for i in range(count)])]
    convert_element_type x8, other arithmetic: 10.7 us -> 5.86 us  [add(): return sum((value.astype(f32) for value in values)).astype(bf16)]
  transfers between devices with their start and end apart: 45 -> 45, of which waited for: 19 -> 22; matrix products, arithmetic and copies ran while one was open for 7% -> 5% of each run, Pallas kernels for 33% -> 31%
where the time goes in v2:
time: 263 us
  Pallas kernels  104 us (40%)
  starting transfers between devices  71.5 us (27%)
  waiting for transfers between devices  61.7 us (23%)
  local copies, waits for them, and re-layouts  14.7 us (6%)
  other arithmetic  9.08 us (3%)
    pallas_call x29, Pallas kernels, call(): return lambda *arrays: made(*arrays, *needs)  104 us
    ppermute x40, waiting for transfers between devices, swap(): return lax.ppermute(value, axis, [(i, i ^ mask) for i in range(count)])  58.6 us
    ppermute x40, starting transfers between devices, swap(): return lax.ppermute(value, axis, [(i, i ^ mask) for i in range(count)])  56.6 us
    ppermute x4, starting transfers between devices, hop(): return lax.ppermute(value, 'ctx', pairs)  12.2 us
    unnamed x98, local copies, waits for them, and re-layouts  9.61 us
    convert_element_type x8, other arithmetic, add(): return sum((value.astype(f32) for value in values)).astype(bf16)  5.86 us
  transfers between devices with their start and end apart: 45, of which 22 were waited for; matrix products, arithmetic and copies ran while one was open for 5% of the time, Pallas kernels for 31%

profile of v2, /device:TPU:0, one launch (start us, length us, event | category | flops | bytes accessed | tf_op | source)
XLA Modules:
  0.0 262.5 jit_solution(11401657279445969192)
XLA Ops:
  2.6 3.1 %collective-permute-start = (bf16[256,1024]{1,0:T(8,128)(2,1)S(1)}, bf16[256,1024]{1,0:T(8,128)(2,1)S(1)}, u32[]{:S(2)}, u32[]{:S(2)}) collective-permute-start(bf16[256,1024]{1,0:T(8,128)(2,1)S(1)} %shard_map.221.refs_3_), channel_id=1, source_target_pairs={{0,1},{1,0},{2,3},{3,2},{4,5},{5,4},{6,7},{7,6},{8,9},{9,8},{10,11... | collective-permute-start | bytes 1572872 | tf_op jit(solution)/shard_map/ppermute | solution.py:36
  13.0 8.5 %collective-permute-done.refs_2_ = bf16[256,1024]{1,0:T(8,128)(2,1)S(1)} collective-permute-done((bf16[256,1024]{1,0:T(8,128)(2,1)S(1)}, bf16[256,1024]{1,0:T(8,128)(2,1)S(1)}, u32[]{:S(2)}, u32[]{:S(2)}) %collective-permute-start) | collective-permute-done | bytes 524320 | tf_op jit(solution)/shard_map/ppermute | solution.py:36
  27.4 2.9 %collective-permute-start.13 = (bf16[2,64,1024]{2,1,0:T(8,128)(2,1)S(1)}, bf16[2,64,1024]{2,1,0:T(8,128)(2,1)S(1)}, u32[]{:S(2)}, u32[]{:S(2)}) collective-permute-start(bf16[2,64,1024]{2,1,0:T(8,128)(2,1)S(1)} %shard_map.229), channel_id=1, source_target_pairs={{0,2},{1,3},{2,0},{3,1},{4,6},{5,7},{6,4},{7,5},{8,10},{9,11},{10,... | collective-permute-start | bytes 786440 | tf_op jit(solution)/shard_map/ppermute | solution.py:36
  35.8 3.6 %collective-permute-start.3 = (bf16[16,1024]{1,0:T(8,128)(2,1)S(1)}, bf16[16,1024]{1,0:T(8,128)(2,1)S(1)}, u32[]{:S(2)}, u32[]{:S(2)}) collective-permute-start(bf16[16,1024]{1,0:T(8,128)(2,1)S(1)} %shard_map.225.refs_2_), channel_id=1, source_target_pairs={{0,2},{1,3},{4,6},{5,7},{8,10},{9,11},{12,14},{13,15},{16,18},{17,... | collective-permute-start | bytes 98312 | tf_op jit(solution)/shard_map/ppermute | solution.py:42
  46.2 5.6 %collective-permute-done.11.refs_0_.refs_9_ = bf16[2,2,32,1408]{3,2,1,0:T(8,128)(2,1)S(1)} collective-permute-done((bf16[2,2,32,1408]{3,2,1,0:T(8,128)(2,1)S(1)}, bf16[2,2,32,1408]{3,2,1,0:T(8,128)(2,1)S(1)}, u32[]{:S(2)}, u32[]{:S(2)}) %collective-permute-start.11) | collective-permute-done | bytes 360480 | tf_op jit(solution)/shard_map/ppermute | solution.py:36
  54.8 6.0 %collective-permute-done.14.refs_1_.refs_11_ = bf16[2,32,1408]{2,1,0:T(8,128)(2,1)S(1)} collective-permute-done((bf16[2,32,1408]{2,1,0:T(8,128)(2,1)S(1)}, bf16[2,32,1408]{2,1,0:T(8,128)(2,1)S(1)}, u32[]{:S(2)}, u32[]{:S(2)}) %collective-permute-start.14) | collective-permute-done | bytes 180256 | tf_op jit(solution)/shard_map/ppermute | solution.py:36
  66.3 12.4 %shard_map.236 = (bf16[1024,1024]{1,0:T(8,128)(2,1)}, bf16[4,272,1408]{2,1,0:T(8,128)(2,1)}, bf16[1024,1024]{1,0:T(8,128)(2,1)}, bf16[1024,1024]{1,0:T(8,128)(2,...) custom-call(bf16[512,1024]{1,0:T(8,128)(2,1)S(1)} %bitcast.136, ...), custom_call_target="tpu_custom_call" | custom-call | flops 16000000000 | bytes 56000000 | tf_op jit(solution)/shard_map/pallas_call | solution.py:863
  80.1 5.6 %collective-permute-start.23 = (bf16[2,128,1024]{2,1,0:T(8,128)(2,1)S(1)}, bf16[2,128,1024]{2,1,0:T(8,128)(2,1)S(1)}, u32[]{:S(2)}, u32[]{:S(2)}) collective-permute-start(bf16[2,128,1024]{2,1,0:T(8,128)(2,1)S(1)} %get-tuple-element.94.refs_4_), channel_id=1, source_target_pairs={{0,2},{1,3},{4,6},{5,7},{8,10},{9,11},{12,14},{13,15},{16,18},{17,... | collective-permute-start | bytes 1572872 | tf_op jit(solution)/shard_map/ppermute | solution.py:42
  88.0 5.0 %shard_map.239.refs_6_.refs_5_ = bf16[1024,1024]{1,0:T(8,128)(2,1)S(1)} custom-call(bf16[1024,1024]{1,0:T(8,128)(2,1)S(1)} %copy-done.30, bf16[1024,256]{1,0:T(8,128)(2,1)S(1)} %copy-done.38, f32[1024,128]{1,0:T(8,128)S(1)} %copy-done.36, f32[4,128,256]{2,1,0:T(8,128)S(1)} %copy-done.40, bf16[4,64,1024]{2,1,0:T(8,128)(2,1)S(1)} %get-tuple-element.95.refs_4_, ...), custom_call_target="tpu_custom_call" | custom-call | flops 8000000000 | bytes 28000000 | tf_op jit(solution)/shard_map/pallas_call | solution.py:863
  93.0 6.7 %collective-permute-done.21.refs_4_ = bf16[4,64,1024]{2,1,0:T(8,128)(2,1)S(1)} collective-permute-done((bf16[4,64,1024]{2,1,0:T(8,128)(2,1)S(1)}, bf16[4,64,1024]{2,1,0:T(8,128)(2,1)S(1)}, u32[]{:S(2)}, u32[]{:S(2)}) %collective-permute-start.21) | collective-permute-done | bytes 524320 | tf_op jit(solution)/shard_map/ppermute | solution.py:36
  100.8 9.1 %shard_map.241 = (bf16[1024,1024]{1,0:T(8,128)(2,1)}, bf16[1024,1024]{1,0:T(8,128)(2,1)}, bf16[1024,1024]{1,0:T(8,128)(2,1)}, bf16[4,128,1024]{2,1,0:T(8,128)(2,1)}, f32[8,1024]{1,0:T(8,128)S(1)}) custom-call(bf16[1024,1024]{1,0:T(8,128)(2,1)S(1)} %copy-done.32, bf16[512,1024]{1,0:T(8,128)(2,1)S(1)} %bitcast.132, ...), custom_call_target="tpu_custom_call" | custom-call | flops 16000000000 | bytes 56000000 | tf_op jit(solution)/shard_map/pallas_call | solution.py:863
  112.2 10.4 %shard_map.242 = (bf16[1024,1024]{1,0:T(8,128)(2,1)S(1)}, bf16[1024,1024]{1,0:T(8,128)(2,1)S(1)}, bf16[1024,1024]{1,0:T(8,128)(2,1)S(1)}, f32[1024,128]{1,0:T(8,...) custom-call(bf16[1024,1024]{1,0:T(8,128)(2,1)} %get-tuple-element.10, ...), custom_call_target="tpu_custom_call" | custom-call | flops 12000000000 | bytes 42000000 | tf_op jit(solution)/shard_map/pallas_call | solution.py:863
  124.2 20.2 %shard_map.243 = (bf16[512,1024]{1,0:T(8,128)(2,1)S(1)}, bf16[512,1024]{1,0:T(8,128)(2,1)S(1)}, bf16[1024,1024]{1,0:T(8,128)(2,1)S(1)}, f32[1024,256]{1,0:T(8,12...) custom-call(s32[3]{0:T(128)S(1)} %pad_add_fusion.refs_0_, ...), custom_call_target="tpu_custom_call" | custom-call | flops 24000000000 | bytes 84000000 | tf_op jit(solution)/shard_map/pallas_call | solution.py:863
  147.7 2.9 %collective-permute-done.25.refs_15_ = bf16[2,128,1024]{2,1,0:T(8,128)(2,1)S(1)} collective-permute-done((bf16[2,128,1024]{2,1,0:T(8,128)(2,1)S(1)}, bf16[2,128,1024]{2,1,0:T(8,128)(2,1)S(1)}, u32[]{:S(2)}, u32[]{:S(2)}) %collective-permute-start.25) | collective-permute-done | bytes 524320 | tf_op jit(solution)/shard_map/ppermute | solution.py:42
  150.6 16.5 %shard_map.244 = (bf16[2,512,1408]{2,1,0:T(8,128)(2,1)S(1)}, f32[2,8,1280]{2,1,0:T(8,128)S(1)}, f32[2,32,1280]{2,1,0:T(8,128)S(1)}, f32[8,1280]{1,0:T(8,128)S(1)}, f32[8,128]{1,0:T(8,128)S(1)}) custom-call(bf16[4,272,1408]{2,1,0:T(8,128)(2,1)S(1)} %copy-done.35, f32[8,1280]{1,0:T(8,128)S(1)} %get-tuple-element.90.refs_6_.refs_1_, ...), custom_call_target="tpu_custom_call" | custom-call | flops 24000000000 | bytes 84000000 | tf_op jit(solution)/shard_map/pallas_call | solution.py:863
  175.0 7.6 %collective-permute-start.27 = (bf16[256,1024]{1,0:T(8,128)(2,1)}, bf16[256,1024]{1,0:T(8,128)(2,1)}, u32[]{:S(2)}, u32[]{:S(2)}) collective-permute-start(bf16[256,1024]{1,0:T(8,128)(2,1)} %get-tuple-element.163.refs_10_), channel_id=1, source_target_pairs={{0,1},{1,0},{2,3},{3,2},{4,5},{5,4},{6,7},{7,6},{8,9},{9,8},{10,11... | collective-permute-start | bytes 1572872 | tf_op jit(solution)/shard_map/ppermute | solution.py:36
  182.6 7.2 %shard_map.247 = (bf16[512,1024]{1,0:T(8,128)(2,1)S(1)}, bf16[512,1024]{1,0:T(8,128)(2,1)S(1)}, f32[1,1024]{1,0:T(1,128)S(1)}) custom-call(bf16[512,1024]{1,0:T(8,128)(2,1)S(1)} %bitcast.137, bf16[512,1024]{1,0:T(8,128)(2,1)S(1)} %copy-done.22, bf16[1024,1024]{1,0:T(8,128)(2,1)S(1)} %get-tuple-element.112.refs_2_, bf16[1024,1024]{1,0:T(8,128)(2,1)S(1)} %copy-done.18, ...), custom_call_target="tpu_custom_call" | custom-call | flops 12000000000 | bytes 42000000 | tf_op jit(solution)/shard_map/pallas_call | solution.py:863
  190.7 3.1 %collective-permute-start.34 = (bf16[2,2,64,1024]{3,2,0,1:T(8,128)(2,1)S(1)}, bf16[2,2,64,1024]{3,2,0,1:T(8,128)(2,1)S(1)}, u32[]{:S(2)}, u32[]{:S(2)}) collective-permute-start(bf16[2,2,64,1024]{3,2,0,1:T(8,128)(2,1)S(1)} %copy.35), channel_id=1, source_target_pairs={{0,1},{1,0},{2,3},{3,2},{4,5},{5,4},{6,7},{7,6},{8,9},{9,8},{10,11... | collective-permute-start | bytes 1572872 | tf_op jit(solution)/shard_map/ppermute | solution.py:36
  193.8 6.6 %shard_map.249 = (f32[1024,128]{1,0:T(8,128)S(1)}, bf16[2,4,32,1280]{3,2,1,0:T(8,128)(2,1)S(1)}, bf16[2,4,32,1280]{3,2,1,0:T(8,128)(2,1)}, bf16[2,4,32,1280]{3,2...) custom-call(s32[3]{0:T(128)S(1)} %pad_add_fusion.refs_0_, ...), custom_call_target="tpu_custom_call" | custom-call | flops 10000000000 | bytes 35000000 | tf_op jit(solution)/shard_map/pallas_call | solution.py:863
  206.1 3.4 %collective-permute-start.38 = (bf16[2,64,1024]{2,1,0:T(8,128)(2,1)}, bf16[2,64,1024]{2,1,0:T(8,128)(2,1)}, u32[]{:S(2)}, u32[]{:S(2)}) collective-permute-start(bf16[2,64,1024]{2,1,0:T(8,128)(2,1)} %get-tuple-element.158.refs_10_), channel_id=1, source_target_pairs={{0,2},{1,3},{2,0},{3,1},{4,6},{5,7},{6,4},{7,5},{8,10},{9,11},{10,... | collective-permute-start | bytes 786440 | tf_op jit(solution)/shard_map/ppermute | solution.py:36
  229.4 2.9 %collective-permute-done.35.refs_4_ = bf16[256,1024]{1,0:T(8,128)(2,1)} collective-permute-done((bf16[256,1024]{1,0:T(8,128)(2,1)}, bf16[256,1024]{1,0:T(8,128)(2,1)}, u32[]{:S(2)}, u32[]{:S(2)}) %collective-permute-start.35) | collective-permute-done | bytes 524320 | tf_op jit(solution)/shard_map/ppermute | solution.py:36
  232.3 3.1 %shard_map.254.refs_1_ = f32[2,256,1024]{2,1,0:T(8,128)} custom-call(s32[3]{0:T(128)S(1)} %pad_add_fusion.refs_0_, bf16[2,256,1024]{2,1,0:T(8,128)(2,1)S(1)} %copy-done.6, bf16[2,256,1024]{2,1,0:T(8,128)(2,1)S(1)} %copy-done, bf16[256,1024]{1,0:T(8,128)(2,1)S(1)} %copy-done.10, bf16[256,1024]{1,0:T(8,128)(2,1)} %collective-permute-done.35.refs_4_, ...), custom_call_target="tpu_custom_call" | custom-call | flops 8000000000 | bytes 28000000 | tf_op jit(solution)/shard_map/pallas_call | solution.py:863
  241.1 8.1 %collective-permute-done.41 = bf16[2,2,32,1280]{3,2,0,1:T(8,128)(2,1)S(1)} collective-permute-done((bf16[2,2,32,1280]{3,2,0,1:T(8,128)(2,1)S(1)}, bf16[2,2,32,1280]{3,2,0,1:T(8,128)(2,1)S(1)}, u32[]{:S(2)}, u32[]{:S(2)}) %collective-permute-start.41) | collective-permute-done | bytes 327712 | tf_op jit(solution)/shard_map/ppermute | solution.py:36
  252.6 5.4 %collective-permute-done.42.refs_1_ = bf16[2,32,1280]{2,1,0:T(8,128)(2,1)S(1)} collective-permute-done((bf16[2,32,1280]{2,1,0:T(8,128)(2,1)S(1)}, bf16[2,32,1280]{2,1,0:T(8,128)(2,1)S(1)}, u32[]{:S(2)}, u32[]{:S(2)}) %collective-permute-start.42) | collective-permute-done | bytes 163872 | tf_op jit(solution)/shard_map/ppermute | solution.py:36
  (227 shorter events, 95.3 us)
Async XLA Ops:
  2.6 18.9 %collective-permute-start = (bf16[256,1024]{1,0:T(8,128)(2,1)S(1)}, bf16[256,1024]{1,0:T(8,128)(2,1)S(1)}, u32[]{:S(2)}, u32[]{:S(2)}) collective-permute-start(bf16[256,1024]{1,0:T(8,128)(2,1)S(1)} %shard_map.221.refs_3_), channel_id=1, source_target_pairs={{0,1},{1,0},{2,3},{3,2},{4,5},{5,4},{6,7},{7,6},{8,9},{9,8},{10,11... | collective-permute-start | bytes 1572872 | tf_op jit(solution)/shard_map/ppermute | solution.py:36
  26.1 14.3 %collective-permute-start.10 = (bf16[2,2,32,1408]{3,2,1,0:T(8,128)(2,1)S(1)}, bf16[2,2,32,1408]{3,2,1,0:T(8,128)(2,1)S(1)}, u32[]{:S(2)}, u32[]{:S(2)}) collective-permute-start(bf16[2,2,32,1408]{3,2,1,0:T(8,128)(2,1)S(1)} %shard_map.226.refs_1_.refs_3_), channel_id=1, source_target_pairs={{0,1},{1,0},{2,3},{3,2},{4,5},{5,4},{6,7},{7,6},{8,9},{9,8},{10,11... | collective-permute-start | bytes 1081352 | tf_op jit(solution)/shard_map/ppermute | solution.py:36
  45.6 19.9 %collective-permute-start.2 = (bf16[512,1024]{1,0:T(8,128)(2,1)S(1)}, bf16[512,1024]{1,0:T(8,128)(2,1)S(1)}, u32[]{:S(2)}, u32[]{:S(2)}) collective-permute-start(bf16[512,1024]{1,0:T(8,128)(2,1)S(1)} %bitcast.135), channel_id=1, source_target_pairs={{0,4},{4,0},{8,12},{12,8},{16,20},{20,16},{24,28},{28,24},{1,5},{5... | collective-permute-start | bytes 3145736 | tf_op jit(solution)/shard_map/ppermute | solution.py:36
  45.7 17.9 %collective-permute-start.4 = (bf16[16,1024]{1,0:T(8,128)(2,1)S(1)}, bf16[16,1024]{1,0:T(8,128)(2,1)S(1)}, u32[]{:S(2)}, u32[]{:S(2)}) collective-permute-start(bf16[16,1024]{1,0:T(8,128)(2,1)S(1)} %collective-permute-done.3.refs_3_.refs_2_), channel_id=1, source_target_pairs={{0,4},{4,0},{8,12},{12,8},{16,20},{20,16},{24,28},{28,24},{1,5},{5... | collective-permute-start | bytes 98312 | tf_op jit(solution)/shard_map/ppermute | solution.py:36
  61.6 24.1 %collective-permute-start.19 = (bf16[2,4,64,1024]{3,2,1,0:T(8,128)(2,1)S(1)}, bf16[2,4,64,1024]{3,2,1,0:T(8,128)(2,1)S(1)}, u32[]{:S(2)}, u32[]{:S(2)}) collective-permute-start(bf16[2,4,64,1024]{3,2,1,0:T(8,128)(2,1)S(1)} %shard_map.233.refs_13_.refs_1_), channel_id=1, source_target_pairs={{0,8},{4,12},{8,0},{12,4},{16,24},{20,28},{24,16},{28,20},{1,9},{5... | collective-permute-start | bytes 3145736 | tf_op jit(solution)/shard_map/ppermute | solution.py:36
  62.1 23.6 %collective-permute-start.20 = (bf16[2,4,64,1024]{3,2,1,0:T(8,128)(2,1)S(1)}, bf16[2,4,64,1024]{3,2,1,0:T(8,128)(2,1)S(1)}, u32[]{:S(2)}, u32[]{:S(2)}) collective-permute-start(bf16[2,4,64,1024]{3,2,1,0:T(8,128)(2,1)S(1)} %shard_map.233.refs_13_.refs_1_), channel_id=1, source_target_pairs={{0,16},{4,20},{8,24},{12,28},{16,0},{20,4},{24,8},{28,12},{1,17},{... | collective-permute-start | bytes 3145736 | tf_op jit(solution)/shard_map/ppermute | solution.py:36
  80.0 20.7 %collective-permute-start.18 = (bf16[512,1024]{1,0:T(8,128)(2,1)S(1)}, bf16[512,1024]{1,0:T(8,128)(2,1)S(1)}, u32[]{:S(2)}, u32[]{:S(2)}) collective-permute-start(bf16[512,1024]{1,0:T(8,128)(2,1)S(1)} %bitcast.130), channel_id=1, source_target_pairs={{0,4},{4,0},{8,12},{12,8},{16,20},{20,16},{24,28},{28,24},{1,5},{5... | collective-permute-start | bytes 3145736 | tf_op jit(solution)/shard_map/ppermute | solution.py:36
  80.1 20.6 %collective-permute-start.23 = (bf16[2,128,1024]{2,1,0:T(8,128)(2,1)S(1)}, bf16[2,128,1024]{2,1,0:T(8,128)(2,1)S(1)}, u32[]{:S(2)}, u32[]{:S(2)}) collective-permute-start(bf16[2,128,1024]{2,1,0:T(8,128)(2,1)S(1)} %get-tuple-element.94.refs_4_), channel_id=1, source_target_pairs={{0,2},{1,3},{4,6},{5,7},{8,10},{9,11},{12,14},{13,15},{16,18},{17,... | collective-permute-start | bytes 1572872 | tf_op jit(solution)/shard_map/ppermute | solution.py:42
  85.8 13.8 %collective-permute-start.21 = (bf16[4,64,1024]{2,1,0:T(8,128)(2,1)S(1)}, bf16[4,64,1024]{2,1,0:T(8,128)(2,1)S(1)}, u32[]{:S(2)}, u32[]{:S(2)}) collective-permute-start(bf16[4,64,1024]{2,1,0:T(8,128)(2,1)S(1)} %get-tuple-element.95.refs_4_), channel_id=1, source_target_pairs={{0,16},{4,20},{8,24},{12,28},{16,0},{20,4},{24,8},{28,12},{1,17},{... | collective-permute-start | bytes 1572872 | tf_op jit(solution)/shard_map/ppermute | solution.py:36
  122.6 28.0 %collective-permute-start.25 = (bf16[2,128,1024]{2,1,0:T(8,128)(2,1)S(1)}, bf16[2,128,1024]{2,1,0:T(8,128)(2,1)S(1)}, u32[]{:S(2)}, u32[]{:S(2)}) collective-permute-start(bf16[2,128,1024]{2,1,0:T(8,128)(2,1)S(1)} %get-tuple-element.123), channel_id=1, source_target_pairs={{2,0},{3,1},{6,4},{7,5},{10,8},{11,9},{14,12},{15,13},{18,16},{19,... | collective-permute-start | bytes 1572872 | tf_op jit(solution)/shard_map/ppermute | solution.py:42
  144.4 25.3 %collective-permute-start.30 = (bf16[2,4,64,1024]{3,2,1,0:T(8,128)(2,1)S(1)}, bf16[2,4,64,1024]{3,2,1,0:T(8,128)(2,1)S(1)}, u32[]{:S(2)}, u32[]{:S(2)}) collective-permute-start(bf16[2,4,64,1024]{3,2,1,0:T(8,128)(2,1)S(1)} %get-tuple-element.131), channel_id=1, source_target_pairs={{0,8},{4,12},{8,0},{12,4},{16,24},{20,28},{24,16},{28,20},{1,9},{5... | collective-permute-start | bytes 3145736 | tf_op jit(solution)/shard_map/ppermute | solution.py:36
  146.1 25.4 %collective-permute-start.29 = (bf16[2,4,64,1024]{3,2,1,0:T(8,128)(2,1)S(1)}, bf16[2,4,64,1024]{3,2,1,0:T(8,128)(2,1)S(1)}, u32[]{:S(2)}, u32[]{:S(2)}) collective-permute-start(bf16[2,4,64,1024]{3,2,1,0:T(8,128)(2,1)S(1)} %get-tuple-element.129), channel_id=1, source_target_pairs={{0,16},{4,20},{8,24},{12,28},{16,0},{20,4},{24,8},{28,12},{1,17},{... | collective-permute-start | bytes 3145736 | tf_op jit(solution)/shard_map/ppermute | solution.py:36
  147.7 25.8 %collective-permute-start.26 = (bf16[512,1024]{1,0:T(8,128)(2,1)S(1)}, bf16[512,1024]{1,0:T(8,128)(2,1)S(1)}, u32[]{:S(2)}, u32[]{:S(2)}) collective-permute-start(bf16[512,1024]{1,0:T(8,128)(2,1)S(1)} %get-tuple-element.125), channel_id=1, source_target_pairs={{0,4},{4,0},{8,12},{12,8},{16,20},{20,16},{24,28},{28,24},{1,5},{5... | collective-permute-start | bytes 3145736 | tf_op jit(solution)/shard_map/ppermute | solution.py:36
  167.2 15.4 %collective-permute-start.28 = (f32[2,8,1280]{2,1,0:T(8,128)S(1)}, f32[2,8,1280]{2,1,0:T(8,128)S(1)}, u32[]{:S(2)}, u32[]{:S(2)}) collective-permute-start(f32[2,8,1280]{2,1,0:T(8,128)S(1)} %get-tuple-element.127), channel_id=1, source_target_pairs={{2,0},{3,1},{6,4},{7,5},{10,8},{11,9},{14,12},{15,13},{18,16},{19,... | collective-permute-start | bytes 245768 | tf_op jit(solution)/shard_map/ppermute | solution.py:42
  169.9 20.0 %collective-permute-start.32 = (bf16[4,64,1024]{2,1,0:T(8,128)(2,1)S(1)}, bf16[4,64,1024]{2,1,0:T(8,128)(2,1)S(1)}, u32[]{:S(2)}, u32[]{:S(2)}) collective-permute-start(bf16[4,64,1024]{2,1,0:T(8,128)(2,1)S(1)} %fusion.refs_9_), channel_id=1, source_target_pairs={{0,16},{4,20},{8,24},{12,28},{16,0},{20,4},{24,8},{28,12},{1,17},{... | collective-permute-start | bytes 1572872 | tf_op jit(solution)/shard_map/ppermute | solution.py:36
  171.8 18.1 %collective-permute-start.31 = (bf16[4,64,1024]{2,1,0:T(8,128)(2,1)S(1)}, bf16[4,64,1024]{2,1,0:T(8,128)(2,1)S(1)}, u32[]{:S(2)}, u32[]{:S(2)}) collective-permute-start(bf16[4,64,1024]{2,1,0:T(8,128)(2,1)S(1)} %fusion.1.refs_8_), channel_id=1, source_target_pairs={{0,8},{4,12},{8,0},{12,4},{16,24},{20,28},{24,16},{28,20},{1,9},{5... | collective-permute-start | bytes 1572872 | tf_op jit(solution)/shard_map/ppermute | solution.py:36
  175.0 41.8 %collective-permute-start.27 = (bf16[256,1024]{1,0:T(8,128)(2,1)}, bf16[256,1024]{1,0:T(8,128)(2,1)}, u32[]{:S(2)}, u32[]{:S(2)}) collective-permute-start(bf16[256,1024]{1,0:T(8,128)(2,1)} %get-tuple-element.163.refs_10_), channel_id=1, source_target_pairs={{0,1},{1,0},{2,3},{3,2},{4,5},{5,4},{6,7},{7,6},{8,9},{9,8},{10,11... | collective-permute-start | bytes 1572872 | tf_op jit(solution)/shard_map/ppermute | solution.py:36
  189.9 19.6 %collective-permute-start.33 = (bf16[512,1024]{1,0:T(8,128)(2,1)S(1)}, bf16[512,1024]{1,0:T(8,128)(2,1)S(1)}, u32[]{:S(2)}, u32[]{:S(2)}) collective-permute-start(bf16[512,1024]{1,0:T(8,128)(2,1)S(1)} %get-tuple-element.140), channel_id=1, source_target_pairs={{0,4},{4,0},{8,12},{12,8},{16,20},{20,16},{24,28},{28,24},{1,5},{5... | collective-permute-start | bytes 3145736 | tf_op jit(solution)/shard_map/ppermute | solution.py:36
  190.7 14.4 %collective-permute-start.34 = (bf16[2,2,64,1024]{3,2,0,1:T(8,128)(2,1)S(1)}, bf16[2,2,64,1024]{3,2,0,1:T(8,128)(2,1)S(1)}, u32[]{:S(2)}, u32[]{:S(2)}) collective-permute-start(bf16[2,2,64,1024]{3,2,0,1:T(8,128)(2,1)S(1)} %copy.35), channel_id=1, source_target_pairs={{0,1},{1,0},{2,3},{3,2},{4,5},{5,4},{6,7},{7,6},{8,9},{9,8},{10,11... | collective-permute-start | bytes 1572872 | tf_op jit(solution)/shard_map/ppermute | solution.py:36
  200.4 22.2 %collective-permute-start.37 = (bf16[2,4,32,1280]{3,2,1,0:T(8,128)(2,1)}, bf16[2,4,32,1280]{3,2,1,0:T(8,128)(2,1)}, u32[]{:S(2)}, u32[]{:S(2)}) collective-permute-start(bf16[2,4,32,1280]{3,2,1,0:T(8,128)(2,1)} %get-tuple-element.144), channel_id=1, source_target_pairs={{0,8},{4,12},{8,0},{12,4},{16,24},{20,28},{24,16},{28,20},{1,9},{5... | collective-permute-start | bytes 1966088 | tf_op jit(solution)/shard_map/ppermute | solution.py:36
  201.4 24.7 %collective-permute-start.36 = (bf16[2,4,32,1280]{3,2,1,0:T(8,128)(2,1)}, bf16[2,4,32,1280]{3,2,1,0:T(8,128)(2,1)}, u32[]{:S(2)}, u32[]{:S(2)}) collective-permute-start(bf16[2,4,32,1280]{3,2,1,0:T(8,128)(2,1)} %get-tuple-element.142), channel_id=1, source_target_pairs={{0,16},{4,20},{8,24},{12,28},{16,0},{20,4},{24,8},{28,12},{1,17},{... | collective-permute-start | bytes 1966088 | tf_op jit(solution)/shard_map/ppermute | solution.py:36
  206.1 23.3 %collective-permute-start.38 = (bf16[2,64,1024]{2,1,0:T(8,128)(2,1)}, bf16[2,64,1024]{2,1,0:T(8,128)(2,1)}, u32[]{:S(2)}, u32[]{:S(2)}) collective-permute-start(bf16[2,64,1024]{2,1,0:T(8,128)(2,1)} %get-tuple-element.158.refs_10_), channel_id=1, source_target_pairs={{0,2},{1,3},{2,0},{3,1},{4,6},{5,7},{6,4},{7,5},{8,10},{9,11},{10,... | collective-permute-start | bytes 786440 | tf_op jit(solution)/shard_map/ppermute | solution.py:36
  211.0 21.4 %collective-permute-start.35 = (bf16[256,1024]{1,0:T(8,128)(2,1)}, bf16[256,1024]{1,0:T(8,128)(2,1)}, u32[]{:S(2)}, u32[]{:S(2)}) collective-permute-start(bf16[256,1024]{1,0:T(8,128)(2,1)} %get-tuple-element.160.refs_9_), channel_id=1, source_target_pairs={{0,1},{1,0},{2,3},{3,2},{4,5},{5,4},{6,7},{7,6},{8,9},{9,8},{10,11... | collective-permute-start | bytes 1572872 | tf_op jit(solution)/shard_map/ppermute | solution.py:36
  214.2 21.2 %all-to-all-start = ((f32[32,16,128]{2,1,0:T(8,128)}), f32[32,16,128]{2,1,0:T(8,128)S(1)}, u32[]{:S(2)}, u32[]{:S(2)}) async-start(f32[32,16,128]{2,1,0:T(8,128)} %copy-done.13), calls=%async_computation | async-start | bytes 524288 | tf_op jit(solution)/shard_map/all_to_all | solution.py:1271
  (70 other events, 598.7 us)

commit v3 on v2

--- a/solution.py
+++ b/solution.py
@@ -983,7 +983,8 @@
             return swap(send_y, "dp", 4), swap(send_x, "dp", 2)
 
         first_got = swap(front_shard, "ctx", 2)
-        inside = enter_line(tokens, tokens_send, needs=[front_shard], cost=8)
+        cot_send = piece_to_send(cotangent, needs=[front_shard])
+        inside = enter_line(tokens, tokens_send, needs=[cot_send], cost=8)
         other = swap(inside, "dp", 1)
         ends = ends_of(inside)
         before = hop(ends, 2)
@@ -1000,6 +1001,7 @@
         far_across = across_of(*far_across_send)
         late_far = swap(late_near, "ctx", 1)
         before_other = swap(before, "dp", 1)
+        cot = enter_line(cotangent, cot_send, needs=far_across_send, cost=0.1)
         late_own = after(pair(late_near, late_far, needs=far_across_send, cost=8), *far_across)
         front_pieces = [near, *sides, *across, far, *far_sides, *far_across]
     else:
@@ -1033,12 +1035,14 @@
          sds((8, LANES)), sds((1, MINE)), sds((LANES, LANES), bf16)],
         [pltpu.VMEM((width, LANES), f32), pltpu.VMEM((8, XBC), f32), pltpu.VMEM((1, INNER), f32)],
         cost=8,
-        needs=[late_own, before_other] if fast else (),
+        needs=[late_own, before_other, cot] if fast else (),
         placed=True,
     )
     if fast:
         late_sides = sides_of(late_own)
-    cot_send = piece_to_send(cotangent, needs=[w_front])
+    else:
+        cot = enter_line(cotangent, piece_to_send(cotangent))
+    cot_other = swap(cot, "dp", 1)
 
     grid = (seqs, blocks)
 
@@ -1086,11 +1090,7 @@
          pltpu.VMEM((BLOCK + AHEAD, CONVD), f32), pltpu.VMEM((BLOCK, MINE), bf16),
          pltpu.VMEM((BLOCK, MINE), f32), pltpu.VMEM((BLOCK, MINE), f32)],
         cost=16,
-        needs=[cot_send],
     )(inside, other, before, before_other, norm_full, w_front, *conv_args)
-
-    cot = enter_line(cotangent, cot_send, needs=[state_total])
-    cot_other = swap(cot, "dp", 1)
 
     def relay(local, decay, steps):
         received = hop(local, steps)
@@ -1099,7 +1099,7 @@
         return received
 
     incoming = relay(state_total, state_decay, 2)
-    late_across_send = across_parts(*late_sides, needs=[cot]) if fast else ()
+    late_across_send = across_parts(*late_sides, needs=[state_total]) if fast else ()
     y = call(
         within_kernel,
         grid,

time: 263 us -> 260 us (0.989)
  starting transfers between devices: 71.5 us -> 64.6 us
  waiting for transfers between devices: 61.7 us -> 65.3 us
    ppermute x40, starting transfers between devices: 56.6 us -> 49.8 us  [swap(): return lax.ppermute(value, axis, [(i, i ^ mask) for i in range(count)])]
    ppermute x40, waiting for transfers between devices: 58.6 us -> 61.7 us  [swap(): return lax.ppermute(value, axis, [(i, i ^ mask) for i in range(count)])]
    unnamed x98 -> x92, local copies, waits for them, and re-layouts: 9.61 us -> 11 us
  transfers between devices with their start and end apart: 45 -> 45, of which waited for: 22 -> 21; matrix products, arithmetic and copies ran while one was open for 5% -> 4% of each run, Pallas kernels for 31% -> 31%
where the time goes in v3:
time: 260 us; the launch traced here: 259 us
  Pallas kernels  105 us (40%)
  waiting for transfers between devices  65.3 us (25%)
  starting transfers between devices  64.6 us (25%)
  local copies, waits for them, and re-layouts  15.9 us (6%)
  other arithmetic  7.53 us (3%)
    pallas_call x29, Pallas kernels, call(): return lambda *arrays: made(*arrays, *needs)  104 us
    ppermute x40, waiting for transfers between devices, swap(): return lax.ppermute(value, axis, [(i, i ^ mask) for i in range(count)])  61.7 us
    ppermute x40, starting transfers between devices, swap(): return lax.ppermute(value, axis, [(i, i ^ mask) for i in range(count)])  49.8 us
    ppermute x4, starting transfers between devices, hop(): return lax.ppermute(value, 'ctx', pairs)  12.3 us
    unnamed x92, local copies, waits for them, and re-layouts  11 us
  transfers between devices with their start and end apart: 45, of which 21 were waited for; matrix products, arithmetic and copies ran while one was open for 4% of the time, Pallas kernels for 31%

profile of v3, /device:TPU:0, one launch (start us, length us, event | category | flops | bytes accessed | tf_op | source)
XLA Modules:
  0.0 259.4 jit_solution(13308441157098689440)
XLA Ops:
  2.6 3.1 %collective-permute-start = (bf16[256,1024]{1,0:T(8,128)(2,1)S(1)}, bf16[256,1024]{1,0:T(8,128)(2,1)S(1)}, u32[]{:S(2)}, u32[]{:S(2)}) collective-permute-start(bf16[256,1024]{1,0:T(8,128)(2,1)S(1)} %shard_map.221.refs_3_), channel_id=1, source_target_pairs={{0,1},{1,0},{2,3},{3,2},{4,5},{5,4},{6,7},{7,6},{8,9},{9,8},{10,11... | collective-permute-start | bytes 1572872 | tf_op jit(solution)/shard_map/ppermute | solution.py:36
  13.7 7.8 %collective-permute-done.refs_2_ = bf16[256,1024]{1,0:T(8,128)(2,1)S(1)} collective-permute-done((bf16[256,1024]{1,0:T(8,128)(2,1)S(1)}, bf16[256,1024]{1,0:T(8,128)(2,1)S(1)}, u32[]{:S(2)}, u32[]{:S(2)}) %collective-permute-start) | collective-permute-done | bytes 524320 | tf_op jit(solution)/shard_map/ppermute | solution.py:36
  35.8 3.6 %collective-permute-start.3 = (bf16[16,1024]{1,0:T(8,128)(2,1)S(1)}, bf16[16,1024]{1,0:T(8,128)(2,1)S(1)}, u32[]{:S(2)}, u32[]{:S(2)}) collective-permute-start(bf16[16,1024]{1,0:T(8,128)(2,1)S(1)} %shard_map.226.refs_2_), channel_id=1, source_target_pairs={{0,2},{1,3},{4,6},{5,7},{8,10},{9,11},{12,14},{13,15},{16,18},{17,... | collective-permute-start | bytes 98312 | tf_op jit(solution)/shard_map/ppermute | solution.py:42
  45.7 5.7 %collective-permute-done.11.refs_0_.refs_9_ = bf16[2,2,32,1408]{3,2,1,0:T(8,128)(2,1)S(1)} collective-permute-done((bf16[2,2,32,1408]{3,2,1,0:T(8,128)(2,1)S(1)}, bf16[2,2,32,1408]{3,2,1,0:T(8,128)(2,1)S(1)}, u32[]{:S(2)}, u32[]{:S(2)}) %collective-permute-start.11) | collective-permute-done | bytes 360480 | tf_op jit(solution)/shard_map/ppermute | solution.py:36
  57.5 5.8 %collective-permute-done.16.refs_1_ = bf16[2,2,64,1024]{3,2,1,0:T(8,128)(2,1)S(1)} collective-permute-done((bf16[2,2,64,1024]{3,2,1,0:T(8,128)(2,1)S(1)}, bf16[2,2,64,1024]{3,2,1,0:T(8,128)(2,1)S(1)}, u32[]{:S(2)}, u32[]{:S(2)}) %collective-permute-start.16) | collective-permute-done | bytes 524320 | tf_op jit(solution)/shard_map/ppermute | solution.py:36
  66.0 12.6 %shard_map.237 = (bf16[1024,1024]{1,0:T(8,128)(2,1)}, bf16[4,272,1408]{2,1,0:T(8,128)(2,1)}, bf16[1024,1024]{1,0:T(8,128)(2,1)}, bf16[1024,1024]{1,0:T(8,128)(2,...) custom-call(bf16[512,1024]{1,0:T(8,128)(2,1)S(1)} %bitcast.136, ...), custom_call_target="tpu_custom_call" | custom-call | flops 16000000000 | bytes 56000000 | tf_op jit(solution)/shard_map/pallas_call | solution.py:863
  78.6 5.6 %collective-permute-start.23 = (bf16[2,128,1024]{2,1,0:T(8,128)(2,1)S(1)}, bf16[2,128,1024]{2,1,0:T(8,128)(2,1)S(1)}, u32[]{:S(2)}, u32[]{:S(2)}) collective-permute-start(bf16[2,128,1024]{2,1,0:T(8,128)(2,1)S(1)} %get-tuple-element.94.refs_2_), channel_id=1, source_target_pairs={{0,2},{1,3},{4,6},{5,7},{8,10},{9,11},{12,14},{13,15},{16,18},{17,... | collective-permute-start | bytes 1572872 | tf_op jit(solution)/shard_map/ppermute | solution.py:42
  84.2 4.9 %collective-permute-done.19.refs_0_.refs_2_ = bf16[2,4,64,1024]{3,2,1,0:T(8,128)(2,1)S(1)} collective-permute-done((bf16[2,4,64,1024]{3,2,1,0:T(8,128)(2,1)S(1)}, bf16[2,4,64,1024]{3,2,1,0:T(8,128)(2,1)S(1)}, u32[]{:S(2)}, u32[]{:S(2)}) %collective-permute-start.19) | collective-permute-done | bytes 1048608 | tf_op jit(solution)/shard_map/ppermute | solution.py:36
  93.7 4.9 %shard_map.239.refs_6_.refs_5_ = bf16[1024,1024]{1,0:T(8,128)(2,1)S(1)} custom-call(bf16[1024,1024]{1,0:T(8,128)(2,1)S(1)} %copy-done.26, bf16[1024,256]{1,0:T(8,128)(2,1)S(1)} %copy-done.34, f32[1024,128]{1,0:T(8,128)S(1)} %copy-done.32, f32[4,128,256]{2,1,0:T(8,128)S(1)} %copy-done.37, bf16[4,64,1024]{2,1,0:T(8,128)(2,1)S(1)} %get-tuple-element.95.refs_4_, ...), custom_call_target="tpu_custom_call" | custom-call | flops 8000000000 | bytes 28000000 | tf_op jit(solution)/shard_map/pallas_call | solution.py:863
  98.7 4.2 %collective-permute-done.21.refs_4_ = bf16[4,64,1024]{2,1,0:T(8,128)(2,1)S(1)} collective-permute-done((bf16[4,64,1024]{2,1,0:T(8,128)(2,1)S(1)}, bf16[4,64,1024]{2,1,0:T(8,128)(2,1)S(1)}, u32[]{:S(2)}, u32[]{:S(2)}) %collective-permute-start.21) | collective-permute-done | bytes 524320 | tf_op jit(solution)/shard_map/ppermute | solution.py:36
  104.3 9.1 %shard_map.241 = (bf16[1024,1024]{1,0:T(8,128)(2,1)}, bf16[1024,1024]{1,0:T(8,128)(2,1)}, bf16[1024,1024]{1,0:T(8,128)(2,1)}, bf16[4,128,1024]{2,1,0:T(8,128)(2,1)}, f32[8,1024]{1,0:T(8,128)S(1)}) custom-call(bf16[1024,1024]{1,0:T(8,128)(2,1)S(1)} %copy-done.28, bf16[512,1024]{1,0:T(8,128)(2,1)S(1)} %bitcast.132, ...), custom_call_target="tpu_custom_call" | custom-call | flops 16000000000 | bytes 56000000 | tf_op jit(solution)/shard_map/pallas_call | solution.py:863
  115.8 10.4 %shard_map.242 = (bf16[1024,1024]{1,0:T(8,128)(2,1)S(1)}, bf16[1024,1024]{1,0:T(8,128)(2,1)S(1)}, bf16[1024,1024]{1,0:T(8,128)(2,1)S(1)}, f32[1024,128]{1,0:T(8,...) custom-call(bf16[1024,1024]{1,0:T(8,128)(2,1)} %get-tuple-element.10, ...), custom_call_target="tpu_custom_call" | custom-call | flops 12000000000 | bytes 42000000 | tf_op jit(solution)/shard_map/pallas_call | solution.py:863
  127.7 20.2 %shard_map.243 = (bf16[512,1024]{1,0:T(8,128)(2,1)S(1)}, bf16[512,1024]{1,0:T(8,128)(2,1)S(1)}, bf16[1024,1024]{1,0:T(8,128)(2,1)S(1)}, f32[1024,256]{1,0:T(8,12...) custom-call(s32[3]{0:T(128)S(1)} %pad_add_fusion.refs_0_, ...), custom_call_target="tpu_custom_call" | custom-call | flops 24000000000 | bytes 84000000 | tf_op jit(solution)/shard_map/pallas_call | solution.py:863
  150.7 3.7 %collective-permute-done.25.refs_15_ = bf16[2,128,1024]{2,1,0:T(8,128)(2,1)S(1)} collective-permute-done((bf16[2,128,1024]{2,1,0:T(8,128)(2,1)S(1)}, bf16[2,128,1024]{2,1,0:T(8,128)(2,1)S(1)}, u32[]{:S(2)}, u32[]{:S(2)}) %collective-permute-start.25) | collective-permute-done | bytes 524320 | tf_op jit(solution)/shard_map/ppermute | solution.py:42
  154.4 16.7 %shard_map.244 = (bf16[2,512,1408]{2,1,0:T(8,128)(2,1)S(1)}, f32[2,8,1280]{2,1,0:T(8,128)S(1)}, f32[2,32,1280]{2,1,0:T(8,128)S(1)}, f32[8,1280]{1,0:T(8,128)S(1)}, f32[8,128]{1,0:T(8,128)S(1)}) custom-call(bf16[4,272,1408]{2,1,0:T(8,128)(2,1)S(1)} %copy-done.31, f32[8,1280]{1,0:T(8,128)S(1)} %get-tuple-element.90.refs_6_.refs_1_, ...), custom_call_target="tpu_custom_call" | custom-call | flops 24000000000 | bytes 84000000 | tf_op jit(solution)/shard_map/pallas_call | solution.py:863
  177.8 4.1 %collective-permute-start.27 = (bf16[256,1024]{1,0:T(8,128)(2,1)}, bf16[256,1024]{1,0:T(8,128)(2,1)}, u32[]{:S(2)}, u32[]{:S(2)}) collective-permute-start(bf16[256,1024]{1,0:T(8,128)(2,1)} %get-tuple-element.163.refs_10_), channel_id=1, source_target_pairs={{0,1},{1,0},{2,3},{3,2},{4,5},{5,4},{6,7},{7,6},{8,9},{9,8},{10,11... | collective-permute-start | bytes 1572872 | tf_op jit(solution)/shard_map/ppermute | solution.py:36
  181.9 7.3 %shard_map.247 = (bf16[512,1024]{1,0:T(8,128)(2,1)S(1)}, bf16[512,1024]{1,0:T(8,128)(2,1)S(1)}, f32[1,1024]{1,0:T(1,128)S(1)}) custom-call(bf16[512,1024]{1,0:T(8,128)(2,1)S(1)} %bitcast.137, bf16[512,1024]{1,0:T(8,128)(2,1)S(1)} %collective-permute-done.2.refs_1_, bf16[1024,1024]{1,0:T(8,128)(2,1)S(1)} %get-tuple-element.112.refs_2_, ...), custom_call_target="tpu_custom_call" | custom-call | flops 12000000000 | bytes 42000000 | tf_op jit(solution)/shard_map/pallas_call | solution.py:863
  192.8 6.5 %shard_map.249 = (f32[1024,128]{1,0:T(8,128)S(1)}, bf16[2,4,32,1280]{3,2,1,0:T(8,128)(2,1)S(1)}, bf16[2,4,32,1280]{3,2,1,0:T(8,128)(2,1)}, bf16[2,4,32,1280]{3,2...) custom-call(s32[3]{0:T(128)S(1)} %pad_add_fusion.refs_0_, ...), custom_call_target="tpu_custom_call" | custom-call | flops 10000000000 | bytes 35000000 | tf_op jit(solution)/shard_map/pallas_call | solution.py:863
  201.4 3.1 %collective-permute-done.34 = bf16[2,2,64,1024]{3,2,0,1:T(8,128)(2,1)S(1)} collective-permute-done((bf16[2,2,64,1024]{3,2,0,1:T(8,128)(2,1)S(1)}, bf16[2,2,64,1024]{3,2,0,1:T(8,128)(2,1)S(1)}, u32[]{:S(2)}, u32[]{:S(2)}) %collective-permute-start.34) | collective-permute-done | bytes 524320 | tf_op jit(solution)/shard_map/ppermute | solution.py:36
  205.4 3.4 %collective-permute-start.38 = (bf16[2,64,1024]{2,1,0:T(8,128)(2,1)}, bf16[2,64,1024]{2,1,0:T(8,128)(2,1)}, u32[]{:S(2)}, u32[]{:S(2)}) collective-permute-start(bf16[2,64,1024]{2,1,0:T(8,128)(2,1)} %get-tuple-element.158.refs_10_), channel_id=1, source_target_pairs={{0,2},{1,3},{2,0},{3,1},{4,6},{5,7},{6,4},{7,5},{8,10},{9,11},{10,... | collective-permute-start | bytes 786440 | tf_op jit(solution)/shard_map/ppermute | solution.py:36
  227.2 5.4 %collective-permute-done.35.refs_4_ = bf16[256,1024]{1,0:T(8,128)(2,1)} collective-permute-done((bf16[256,1024]{1,0:T(8,128)(2,1)}, bf16[256,1024]{1,0:T(8,128)(2,1)}, u32[]{:S(2)}, u32[]{:S(2)}) %collective-permute-start.35) | collective-permute-done | bytes 524320 | tf_op jit(solution)/shard_map/ppermute | solution.py:36
  232.6 3.1 %shard_map.254.refs_1_ = f32[2,256,1024]{2,1,0:T(8,128)} custom-call(s32[3]{0:T(128)S(1)} %pad_add_fusion.refs_0_, bf16[2,256,1024]{2,1,0:T(8,128)(2,1)S(1)} %copy-done.5, bf16[2,256,1024]{2,1,0:T(8,128)(2,1)S(1)} %copy-done.1, bf16[256,1024]{1,0:T(8,128)(2,1)S(1)} %copy-done.7, bf16[256,1024]{1,0:T(8,128)(2,1)} %collective-permute-done.35.refs_4_, ...), custom_call_target="tpu_custom_call" | custom-call | flops 8000000000 | bytes 28000000 | tf_op jit(solution)/shard_map/pallas_call | solution.py:863
  239.1 7.7 %collective-permute-done.41 = bf16[2,2,32,1280]{3,2,0,1:T(8,128)(2,1)S(1)} collective-permute-done((bf16[2,2,32,1280]{3,2,0,1:T(8,128)(2,1)S(1)}, bf16[2,2,32,1280]{3,2,0,1:T(8,128)(2,1)S(1)}, u32[]{:S(2)}, u32[]{:S(2)}) %collective-permute-start.41) | collective-permute-done | bytes 327712 | tf_op jit(solution)/shard_map/ppermute | solution.py:36
  250.4 4.5 %collective-permute-done.42.refs_1_ = bf16[2,32,1280]{2,1,0:T(8,128)(2,1)S(1)} collective-permute-done((bf16[2,32,1280]{2,1,0:T(8,128)(2,1)S(1)}, bf16[2,32,1280]{2,1,0:T(8,128)(2,1)S(1)}, u32[]{:S(2)}, u32[]{:S(2)}) %collective-permute-start.42) | collective-permute-done | bytes 163872 | tf_op jit(solution)/shard_map/ppermute | solution.py:36
  (221 shorter events, 94.3 us)
Async XLA Ops:
  2.6 18.9 %collective-permute-start = (bf16[256,1024]{1,0:T(8,128)(2,1)S(1)}, bf16[256,1024]{1,0:T(8,128)(2,1)S(1)}, u32[]{:S(2)}, u32[]{:S(2)}) collective-permute-start(bf16[256,1024]{1,0:T(8,128)(2,1)S(1)} %shard_map.221.refs_3_), channel_id=1, source_target_pairs={{0,1},{1,0},{2,3},{3,2},{4,5},{5,4},{6,7},{7,6},{8,9},{9,8},{10,11... | collective-permute-start | bytes 1572872 | tf_op jit(solution)/shard_map/ppermute | solution.py:36
  27.4 14.5 %collective-permute-start.13 = (bf16[2,64,1024]{2,1,0:T(8,128)(2,1)S(1)}, bf16[2,64,1024]{2,1,0:T(8,128)(2,1)S(1)}, u32[]{:S(2)}, u32[]{:S(2)}) collective-permute-start(bf16[2,64,1024]{2,1,0:T(8,128)(2,1)S(1)} %shard_map.230), channel_id=1, source_target_pairs={{0,2},{1,3},{2,0},{3,1},{4,6},{5,7},{6,4},{7,5},{8,10},{9,11},{10,... | collective-permute-start | bytes 786440 | tf_op jit(solution)/shard_map/ppermute | solution.py:36
  40.5 14.9 %collective-permute-start.17 = (bf16[256,1024]{1,0:T(8,128)(2,1)S(1)}, bf16[256,1024]{1,0:T(8,128)(2,1)S(1)}, u32[]{:S(2)}, u32[]{:S(2)}) collective-permute-start(bf16[256,1024]{1,0:T(8,128)(2,1)S(1)} %shard_map.224.refs_4_), channel_id=1, source_target_pairs={{0,1},{1,0},{2,3},{3,2},{4,5},{5,4},{6,7},{7,6},{8,9},{9,8},{10,11... | collective-permute-start | bytes 1572872 | tf_op jit(solution)/shard_map/ppermute | solution.py:36
  42.1 21.3 %collective-permute-start.16 = (bf16[2,2,64,1024]{3,2,1,0:T(8,128)(2,1)S(1)}, bf16[2,2,64,1024]{3,2,1,0:T(8,128)(2,1)S(1)}, u32[]{:S(2)}, u32[]{:S(2)}) collective-permute-start(bf16[2,2,64,1024]{3,2,1,0:T(8,128)(2,1)S(1)} %shard_map.231.refs_2_.refs_0_), channel_id=1, source_target_pairs={{0,1},{1,0},{2,3},{3,2},{4,5},{5,4},{6,7},{7,6},{8,9},{9,8},{10,11... | collective-permute-start | bytes 1572872 | tf_op jit(solution)/shard_map/ppermute | solution.py:36
  45.6 20.3 %collective-permute-start.2 = (bf16[512,1024]{1,0:T(8,128)(2,1)S(1)}, bf16[512,1024]{1,0:T(8,128)(2,1)S(1)}, u32[]{:S(2)}, u32[]{:S(2)}) collective-permute-start(bf16[512,1024]{1,0:T(8,128)(2,1)S(1)} %bitcast.135), channel_id=1, source_target_pairs={{0,4},{4,0},{8,12},{12,8},{16,20},{20,16},{24,28},{28,24},{1,5},{5... | collective-permute-start | bytes 3145736 | tf_op jit(solution)/shard_map/ppermute | solution.py:36
  63.3 40.9 %collective-permute-start.18 = (bf16[512,1024]{1,0:T(8,128)(2,1)S(1)}, bf16[512,1024]{1,0:T(8,128)(2,1)S(1)}, u32[]{:S(2)}, u32[]{:S(2)}) collective-permute-start(bf16[512,1024]{1,0:T(8,128)(2,1)S(1)} %bitcast.130), channel_id=1, source_target_pairs={{0,4},{4,0},{8,12},{12,8},{16,20},{20,16},{24,28},{28,24},{1,5},{5... | collective-permute-start | bytes 3145736 | tf_op jit(solution)/shard_map/ppermute | solution.py:36
  63.5 25.6 %collective-permute-start.19 = (bf16[2,4,64,1024]{3,2,1,0:T(8,128)(2,1)S(1)}, bf16[2,4,64,1024]{3,2,1,0:T(8,128)(2,1)S(1)}, u32[]{:S(2)}, u32[]{:S(2)}) collective-permute-start(bf16[2,4,64,1024]{3,2,1,0:T(8,128)(2,1)S(1)} %shard_map.234.refs_13_.refs_1_), channel_id=1, source_target_pairs={{0,8},{4,12},{8,0},{12,4},{16,24},{20,28},{24,16},{28,20},{1,9},{5... | collective-permute-start | bytes 3145736 | tf_op jit(solution)/shard_map/ppermute | solution.py:36
  64.1 25.3 %collective-permute-start.20 = (bf16[2,4,64,1024]{3,2,1,0:T(8,128)(2,1)S(1)}, bf16[2,4,64,1024]{3,2,1,0:T(8,128)(2,1)S(1)}, u32[]{:S(2)}, u32[]{:S(2)}) collective-permute-start(bf16[2,4,64,1024]{3,2,1,0:T(8,128)(2,1)S(1)} %shard_map.234.refs_13_.refs_1_), channel_id=1, source_target_pairs={{0,16},{4,20},{8,24},{12,28},{16,0},{20,4},{24,8},{28,12},{1,17},{... | collective-permute-start | bytes 3145736 | tf_op jit(solution)/shard_map/ppermute | solution.py:36
  78.6 25.6 %collective-permute-start.23 = (bf16[2,128,1024]{2,1,0:T(8,128)(2,1)S(1)}, bf16[2,128,1024]{2,1,0:T(8,128)(2,1)S(1)}, u32[]{:S(2)}, u32[]{:S(2)}) collective-permute-start(bf16[2,128,1024]{2,1,0:T(8,128)(2,1)S(1)} %get-tuple-element.94.refs_2_), channel_id=1, source_target_pairs={{0,2},{1,3},{4,6},{5,7},{8,10},{9,11},{12,14},{13,15},{16,18},{17,... | collective-permute-start | bytes 1572872 | tf_op jit(solution)/shard_map/ppermute | solution.py:42
  126.1 28.3 %collective-permute-start.25 = (bf16[2,128,1024]{2,1,0:T(8,128)(2,1)S(1)}, bf16[2,128,1024]{2,1,0:T(8,128)(2,1)S(1)}, u32[]{:S(2)}, u32[]{:S(2)}) collective-permute-start(bf16[2,128,1024]{2,1,0:T(8,128)(2,1)S(1)} %get-tuple-element.123), channel_id=1, source_target_pairs={{2,0},{3,1},{6,4},{7,5},{10,8},{11,9},{14,12},{15,13},{18,16},{19,... | collective-permute-start | bytes 1572872 | tf_op jit(solution)/shard_map/ppermute | solution.py:42
  148.0 25.3 %collective-permute-start.30 = (bf16[2,4,64,1024]{3,2,1,0:T(8,128)(2,1)S(1)}, bf16[2,4,64,1024]{3,2,1,0:T(8,128)(2,1)S(1)}, u32[]{:S(2)}, u32[]{:S(2)}) collective-permute-start(bf16[2,4,64,1024]{3,2,1,0:T(8,128)(2,1)S(1)} %get-tuple-element.131), channel_id=1, source_target_pairs={{0,8},{4,12},{8,0},{12,4},{16,24},{20,28},{24,16},{28,20},{1,9},{5... | collective-permute-start | bytes 3145736 | tf_op jit(solution)/shard_map/ppermute | solution.py:36
  149.2 25.6 %collective-permute-start.29 = (bf16[2,4,64,1024]{3,2,1,0:T(8,128)(2,1)S(1)}, bf16[2,4,64,1024]{3,2,1,0:T(8,128)(2,1)S(1)}, u32[]{:S(2)}, u32[]{:S(2)}) collective-permute-start(bf16[2,4,64,1024]{3,2,1,0:T(8,128)(2,1)S(1)} %get-tuple-element.129), channel_id=1, source_target_pairs={{0,16},{4,20},{8,24},{12,28},{16,0},{20,4},{24,8},{28,12},{1,17},{... | collective-permute-start | bytes 3145736 | tf_op jit(solution)/shard_map/ppermute | solution.py:36
  150.7 25.8 %collective-permute-start.26 = (bf16[512,1024]{1,0:T(8,128)(2,1)S(1)}, bf16[512,1024]{1,0:T(8,128)(2,1)S(1)}, u32[]{:S(2)}, u32[]{:S(2)}) collective-permute-start(bf16[512,1024]{1,0:T(8,128)(2,1)S(1)} %get-tuple-element.125), channel_id=1, source_target_pairs={{0,4},{4,0},{8,12},{12,8},{16,20},{20,16},{24,28},{28,24},{1,5},{5... | collective-permute-start | bytes 3145736 | tf_op jit(solution)/shard_map/ppermute | solution.py:36
  173.4 15.9 %collective-permute-start.32 = (bf16[4,64,1024]{2,1,0:T(8,128)(2,1)S(1)}, bf16[4,64,1024]{2,1,0:T(8,128)(2,1)S(1)}, u32[]{:S(2)}, u32[]{:S(2)}) collective-permute-start(bf16[4,64,1024]{2,1,0:T(8,128)(2,1)S(1)} %fusion.refs_9_), channel_id=1, source_target_pairs={{0,16},{4,20},{8,24},{12,28},{16,0},{20,4},{24,8},{28,12},{1,17},{... | collective-permute-start | bytes 1572872 | tf_op jit(solution)/shard_map/ppermute | solution.py:36
  175.0 14.4 %collective-permute-start.31 = (bf16[4,64,1024]{2,1,0:T(8,128)(2,1)S(1)}, bf16[4,64,1024]{2,1,0:T(8,128)(2,1)S(1)}, u32[]{:S(2)}, u32[]{:S(2)}) collective-permute-start(bf16[4,64,1024]{2,1,0:T(8,128)(2,1)S(1)} %fusion.1.refs_8_), channel_id=1, source_target_pairs={{0,8},{4,12},{8,0},{12,4},{16,24},{20,28},{24,16},{28,20},{1,9},{5... | collective-permute-start | bytes 1572872 | tf_op jit(solution)/shard_map/ppermute | solution.py:36
  177.8 38.2 %collective-permute-start.27 = (bf16[256,1024]{1,0:T(8,128)(2,1)}, bf16[256,1024]{1,0:T(8,128)(2,1)}, u32[]{:S(2)}, u32[]{:S(2)}) collective-permute-start(bf16[256,1024]{1,0:T(8,128)(2,1)} %get-tuple-element.163.refs_10_), channel_id=1, source_target_pairs={{0,1},{1,0},{2,3},{3,2},{4,5},{5,4},{6,7},{7,6},{8,9},{9,8},{10,11... | collective-permute-start | bytes 1572872 | tf_op jit(solution)/shard_map/ppermute | solution.py:36
  189.3 19.6 %collective-permute-start.33 = (bf16[512,1024]{1,0:T(8,128)(2,1)S(1)}, bf16[512,1024]{1,0:T(8,128)(2,1)S(1)}, u32[]{:S(2)}, u32[]{:S(2)}) collective-permute-start(bf16[512,1024]{1,0:T(8,128)(2,1)S(1)} %get-tuple-element.140), channel_id=1, source_target_pairs={{0,4},{4,0},{8,12},{12,8},{16,20},{20,16},{24,28},{28,24},{1,5},{5... | collective-permute-start | bytes 3145736 | tf_op jit(solution)/shard_map/ppermute | solution.py:36
  190.1 14.4 %collective-permute-start.34 = (bf16[2,2,64,1024]{3,2,0,1:T(8,128)(2,1)S(1)}, bf16[2,2,64,1024]{3,2,0,1:T(8,128)(2,1)S(1)}, u32[]{:S(2)}, u32[]{:S(2)}) collective-permute-start(bf16[2,2,64,1024]{3,2,0,1:T(8,128)(2,1)S(1)} %copy.35), channel_id=1, source_target_pairs={{0,1},{1,0},{2,3},{3,2},{4,5},{5,4},{6,7},{7,6},{8,9},{9,8},{10,11... | collective-permute-start | bytes 1572872 | tf_op jit(solution)/shard_map/ppermute | solution.py:36
  199.3 22.5 %collective-permute-start.37 = (bf16[2,4,32,1280]{3,2,1,0:T(8,128)(2,1)}, bf16[2,4,32,1280]{3,2,1,0:T(8,128)(2,1)}, u32[]{:S(2)}, u32[]{:S(2)}) collective-permute-start(bf16[2,4,32,1280]{3,2,1,0:T(8,128)(2,1)} %get-tuple-element.144), channel_id=1, source_target_pairs={{0,8},{4,12},{8,0},{12,4},{16,24},{20,28},{24,16},{28,20},{1,9},{5... | collective-permute-start | bytes 1966088 | tf_op jit(solution)/shard_map/ppermute | solution.py:36
  200.9 23.7 %collective-permute-start.36 = (bf16[2,4,32,1280]{3,2,1,0:T(8,128)(2,1)}, bf16[2,4,32,1280]{3,2,1,0:T(8,128)(2,1)}, u32[]{:S(2)}, u32[]{:S(2)}) collective-permute-start(bf16[2,4,32,1280]{3,2,1,0:T(8,128)(2,1)} %get-tuple-element.142), channel_id=1, source_target_pairs={{0,16},{4,20},{8,24},{12,28},{16,0},{20,4},{24,8},{28,12},{1,17},{... | collective-permute-start | bytes 1966088 | tf_op jit(solution)/shard_map/ppermute | solution.py:36
  205.4 21.8 %collective-permute-start.38 = (bf16[2,64,1024]{2,1,0:T(8,128)(2,1)}, bf16[2,64,1024]{2,1,0:T(8,128)(2,1)}, u32[]{:S(2)}, u32[]{:S(2)}) collective-permute-start(bf16[2,64,1024]{2,1,0:T(8,128)(2,1)} %get-tuple-element.158.refs_10_), channel_id=1, source_target_pairs={{0,2},{1,3},{2,0},{3,1},{4,6},{5,7},{6,4},{7,5},{8,10},{9,11},{10,... | collective-permute-start | bytes 786440 | tf_op jit(solution)/shard_map/ppermute | solution.py:36
  210.3 22.3 %collective-permute-start.35 = (bf16[256,1024]{1,0:T(8,128)(2,1)}, bf16[256,1024]{1,0:T(8,128)(2,1)}, u32[]{:S(2)}, u32[]{:S(2)}) collective-permute-start(bf16[256,1024]{1,0:T(8,128)(2,1)} %get-tuple-element.160.refs_9_), channel_id=1, source_target_pairs={{0,1},{1,0},{2,3},{3,2},{4,5},{5,4},{6,7},{7,6},{8,9},{9,8},{10,11... | collective-permute-start | bytes 1572872 | tf_op jit(solution)/shard_map/ppermute | solution.py:36
  213.4 22.3 %all-to-all-start = ((f32[32,16,128]{2,1,0:T(8,128)}), f32[32,16,128]{2,1,0:T(8,128)S(1)}, u32[]{:S(2)}, u32[]{:S(2)}) async-start(f32[32,16,128]{2,1,0:T(8,128)} %copy-done.8), calls=%async_computation | async-start | bytes 524288 | tf_op jit(solution)/shard_map/all_to_all | solution.py:1271
  222.9 14.4 %collective-permute-start.40 = (bf16[4,32,1280]{2,1,0:T(8,128)(2,1)S(1)}, bf16[4,32,1280]{2,1,0:T(8,128)(2,1)}, u32[]{:S(2)}, u32[]{:S(2)}) collective-permute-start(bf16[4,32,1280]{2,1,0:T(8,128)(2,1)S(1)} %fusion.2.refs_8_), channel_id=1, source_target_pairs={{0,16},{4,20},{8,24},{12,28},{16,0},{20,4},{24,8},{28,12},{1,17},{... | collective-permute-start | bytes 983048 | tf_op jit(solution)/shard_map/ppermute | solution.py:36
  (67 other events, 573.9 us)
